TPU v7x, 32 devices: a whole 2x2x4 slice. The times are simulated.
32 devices in a mesh: gx: 4 (over y, x), gz: 8 (over z, core).
Axes of the slice: x: 2, y: 2, z: 4, core: 2. Of those that a mesh axis runs over, the one named last changes fastest.
Arguments:
- adjoint: float32 [3, 128, 64, 512], P(None, 'gz', 'gx')
- base_flow: float32 [2, 128, 64, 512], P(None, 'gz', 'gx'), may hold values from 0.5 to 1.5
- conductance: float32 [128, 64, 512], P('gz', 'gx'), may hold values from 20 to 80
- ground_mask: int32 [64, 512], P('gx'), may hold values 0 or 1
- turbine_cells: int32 [3, 100], replicated, may hold values from 0 to 511, as said below
- yaw_bin: int32 [100], replicated, may hold values from 0 to 11
- yaw_table: float32 [3, 12], replicated, may hold values from -20 to 20
Outputs:
- adjoint_out: float32 [3, 128, 64, 512], P(None, 'gz', 'gx')
Inputs may be any that keep to these rules, and one draw needn't show every extreme that they name: `turbine_cells`: row 0 holds a turbine's vertical cell, below 128; row 1 its streamwise cell, below 64; row 2 its spanwise cell, below 512. Turbines may share a cell. Some turbine stands in the cell (0, 0, 0) and some in the cell (127, 63, 511).
All inputs are finite; a program needn't handle non-finite values. No bound on the sum of `ground_mask` on one device may be relied on, other than what follows from the above.
Results may differ from a plain program's by a relative error of at most 0.0003.
Values sent between devices are 32-bit elements; how exact they have to be, the bound alone decides.
No kernel may reach another device: no remote copies, remote signals or barrier semaphores. Data moves between devices by JAX's collectives and lax.ppermute only.
A program may use at most 192 MiB of HBM per device.

v0:
```python
import jax
import jax.numpy as jnp
from jax import lax
from jax.sharding import PartitionSpec as P

SWEEPS = 2


PSEUDO_STEP = 0.2
LATERAL_VISC = 1.0


def padded_2(cells, sides, width):
    for axis, dim in sides:
        count = lax.axis_size(axis)
        ends = count - 1
        head = lax.slice_in_dim(cells, 0, width, axis=dim)
        tail = lax.slice_in_dim(cells, cells.shape[dim] - width, cells.shape[dim], axis=dim)
        cells = jnp.concatenate(
            [
                lax.ppermute(tail, axis, [(i, (i + 1) % count) for i in range(ends)]),
                cells,
                lax.ppermute(head, axis, [((i + 1) % count, i) for i in range(ends)]),
            ],
            axis=dim,
        )
    return cells


def thomas(sub_diag, main_diag, super_diag, right_side):

    def forward(carry, row_values):
        ratio_prev, value_prev = carry
        lower_c, centre, upper_c, target = row_values
        pivot = centre - lower_c * ratio_prev
        ratio_next = upper_c / pivot
        value_next = (target - lower_c * value_prev) / pivot
        return ((ratio_next, value_next), (ratio_next, value_next))

    start = (
        jnp.zeros(super_diag.shape[1:], jnp.float32),
        jnp.zeros(right_side.shape[1:], jnp.float32),
    )
    _, (ratios, values) = lax.scan(forward, start, (sub_diag, main_diag, super_diag, right_side))

    def backward(later, row_values):
        ratio_here, value_here = row_values
        result = value_here - ratio_here * later
        return (result, result)

    _, solved = lax.scan(
        backward, jnp.zeros(right_side.shape[1:], jnp.float32), (ratios, values), reverse=True
    )
    return solved


def lateral(adjoint_now, base_flow, x_minus, x_plus):
    padded_y = jnp.pad(adjoint_now, ((0, 0), (0, 0), (0, 0), (1, 1)))
    y_minus = padded_y[:, :, :, :-2]
    y_plus = padded_y[:, :, :, 2:]
    advect = base_flow[0:1] * (x_plus - x_minus) * 0.5 + base_flow[1:2] * (y_plus - y_minus) * 0.5
    spread = x_plus + x_minus + y_plus + y_minus - 4.0 * adjoint_now
    return adjoint_now + PSEUDO_STEP * (advect + LATERAL_VISC * spread)


def per_device(adjoint, base_flow, conductance, ground_mask, turbine_cells, yaw_bin, yaw_table):
    z_cells = adjoint.shape[1]
    x_cells = adjoint.shape[2]
    y_cells = adjoint.shape[3]
    columns = x_cells * y_cells
    slab_index = lax.axis_index("gz")
    strip_index = lax.axis_index("gx")
    bin_count = yaw_table.shape[1]
    selector = (yaw_bin[None, :] == jnp.arange(bin_count, dtype=jnp.int32)[:, None]).astype(
        jnp.float32
    )
    strengths = jnp.dot(yaw_table, selector, precision=lax.Precision.HIGHEST)
    local_z = turbine_cells[0] - slab_index * z_cells
    local_x = turbine_cells[1] - strip_index * x_cells
    inside = (local_z >= 0) & (local_z < z_cells) & (local_x >= 0) & (local_x < x_cells)
    weights = strengths * inside.astype(jnp.float32)[None, :]
    source = (
        jnp.zeros(adjoint.shape, jnp.float32)
        .at[
            :,
            jnp.clip(local_z, 0, z_cells - 1),
            jnp.clip(local_x, 0, x_cells - 1),
            turbine_cells[2],
        ]
        .add(weights)
    )
    cond_cols = conductance.reshape(z_cells, columns)
    wall_flag = ground_mask.reshape(columns).astype(jnp.float32)
    bottom_face = jnp.where(slab_index == 0, cond_cols[0] * wall_flag, cond_cols[0])
    low_face = jnp.concatenate([bottom_face[None], cond_cols[1:]], 0)
    zero_row = jnp.zeros((1, columns), jnp.float32)
    current = adjoint
    interior = z_cells - 1
    first_link = jnp.where(slab_index == 0, jnp.zeros((columns,), jnp.float32), cond_cols[0])
    sub_inner = jnp.concatenate([zero_row, -cond_cols[1:interior]], 0)
    super_inner = -cond_cols[1:z_cells]
    main_inner = 1.0 + low_face[:interior] + cond_cols[1:z_cells]
    spike_right = jnp.zeros((interior, 2, columns), jnp.float32)
    spike_right = spike_right.at[0, 0].set(first_link)
    spike_right = spike_right.at[interior - 1, 1].set(cond_cols[z_cells - 1])
    spikes = thomas(sub_inner[:, None], main_inner[:, None], super_inner[:, None], spike_right)
    spike_below = spikes[:, 0]
    spike_above = spikes[:, 1]
    face_part = jnp.stack(
        [
            cond_cols[0],
            spike_below[0],
            spike_above[0],
            spike_below[interior - 1],
            spike_above[interior - 1],
            cond_cols[z_cells - 1],
        ],
        0,
    )[None]
    face_all = lax.all_gather(face_part, "gz", axis=0, tiled=True)
    next_faces = jnp.concatenate([face_all[1:], jnp.zeros_like(face_all[:1])], 0)
    lower_link = -face_all[:, 5]
    upper_link = -next_faces[:, 0]
    centre = 1.0 + face_all[:, 5] + next_faces[:, 0]
    red_sub = lower_link * face_all[:, 3]
    red_main = lower_link * face_all[:, 4] + centre + upper_link * next_faces[:, 1]
    red_super = upper_link * next_faces[:, 2]
    for sweep_index in range(SWEEPS):
        padded = padded_2(current, (("gx", 2),), 1)
        right_side = lateral(current, base_flow, padded[:, :, :-2], padded[:, :, 2:]) + source
        stacked = jnp.moveaxis(right_side.reshape(3, z_cells, columns), 1, 0)
        local_part = thomas(
            sub_inner[:, None], main_inner[:, None], super_inner[:, None], stacked[:interior]
        )
        right_part = jnp.concatenate(
            [local_part[0], local_part[interior - 1], stacked[z_cells - 1]], 0
        )[None]
        right_all = lax.all_gather(right_part, "gz", axis=0, tiled=True)
        next_first = jnp.concatenate([right_all[1:, 0:3], jnp.zeros_like(right_all[:1, 0:3])], 0)
        red_right = (
            right_all[:, 6:9]
            - lower_link[:, None] * right_all[:, 3:6]
            - upper_link[:, None] * next_first
        )
        interface = thomas(red_sub[:, None], red_main[:, None], red_super[:, None], red_right)
        prev_top = lax.dynamic_index_in_dim(
            interface, jnp.maximum(slab_index - 1, 0), 0, keepdims=False
        )
        prev_top = prev_top * (slab_index > 0).astype(jnp.float32)
        own_top = lax.dynamic_index_in_dim(interface, slab_index, 0, keepdims=False)
        inner_values = (
            local_part
            + spike_below[:, None] * prev_top[None]
            + spike_above[:, None] * own_top[None]
        )
        solved = jnp.concatenate([inner_values, own_top[None]], 0)
        current = jnp.moveaxis(solved, 0, 1).reshape(adjoint.shape)
    return current


def solution(mesh):
    in_specs = (
        P(None, "gz", "gx", None),
        P(None, "gz", "gx", None),
        P("gz", "gx", None),
        P("gx", None),
        P(),
        P(),
        P(),
    )
    out_specs = P(None, "gz", "gx", None)
    return jax.shard_map(
        per_device, mesh=mesh, in_specs=in_specs, out_specs=out_specs, check_vma=False
    )
```

profile of v0, /device:TPU:0, one launch (start us, length us, event | category | flops | bytes accessed | tf_op | source)
XLA Modules:
  0.0 549.8 jit_solution(8781116341680570288)
XLA Ops:
  10.7 6.1 %collective-permute-start.1 = (f32[3,16,1,512]{3,1,2,0:T(8,128)}, f32[3,16,1,512]{3,1,2,0:T(8,128)}, u32[]{:S(2)}, u32[]{:S(2)}) collective-permute-start(f32[3,16,1,512]{3,1,2,0:T(8,128)} %copy.89), channel_id=1, source_target_pairs={{0,8},{8,16},{16,24},{1,9},{9,17},{17,25},{2,10},{10,18},{18,26},{... | collective-permute-start | bytes 294920 | tf_op jit(solution)/shard_map/ppermute | solution.py:21
  23.8 12.7 %while.174 = (s32[]{:T(128)}, f32[1,8192]{1,0:T(1,128)S(1)}, f32[2,8192]{1,0:T(2,128)S(1)}, f32[15,1,8192]{2,1,0:T(1,128)}, f32[15,2,8192]{2,1,0:T(2,128)S(1)}, ...) while((s32[]{:T(128)}, f32[1,8192]{1,0:T(1,128)S(1)}, ...), condition=%wide.region_6.7_spmd.clone, body=%wide.region_5.6_spmd.clone.sunk | while | flops 98307 | bytes 590460 | solution.py:44
  37.9 33.9 %while.175 = (s32[]{:T(128)}, f32[2,8192]{1,0:T(2,128)}, f32[15,2,8192]{2,1,0:T(2,128)S(1)}, f32[15,2,8192]{2,1,0:T(2,128)S(1)}, f32[15,1,8192]{2,1,0:T(1,128)}, /*index=5*/s32[]{:T(128)}, s32[]{:T(128)}, s32[]{:T(128)}) while((s32[]{:T(128)}, f32[2,8192]{1,0:T(2,128)}, f32[15,2,8192]{2,1,0:T(2,128)S(1)}, ...), condition=%wide.region_8.9_spmd.clone, body=%wide.region_7.8_spmd.clone.sunk | while | flops 49156 | bytes 360563 | solution.py:51
  76.9 21.5 %broadcast_in_dim.134 = f32[3,16,16,512]{0,3,2,1:T(8,128)} broadcast(f32[]{:T(128)} %constant.348.clone.1), dimensions={} | broadcast | bytes 1572868 | tf_op jit(solution)/shard_map/broadcast_in_dim | solution.py:83
  98.3 12.2 %scatter_fusion = f32[3,16,16,512]{0,3,2,1:T(8,128)} fusion(f32[3,16,16,512]{0,3,2,1:T(8,128)} %broadcast_in_dim.134, s32[100]{0:T(128)S(1)} %fusion.30, f32[100,3]{1,0:T(8,128)S(1)} %copy.71), kind=kCustom, calls=%fused_computation | custom fusion | flops 300 | bytes 4800 | tf_op jit(solution)/shard_map/scatter-add | solution.py:90
  110.5 38.3 %copy.72 = f32[3,16,16,512]{3,2,1,0:T(8,128)S(1)} copy(f32[3,16,16,512]{0,3,2,1:T(8,128)} %scatter_fusion) | data formatting | bytes 3145728 | tf_op jit(solution)/shard_map/scatter-add | solution.py:90
  150.9 6.9 %add_add_fusion.1 = f32[3,16,16,512]{3,2,1,0:T(8,128)} fusion(f32[3,16,16,512]{3,2,1,0:T(8,128)S(1)} %copy.72, f32[3,16,16,512]{3,2,1,0:T(8,128)} %param.31, f32[3,16,1,512]{3,2,1,0:T(1,128)S(1)} %copy.68, f32[3,16,1,512]{3,2,1,0:T(1,128)S(1)} %copy.70, f32[16,16,512]{2,1,0:T(8,128)S(1)} %get-tuple-element.1237, f32[16,16,512]{2,1,0:T(8,128)S(1)} %get-tuple-element.1236), kind=kLoop, calls=%fused_computation.89 | loop fusion | flops 6684672 | bytes 5963776 | tf_op jit(solution)/shard_map/add | solution.py:130
  163.9 49.0 %while.172 = (s32[]{:T(128)}, f32[1,8192]{1,0:T(1,128)}, f32[3,8192]{1,0:T(4,128)}, f32[15,1,8192]{2,1,0:T(1,128)}, f32[15,3,8192]{2,1,0:T(4,128)S(1)}, /*index=...) while((s32[]{:T(128)}, f32[1,8192]{1,0:T(1,128)}, ...), condition=%wide.region_2.3_spmd.clone, body=%wide.region_1.2_spmd.clone.sunk | while | flops 131075 | bytes 754300 | solution.py:44
  214.6 46.1 %while.173 = (s32[]{:T(128)}, f32[3,8192]{1,0:T(4,128)}, f32[15,3,8192]{2,1,0:T(4,128)S(1)}, f32[15,3,8192]{2,1,0:T(4,128)}, f32[15,1,8192]{2,1,0:T(1,128)}, /*index=5*/s32[]{:T(128)}, s32[]{:T(128)}, s32[]{:T(128)}) while((s32[]{:T(128)}, f32[3,8192]{1,0:T(4,128)}, f32[15,3,8192]{2,1,0:T(4,128)S(1)}, f32[15,3,8192]{2,1,0:T(4,128)}, ...), condition=%wide.region_4.5_spmd.clone, body=%wide.region_3.4_spmd.clone.sunk | while | flops 73732 | bytes 524403 | solution.py:51
  263.0 2.7 copy_bitcast_fusion.2
  267.2 5.1 slice_negate_fusion.1
  273.4 37.7 %all-gather.12.cloned.1.call-done = f32[8,9,8192]{2,1,0:T(8,128)} async-done(((f32[1,9,8192]{2,1,0:T(8,128)}), f32[8,9,8192]{2,1,0:T(8,128)}) %all-gather.12.cloned.1.call-update) | async-done | bytes 2359312 | tf_op jit(solution)/shard_map/all_gather | solution.py:138
  312.8 4.6 fusion.18
  319.4 26.3 %while.176 = (s32[]{:T(128)}, f32[1,8192]{1,0:T(1,128)}, f32[3,8192]{1,0:T(4,128)}, f32[8,1,8192]{2,1,0:T(1,128)}, f32[8,3,8192]{2,1,0:T(4,128)}, /*index=5*/f32...) while((s32[]{:T(128)}, f32[1,8192]{1,0:T(1,128)}, ...), condition=%wide.region_10.11_spmd.clone, body=%wide.region_9.10_spmd.clone.sunk | while | flops 131075 | bytes 853112 | solution.py:44
  346.9 25.1 %while.177 = (s32[]{:T(128)}, f32[3,8192]{1,0:T(4,128)}, f32[8,3,8192]{2,1,0:T(4,128)}, f32[8,3,8192]{2,1,0:T(4,128)}, f32[8,1,8192]{2,1,0:T(1,128)}, /*index=5*/s32[]{:T(128)}, s32[]{:T(128)}, s32[]{:T(128)}) while((s32[]{:T(128)}, f32[3,8192]{1,0:T(4,128)}, f32[8,3,8192]{2,1,0:T(4,128)}, f32[8,3,8192]{2,1,0:T(4,128)}, ...), condition=%wide.region_12.13_spmd.clone, body=%wide.region_11.12_spmd.clone.sunk | while | flops 73732 | bytes 622707 | solution.py:51
  376.9 2.9 reshape.259
  382.0 5.2 collective-permute-start.3
  395.2 29.7 %while.178 = (s32[]{:T(128)}, f32[1,8192]{1,0:T(1,128)S(1)}, f32[3,8192]{1,0:T(4,128)S(1)}, f32[15,1,8192]{2,1,0:T(1,128)S(1)}, f32[15,3,8192]{2,1,0:T(4,128)S(1...) while((s32[]{:T(128)}, f32[1,8192]{1,0:T(1,128)S(1)}, ...), condition=%wide.region_14.15_spmd.clone, body=%wide.region_13.14_spmd.clone.sunk | while | flops 131075 | bytes 819328 | solution.py:44
  426.5 16.7 %while.179 = (s32[]{:T(128)}, f32[3,8192]{1,0:T(4,128)S(1)}, f32[15,3,8192]{2,1,0:T(4,128)S(1)}, f32[15,3,8192]{2,1,0:T(4,128)}, f32[15,1,8192]{2,1,0:T(1,128)S(1)}, /*index=5*/s32[]{:T(128)}, s32[]{:T(128)}, s32[]{:T(128)}) while((s32[]{:T(128)}, f32[3,8192]{1,0:T(4,128)S(1)}, f32[15,3,8192]{2,1,0:T(4,128)S(1)}, ...), condition=%wide.region_16.17_spmd.clone, body=%wide.region_15.16_spmd.clone.sunk | while | flops 73732 | bytes 589939 | solution.py:51
  444.3 47.8 %all-gather.14.cloned.1.call-done = f32[8,9,8192]{2,1,0:T(8,128)} async-done(((f32[1,9,8192]{2,1,0:T(8,128)}), f32[8,9,8192]{2,1,0:T(8,128)}) %all-gather.14.cloned.1.call-update) | async-done | bytes 2359312 | tf_op jit(solution)/shard_map/all_gather | solution.py:138
  493.8 4.9 fusion.16
  500.1 21.0 %while.180 = (s32[]{:T(128)}, f32[1,8192]{1,0:T(1,128)S(1)}, f32[3,8192]{1,0:T(4,128)S(1)}, f32[8,1,8192]{2,1,0:T(1,128)S(1)}, f32[8,3,8192]{2,1,0:T(4,128)}, /*...) while((s32[]{:T(128)}, f32[1,8192]{1,0:T(1,128)S(1)}, ...), condition=%wide.region_18.19_spmd.clone, body=%wide.region_17.18_spmd.clone.sunk | while | flops 131075 | bytes 787068 | solution.py:44
  522.2 14.0 %while.181 = (s32[]{:T(128)}, f32[3,8192]{1,0:T(4,128)S(1)}, f32[8,3,8192]{2,1,0:T(4,128)}, f32[8,3,8192]{2,1,0:T(4,128)}, f32[8,1,8192]{2,1,0:T(1,128)S(1)}, /*index=5*/s32[]{:T(128)}, s32[]{:T(128)}, s32[]{:T(128)}) while((s32[]{:T(128)}, f32[3,8192]{1,0:T(4,128)S(1)}, f32[8,3,8192]{2,1,0:T(4,128)}, f32[8,3,8192]{2,1,0:T(4,128)}, ...), condition=%wide.region_20.21_spmd.clone, body=%wide.region_19.20_spmd.clone.sunk | while | flops 73732 | bytes 557171 | solution.py:51
  540.5 2.8 copy.83
  (401 shorter events, 336.4 us)
Async XLA Ops:
  6.5 70.0 %copy-start = (f32[3,12]{1,0:T(4,128)S(1)}, f32[3,12]{1,0:T(4,128)}, u32[]{:S(2)}) copy-start(f32[3,12]{1,0:T(4,128)} %param.37) | copy-start | bytes 436
  6.5 11.5 %copy-start.15 = (f32[16,16,512]{2,1,0:T(8,128)S(1)}, f32[16,16,512]{2,1,0:T(8,128)}, u32[]{:S(2)}) copy-start(f32[16,16,512]{2,1,0:T(8,128)} %param.33) | copy-start | bytes 1572868
  6.5 12.2 %copy-start.22 = (s32[16,512]{1,0:T(8,128)S(1)}, s32[16,512]{1,0:T(8,128)}, u32[]{:S(2)}) copy-start(s32[16,512]{1,0:T(8,128)} %param.34) | copy-start | bytes 98308
  6.5 259.2 %all-gather.10.cloned.1.call-start = ((), (), s32[]{:S(2)}) async-start(), calls=%async_computation | async-start | bytes 2359296 | tf_op jit(solution)/shard_map/all_gather | solution.py:120
  8.8 140.1 %collective-permute-start = (f32[3,16,1,512]{3,1,2,0:T(8,128)}, f32[3,16,1,512]{3,1,2,0:T(8,128)}, u32[]{:S(2)}, u32[]{:S(2)}) collective-permute-start(f32[3,16,1,512]{3,1,2,0:T(8,128)} %copy.88), channel_id=1, source_target_pairs={{8,0},{16,8},{24,16},{9,1},{17,9},{25,17},{10,2},{18,10},{26,18},{... | collective-permute-start | bytes 294920 | tf_op jit(solution)/shard_map/ppermute | solution.py:23
  10.7 139.1 %collective-permute-start.1 = (f32[3,16,1,512]{3,1,2,0:T(8,128)}, f32[3,16,1,512]{3,1,2,0:T(8,128)}, u32[]{:S(2)}, u32[]{:S(2)}) collective-permute-start(f32[3,16,1,512]{3,1,2,0:T(8,128)} %copy.89), channel_id=1, source_target_pairs={{0,8},{8,16},{16,24},{1,9},{9,17},{17,25},{2,10},{10,18},{18,26},{... | collective-permute-start | bytes 294920 | tf_op jit(solution)/shard_map/ppermute | solution.py:21
  36.6 35.3 %copy-start.21 = (f32[1,1,16,512]{3,2,1,0:T(8,128)S(1)}, f32[1,1,16,512]{3,2,1,0:T(8,128)}, u32[]{:S(2)}) copy-start(f32[1,1,16,512]{3,2,1,0:T(8,128)} %get-tuple-element.1244) | copy-start | bytes 98308
  36.6 35.4 %copy-start.20 = (f32[1,1,16,512]{3,1,2,0:T(1,128)S(1)}, f32[1,1,16,512]{3,1,2,0:T(1,128)}, u32[]{:S(2)}) copy-start(f32[1,1,16,512]{3,1,2,0:T(1,128)} %copy-done.19) | copy-start | bytes 98308
  73.0 3.5 copy-start.23
  73.0 3.6 copy-start.24
  73.0 238.1 %all-gather.12.cloned.1.call-start = ((), (), s32[]{:S(2)}) async-start(), calls=%async_computation.1 | async-start | bytes 4718592 | tf_op jit(solution)/shard_map/all_gather | solution.py:138
  76.5 74.4 %copy-start.5 = (f32[16,16,512]{2,1,0:T(8,128)}, f32[16,16,512]{2,1,0:T(8,128)S(1)}, u32[]{:S(2)}) copy-start(f32[16,16,512]{2,1,0:T(8,128)S(1)} %get-tuple-element.1236) | copy-start | bytes 1572868
  76.5 74.4 %copy-start.7 = (f32[16,16,512]{2,1,0:T(8,128)}, f32[16,16,512]{2,1,0:T(8,128)S(1)}, u32[]{:S(2)}) copy-start(f32[16,16,512]{2,1,0:T(8,128)S(1)} %get-tuple-element.1237) | copy-start | bytes 1572868
  160.4 2.0 copy-start.2
  262.7 229.4 %all-gather.14.cloned.1.call-start = ((), (), s32[]{:S(2)}) async-start(), calls=%async_computation.2 | async-start | bytes 4718592 | tf_op jit(solution)/shard_map/all_gather | solution.py:138
  380.0 7.3 %collective-permute-start.2 = (f32[3,16,1,512]{3,1,2,0:T(8,128)S(1)}, f32[3,16,1,512]{3,1,2,0:T(8,128)}, u32[]{:S(2)}, u32[]{:S(2)}) collective-permute-start(f32[3,16,1,512]{3,1,2,0:T(8,128)S(1)} %copy.75), channel_id=1, source_target_pairs={{8,0},{16,8},{24,16},{9,1},{17,9},{25,17},{10,2},{18,10},{26,18},{... | collective-permute-start | bytes 294920 | tf_op jit(solution)/shard_map/ppermute | solution.py:23
  382.0 7.1 %collective-permute-start.3 = (f32[3,16,1,512]{3,1,2,0:T(8,128)}, f32[3,16,1,512]{3,1,2,0:T(8,128)}, u32[]{:S(2)}, u32[]{:S(2)}) collective-permute-start(f32[3,16,1,512]{3,1,2,0:T(8,128)} %copy.77), channel_id=1, source_target_pairs={{0,8},{8,16},{16,24},{1,9},{9,17},{17,25},{2,10},{10,18},{18,26},{... | collective-permute-start | bytes 294920 | tf_op jit(solution)/shard_map/ppermute | solution.py:21
  387.2 2.9 copy-start.6
  387.2 2.9 copy-start.8
  443.3 50.5 %copy-start.12 = (f32[8,8192]{1,0:T(8,128)S(1)}, f32[8,8192]{1,0:T(8,128)}, u32[]{:S(2)}) copy-start(f32[8,8192]{1,0:T(8,128)} %get-tuple-element.1250) | copy-start | bytes 786436
  443.3 50.5 %copy-start.14 = (f32[8,8192]{1,0:T(8,128)S(1)}, f32[8,8192]{1,0:T(8,128)}, u32[]{:S(2)}) copy-start(f32[8,8192]{1,0:T(8,128)} %get-tuple-element.1251) | copy-start | bytes 786436
  522.2 15.0 %copy-start.3 = (f32[15,8192]{1,0:T(8,128)S(1)}, f32[15,8192]{1,0:T(8,128)}, u32[]{:S(2)}) copy-start(f32[15,8192]{1,0:T(8,128)} %get-tuple-element.1253) | copy-start | bytes 1474564
  522.2 15.0 %copy-start.4 = (f32[15,8192]{1,0:T(8,128)S(1)}, f32[15,8192]{1,0:T(8,128)}, u32[]{:S(2)}) copy-start(f32[15,8192]{1,0:T(8,128)} %get-tuple-element.1254) | copy-start | bytes 1474564
  538.4 4.9 copy-start.1
  (9 other events, 11.1 us)
Sparse Core Ops, SparseCore 0:
  73.1 30.1 all-gather.9
  262.8 48.2 all-gather.11
  444.4 47.7 all-gather.13
where the time goes:
time: 559 us; the launch traced here: 550 us
  other arithmetic  277 us (50%)
  local copies, waits for them, and re-layouts  158 us (28%)
  waiting for transfers between devices  86.2 us (15%)
  starting transfers between devices  14.3 us (3%)
  between operations  13.9 us (2%)
    dynamic_update_slice x183, other arithmetic, thomas(): lax.scan(forward, start, (sub_diag, main_diag, super_diag, right_side))  231 us
    all_gather x2, waiting for transfers between devices, per_device(): right_all = lax.all_gather(right_part, 'gz', axis=0, tiled=True)  85.5 us
    dynamic_slice x61, local copies, waits for them, and re-layouts, thomas(): lax.scan(forward, start, (sub_diag, main_diag, super_diag, right_side))  43 us
    scatter-add x1, local copies, waits for them, and re-layouts, per_device(): source = jnp.zeros(adjoint.shape, jnp.float32).at[:, jnp.clip(local_z, 0,...  38.3 us
    broadcast_in_dim x1, local copies, waits for them, and re-layouts, per_device(): jnp.zeros(adjoint.shape, jnp.float32)  21.5 us
    scatter-add x1, other arithmetic, per_device(): source = jnp.zeros(adjoint.shape, jnp.float32).at[:, jnp.clip(local_z, 0,...  12.2 us
    ppermute x2, starting transfers between devices, padded_2(): lax.ppermute(tail, axis, [(i, (i + 1) % count) for i in range(ends)])  11.3 us
  transfers between devices with their start and end apart: 7, of which 3 were waited for; matrix products, arithmetic and copies ran while one was open for 46% of the time, Pallas kernels for 0%

commit v1 on v0

v1 whole, which is shorter than its diff:
```python
import functools

import jax
import jax.numpy as jnp
from jax import lax
from jax.experimental import pallas as pl
from jax.experimental.pallas import tpu as pltpu
from jax.sharding import PartitionSpec as P

SWEEPS = 2
PSEUDO_STEP = 0.2
LATERAL_VISC = 1.0


F32 = jnp.float32
VMEM = pl.BlockSpec(memory_space=pltpu.VMEM)
SMEM = pl.BlockSpec(memory_space=pltpu.SMEM)
PARAMS = pltpu.CompilerParams(vmem_limit_bytes=48 * 1024 * 1024)


def call(body, outs, ins, specs=None, scratch=()):
    return pl.pallas_call(
        body,
        out_shape=[jax.ShapeDtypeStruct(s, F32) for s in outs],
        in_specs=specs or [VMEM] * len(ins),
        out_specs=[VMEM] * len(outs),
        scratch_shapes=list(scratch),
        compiler_params=PARAMS,
    )(*ins)


def slab_kernel(
    cells_ref, bin_ref, table_ref, cond_ref,
    source_ref, ratio_ref, recip_ref, bottom_ref, top_ref, keep_ref, send_ref,
):
    nz, nx, ny = cond_ref.shape
    z0 = lax.axis_index("gz") * nz
    x0 = lax.axis_index("gx") * nx
    half = lax.rem(lax.axis_index("gz"), 2)
    source_ref[...] = jnp.zeros(source_ref.shape, F32)
    lanes = lax.broadcasted_iota(jnp.int32, (1, ny), 1)

    def place(t, carry):
        lz = cells_ref[0, t] - z0
        lx = cells_ref[1, t] - x0
        inside = (lz >= 0) & (lz < nz) & (lx >= 0) & (lx < nx)

        @pl.when(inside)
        def _():
            here = lanes == cells_ref[2, t]
            for c in range(3):
                row = source_ref[c, lz, pl.ds(lx, 1), :]
                source_ref[c, lz, pl.ds(lx, 1), :] = row + jnp.where(
                    here, table_ref[c, bin_ref[t]], 0.0
                )

        return carry

    lax.fori_loop(0, cells_ref.shape[1], place, 0)

    ends = []
    for tile in range(2):
        rows = pl.ds(tile * 8, 8)
        sigma = jnp.ones((8, ny), F32)
        ratios = [None]
        for k in range(nz - 1):
            face = cond_ref[k + 1, rows, :]
            recip = 1.0 / (sigma + face)
            ratio = face * recip
            recip_ref[k, rows, :] = recip
            ratio_ref[k + 1, rows, :] = ratio
            sigma = 1.0 + sigma * ratio
            ratios.append(ratio)
        weight = 1.0 / sigma
        recip_ref[nz - 1, rows, :] = weight
        ratio_ref[0, rows, :] = jnp.zeros((8, ny), F32)
        top = weight
        top_ref[nz - 1, rows, :] = weight
        for k in range(nz - 2, -1, -1):
            weight = weight * ratios[k + 1]
            top_ref[k, rows, :] = weight
        cross = weight
        tau = jnp.ones((8, ny), F32)
        ratios = [None] * nz
        for k in range(nz - 2, -1, -1):
            face = cond_ref[k + 1, rows, :]
            ratios[k] = face / (tau + face)
            tau = 1.0 + tau * ratios[k]
        weight = 1.0 / tau
        bottom = weight
        bottom_ref[0, rows, :] = weight
        for k in range(nz - 1):
            weight = weight * ratios[k]
            bottom_ref[k + 1, rows, :] = weight
        ends.append((bottom + 1.0 / cond_ref[0, rows, :], cross, top))
    for i in range(3):
        keep_ref[i] = jnp.where(half == 0, ends[0][i], ends[1][i])
        send_ref[i] = jnp.where(half == 0, ends[1][i], ends[0][i])


def right_kernel(
    state_ref, flow_ref, source_ref, ratio_ref, recip_ref, halo_a_ref, halo_b_ref,
    solved_ref, keep_ref, send_ref,
):
    _, nz, nx, ny = state_ref.shape
    strip = lax.axis_index("gx")
    even = lax.rem(strip, 2) == 0
    half = lax.rem(lax.axis_index("gz"), 2)
    inner = ((strip > 0) & (strip < lax.axis_size("gx") - 1)).astype(F32)
    lanes = lax.broadcasted_iota(jnp.int32, (nx, ny), 1)
    rows = lax.broadcasted_iota(jnp.int32, (nx, ny), 0)
    values = [None] * 3
    for k in range(nz):
        u = 0.5 * PSEUDO_STEP * flow_ref[0, k]
        v = 0.5 * PSEUDO_STEP * flow_ref[1, k]
        visc = PSEUDO_STEP * LATERAL_VISC
        x_plus_w = visc + u
        x_minus_w = visc - u
        y_plus_w = jnp.where(lanes == ny - 1, 0.0, visc + v)
        y_minus_w = jnp.where(lanes == 0, 0.0, visc - v)
        ratio = ratio_ref[k]
        for c in range(3):
            a = state_ref[c, k]
            halo_a = halo_a_ref[c, k : k + 1, :]
            halo_b = halo_b_ref[c, k : k + 1, :] * inner
            left = jnp.where(even, halo_b, halo_a)
            right = jnp.where(even, halo_a, halo_b)
            x_minus = jnp.where(rows == 0, left, pltpu.roll(a, 1, 0))
            x_plus = jnp.where(rows == nx - 1, right, pltpu.roll(a, nx - 1, 0))
            y_minus = pltpu.roll(a, 1, 1)
            y_plus = pltpu.roll(a, ny - 1, 1)
            value = (
                (1.0 - 4.0 * visc) * a
                + x_plus_w * x_plus
                + x_minus_w * x_minus
                + y_plus_w * y_plus
                + y_minus_w * y_minus
                + source_ref[c, k]
            )
            if k:
                value = value + ratio * values[c]
            values[c] = value
            solved_ref[c, k] = value
    for k in range(nz - 1, -1, -1):
        recip = recip_ref[k]
        for c in range(3):
            value = solved_ref[c, k] * recip
            if k < nz - 1:
                value = value + ratio_ref[k + 1] * values[c]
            else:
                last = value
                keep_ref[3 + c] = jnp.where(half == 0, last[:8], last[8:])
                send_ref[3 + c] = jnp.where(half == 0, last[8:], last[:8])
            values[c] = value
            solved_ref[c, k] = value
    for c in range(3):
        first = values[c]
        keep_ref[c] = jnp.where(half == 0, first[:8], first[8:])
        send_ref[c] = jnp.where(half == 0, first[8:], first[:8])


def own_pair(half, keep_ref, recv_ref, i):
    mine, other = keep_ref[i], recv_ref[i]
    return jnp.where(half == 0, mine, other), jnp.where(half == 0, other, mine)


def chip_kernel(coef_keep, coef_recv, keep, recv, out_ref, mid_ref):
    half = lax.rem(lax.axis_index("gz"), 2)
    a0, a1 = own_pair(half, coef_keep, coef_recv, 0)
    c0, c1 = own_pair(half, coef_keep, coef_recv, 1)
    d0, d1 = own_pair(half, coef_keep, coef_recv, 2)
    inv = 1.0 / (d0 + a1)
    out_ref[6] = a0 - c0 * c0 * inv
    out_ref[7] = c0 * c1 * inv
    out_ref[8] = d1 - c1 * c1 * inv
    mid_ref[0] = inv
    mid_ref[1] = c0
    mid_ref[2] = c1
    for c in range(3):
        first0, first1 = own_pair(half, keep, recv, c)
        last0, last1 = own_pair(half, keep, recv, 3 + c)
        gap = last0 - first1
        current = gap * inv
        out_ref[c] = first0 - c0 * current
        out_ref[3 + c] = last1 + c1 * current
        mid_ref[3 + c] = current


def join_kernel(chips, *refs):
    own_ref, others = refs[0], refs[1:chips]
    mid_ref, mask_ref = refs[chips : chips + 2]
    keep_ref, send_ref, below_ref, above_ref, own_out, all_ref = refs[chips + 2 :]
    index = lax.axis_index("gz")
    chip, half = lax.div(index, 2), lax.rem(index, 2)
    all_ref[chip] = own_ref[...]
    for j in range(1, chips):
        all_ref[chip ^ j] = others[j - 1][...]
    mask = mask_ref[...].astype(F32)
    mask = jnp.where(half == 0, mask[:8], mask[8:])
    zero = jnp.zeros(mask.shape, F32)

    volt, imp = [zero] * 3, zero
    for t in range(chips - 1):
        inv = 1.0 / (all_ref[t, 6] + imp)
        if t == 0:
            inv = inv * mask
        cross = all_ref[t, 7]
        kappa = cross * inv
        below_ref[t] = kappa
        use = t < chip
        volt = [
            jnp.where(use, all_ref[t, 3 + c] + kappa * (volt[c] - all_ref[t, c]), volt[c])
            for c in range(3)
        ]
        imp = jnp.where(use, all_ref[t, 8] - kappa * cross, imp)
    low_volt, low_imp = volt, imp

    volt, imp = [zero] * 3, zero
    for t in range(chips - 1, 0, -1):
        cross = all_ref[t, 7]
        if t == chips - 1:
            kappa = zero
        else:
            kappa = cross / (all_ref[t, 8] + imp)
        above_ref[t] = kappa
        use = t > chip
        volt = [
            jnp.where(use, all_ref[t, c] + kappa * (volt[c] - all_ref[t, 3 + c]), volt[c])
            for c in range(3)
        ]
        imp = jnp.where(use, all_ref[t, 6] - kappa * cross, imp)
    high_volt, high_imp = volt, imp

    cross, near, far = own_ref[7], own_ref[6], own_ref[8]
    bottom_on = jnp.where(chip == 0, mask, 1.0)
    top_on = jnp.where(chip == chips - 1, 0.0, 1.0)
    up = cross * bottom_on / (near + low_imp)
    down = cross * top_on / (far + high_imp)
    bottom_g = bottom_on / (low_imp + near - down * cross)
    top_g = top_on / (high_imp + far - up * cross)
    own_out[0] = up
    own_out[1] = down
    own_out[2] = bottom_g
    own_out[3] = top_g
    inv, c0, c1 = mid_ref[0], mid_ref[1], mid_ref[2]
    for c in range(3):
        first, last = own_ref[c], own_ref[3 + c]
        j_bottom = (low_volt[c] - first - down * (high_volt[c] - last)) * bottom_g
        j_top = (last + up * (low_volt[c] - first) - high_volt[c]) * top_g
        j_mid = mid_ref[3 + c] + (c0 * j_bottom + c1 * j_top) * inv
        keep_ref[c] = jnp.where(half == 0, j_bottom, j_mid)
        keep_ref[3 + c] = jnp.where(half == 0, j_mid, j_top)
        send_ref[c] = jnp.where(half == 0, j_mid, j_bottom)
        send_ref[3 + c] = jnp.where(half == 0, j_top, j_mid)


def chip_again_kernel(chips, keep, recv, mid_ref, own_coef, *outs):
    volt_ref, parts = outs[0], outs[1:]
    index = lax.axis_index("gz")
    chip, half = lax.div(index, 2), lax.rem(index, 2)
    inv, c0, c1 = mid_ref[0], mid_ref[1], mid_ref[2]
    up, down = own_coef[0], own_coef[1]
    for c in range(3):
        first0, first1 = own_pair(half, keep, recv, c)
        last0, last1 = own_pair(half, keep, recv, 3 + c)
        current = (last0 - first1) * inv
        first = first0 - c0 * current
        last = last1 + c1 * current
        volt_ref[c] = first
        volt_ref[3 + c] = last
        volt_ref[6 + c] = current
        to_above = last - up * first
        to_below = first - down * last
        for j in range(1, chips):
            parts[j - 1][c] = jnp.where((chip ^ j) > chip, to_above, to_below)


def join_again_kernel(chips, *refs):
    others = refs[: chips - 1]
    volt_ref, mid_ref, below_ref, above_ref, own_coef = refs[chips - 1 : chips + 4]
    keep_ref, send_ref, all_ref = refs[chips + 4 :]
    index = lax.axis_index("gz")
    chip, half = lax.div(index, 2), lax.rem(index, 2)
    for j in range(1, chips):
        all_ref[chip ^ j] = others[j - 1][...]
    inv, c0, c1 = mid_ref[0], mid_ref[1], mid_ref[2]
    up, down, bottom_g, top_g = (own_coef[i] for i in range(4))
    for c in range(3):
        low = jnp.zeros(inv.shape, F32)
        for t in range(chips - 1):
            low = jnp.where(t < chip, all_ref[t, c] + below_ref[t] * low, low)
        high = jnp.zeros(inv.shape, F32)
        for t in range(chips - 1, 0, -1):
            high = jnp.where(t > chip, all_ref[t, c] + above_ref[t] * high, high)
        first, last = volt_ref[c], volt_ref[3 + c]
        j_bottom = (low - first - down * (high - last)) * bottom_g
        j_top = (last + up * (low - first) - high) * top_g
        j_mid = volt_ref[6 + c] + (c0 * j_bottom + c1 * j_top) * inv
        keep_ref[c] = jnp.where(half == 0, j_bottom, j_mid)
        keep_ref[3 + c] = jnp.where(half == 0, j_mid, j_top)
        send_ref[c] = jnp.where(half == 0, j_mid, j_bottom)
        send_ref[3 + c] = jnp.where(half == 0, j_top, j_mid)


def update_kernel(solved_ref, bottom_ref, top_ref, keep_ref, recv_ref, *outs):
    out_ref = outs[0]
    _, nz, nx, ny = solved_ref.shape
    half = lax.rem(lax.axis_index("gz"), 2)
    even = lax.rem(lax.axis_index("gx"), 2) == 0
    for c in range(3):
        j_bottom = jnp.concatenate(own_pair(half, keep_ref, recv_ref, c), 0)
        j_top = jnp.concatenate(own_pair(half, keep_ref, recv_ref, 3 + c), 0)
        for k in range(nz):
            value = solved_ref[c, k] + bottom_ref[k] * j_bottom - top_ref[k] * j_top
            out_ref[c, k] = value
            if len(outs) > 1:
                first, last = value[0:1], value[nx - 1 : nx]
                outs[1][c, k : k + 1, :] = jnp.where(even, last, first)
                outs[2][c, k : k + 1, :] = jnp.where(even, first, last)


def per_device(strips, slabs, adjoint, base_flow, conductance, ground_mask, turbine_cells, yaw_bin, yaw_table):
    _, nz, nx, ny = adjoint.shape
    chips = slabs // 2
    cube, field = (nz, nx, ny), adjoint.shape
    pair_a = [(i, i ^ 1) for i in range(strips)]
    pair_b = [((i + 1) % strips, ((i ^ 1) + 1) % strips) for i in range(strips)]
    cores = [(i, i ^ 1) for i in range(slabs)]

    def across(parts):
        return [
            lax.ppermute(part, "gz", [(i, i ^ (2 * (j + 1))) for i in range(slabs)])
            for j, part in enumerate(parts)
        ]

    odd = lax.rem(lax.axis_index("gx"), 2)
    edge_a = lax.dynamic_index_in_dim(adjoint, (1 - odd) * (nx - 1), 2, keepdims=False)
    edge_b = lax.dynamic_index_in_dim(adjoint, odd * (nx - 1), 2, keepdims=False)
    part = lambda n: (n, 8, ny)
    source, ratio, recip, bottom_w, top_w, coef_keep, coef_send = call(
        slab_kernel,
        [field, cube, cube, cube, cube, part(3), part(3)],
        (turbine_cells, yaw_bin, yaw_table, conductance),
        [SMEM, SMEM, SMEM, VMEM],
    )
    coef_recv = lax.ppermute(coef_send, "gz", cores)
    state = adjoint
    for sweep_index in range(SWEEPS):
        halo_a = lax.ppermute(edge_a, "gx", pair_a)
        halo_b = lax.ppermute(edge_b, "gx", pair_b)
        solved, keep, send = call(
            right_kernel,
            [field, part(6), part(6)],
            (state, base_flow, source, ratio, recip, halo_a, halo_b),
        )
        recv = lax.ppermute(send, "gz", cores)
        if sweep_index == 0:
            own, mid = call(chip_kernel, [part(9), part(6)], (coef_keep, coef_recv, keep, recv))
            others = across([own] * (chips - 1))
            j_keep, j_send, below, above, own_coef = call(
                functools.partial(join_kernel, chips),
                [part(6), part(6), (chips, 8, ny), (chips, 8, ny), part(4)],
                (own, *others, mid, ground_mask),
                scratch=[pltpu.VMEM((chips, 9, 8, ny), F32)],
            )
        else:
            volts, *parts = call(
                functools.partial(chip_again_kernel, chips),
                [part(9)] + [part(3)] * (chips - 1),
                (keep, recv, mid, own_coef),
            )
            others = across(parts)
            j_keep, j_send = call(
                functools.partial(join_again_kernel, chips),
                [part(6), part(6)],
                (*others, volts, mid, below, above, own_coef),
                scratch=[pltpu.VMEM((chips, 3, 8, ny), F32)],
            )
        j_recv = lax.ppermute(j_send, "gz", cores)
        last = sweep_index == SWEEPS - 1
        edges = [] if last else [(3, nz, ny)] * 2
        state, *edges = call(
            update_kernel, [field, *edges], (solved, bottom_w, top_w, j_keep, j_recv)
        )
        if not last:
            edge_a, edge_b = edges
    return state


def solution(mesh):
    in_specs = (
        P(None, "gz", "gx", None),
        P(None, "gz", "gx", None),
        P("gz", "gx", None),
        P("gx", None),
        P(),
        P(),
        P(),
    )
    out_specs = P(None, "gz", "gx", None)
    body = functools.partial(per_device, mesh.shape["gx"], mesh.shape["gz"])
    return jax.shard_map(body, mesh=mesh, in_specs=in_specs, out_specs=out_specs, check_vma=False)
```

time: 559 us -> 61.6 us (0.11); the launches traced: 550 us -> 61.3 us
  other arithmetic: 277 us -> 0 us
  local copies, waits for them, and re-layouts: 158 us -> 7.26 us
  waiting for transfers between devices: 86.2 us -> 26.5 us
  between operations: 13.9 us -> 0.13 us
  Pallas kernels: 0 us -> 11.1 us
    dynamic_update_slice x183 -> x0, other arithmetic: 231 us -> none  [thomas(): lax.scan(forward, start, (sub_diag, main_diag, super_diag, right_side))]
    all_gather x3 -> x0, waiting for transfers between devices: 85.5 us -> none  [the longest x2 85.5 us: per_device(): right_all = lax.all_gather(right_part, 'gz', axis=0, tiled=True)]
    dynamic_slice x61 -> x1, local copies, waits for them, and re-layouts: 43 us -> 1.64 us  [per_device(): lax.dynamic_index_in_dim(adjoint, odd * (nx - 1), 2, keepdims=False)]
    scatter-add x1 -> x0, local copies, waits for them, and re-layouts: 38.3 us -> none  [per_device(): source = jnp.zeros(adjoint.shape, jnp.float32).at[:, jnp.clip(local_z, 0,...]
    ppermute x4 -> x15, waiting for transfers between devices: 0.64 us -> 26.5 us  [the longest x6 16.8 us: across(): lax.ppermute(part, 'gz', [(i, i ^ 2 * (j + 1)) for i in range(slabs)])]
    broadcast_in_dim x3 -> x0, local copies, waits for them, and re-layouts: 22.5 us -> none  [the longest x1 21.5 us: per_device(): jnp.zeros(adjoint.shape, jnp.float32)]
    slice x12 -> x0, local copies, waits for them, and re-layouts: 12.8 us -> none  [the longest x2 3.52 us: per_device(): stacked[:interior]]
    scatter-add x1 -> x0, other arithmetic: 12.2 us -> none  [per_device(): source = jnp.zeros(adjoint.shape, jnp.float32).at[:, jnp.clip(local_z, 0,...]
  transfers between devices with their start and end apart: 7 -> 15, of which waited for: 3 -> 11; matrix products, arithmetic and copies ran while one was open for 46% -> 0% of each run, Pallas kernels for 0% -> 5%
where the time goes in v1:
time: 61.6 us; the launch traced here: 61.3 us
  waiting for transfers between devices  26.5 us (43%)
  starting transfers between devices  16.3 us (26%)
  Pallas kernels  11.1 us (18%)
  local copies, waits for them, and re-layouts  7.26 us (12%)
    ppermute x6, waiting for transfers between devices, across(): lax.ppermute(part, 'gz', [(i, i ^ 2 * (j + 1)) for i in range(slabs)])  16.8 us
    pallas_call x9, Pallas kernels, call(): pl.pallas_call(body, out_shape=[jax.ShapeDtypeStruct(s, F32) for s in out...  11.1 us
    ppermute x6, starting transfers between devices, across(): lax.ppermute(part, 'gz', [(i, i ^ 2 * (j + 1)) for i in range(slabs)])  8.9 us
    unnamed x18, local copies, waits for them, and re-layouts  5.62 us
    ppermute x2, starting transfers between devices, per_device(): halo_a = lax.ppermute(edge_a, 'gx', pair_a)  4.55 us
    ppermute x2, waiting for transfers between devices, per_device(): halo_a = lax.ppermute(edge_a, 'gx', pair_a)  3.65 us
    ppermute x2, waiting for transfers between devices, per_device(): j_recv = lax.ppermute(j_send, 'gz', cores)  2.58 us
    ppermute x2, starting transfers between devices, per_device(): halo_b = lax.ppermute(edge_b, 'gx', pair_b)  2.07 us
  transfers between devices with their start and end apart: 15, of which 11 were waited for; matrix products, arithmetic and copies ran while one was open for 0% of the time, Pallas kernels for 5%

profile of v1, /device:TPU:0, one launch (start us, length us, event | category | flops | bytes accessed | tf_op | source)
XLA Modules:
  0.0 61.3 jit_solution(10272989912720207692)
XLA Ops:
  0.0 1.6 %constant_dynamic-slice_fusion = (f32[3,16,1,512]{3,2,1,0:T(1,128)S(1)}, f32[3,16,1,512]{3,2,1,0:T(1,128)S(1)}) fusion(f32[3,16,16,512]{3,2,1,0:T(8,128)} %state_ref.1, s32[]{:T(128)S(6)} %select_n.8, s32[]{:T(128)S(6)} %select_n.7), kind=kLoop, calls=%fused_computation.2 | loop fusion | bytes 393224 | tf_op jit(solution)/shard_map/jit(dynamic_index_in_dim)/dynamic_slice | solution.py:338
  1.7 3.0 %collective-permute-start = (f32[3,16,512]{2,1,0:T(8,128)S(1)}, f32[3,16,512]{2,1,0:T(8,128)S(1)}, u32[]{:S(2)}, u32[]{:S(2)}) collective-permute-start(f32[3,16,512]{2,1,0:T(8,128)S(1)} %bitcast.6), channel_id=1, source_target_pairs={{0,8},{8,0},{16,24},{24,16},{1,9},{9,1},{17,25},{25,17},{2,10},{10... | collective-permute-start | bytes 294920 | tf_op jit(solution)/shard_map/ppermute | solution.py:349
  4.7 1.6 %collective-permute-start.1 = (f32[3,16,512]{2,1,0:T(8,128)S(1)}, f32[3,16,512]{2,1,0:T(8,128)S(1)}, u32[]{:S(2)}, u32[]{:S(2)}) collective-permute-start(f32[3,16,512]{2,1,0:T(8,128)S(1)} %bitcast.7), channel_id=1, source_target_pairs={{8,16},{16,8},{24,0},{0,24},{9,17},{17,9},{25,1},{1,25},{10,18},{1... | collective-permute-start | bytes 294920 | tf_op jit(solution)/shard_map/ppermute | solution.py:350
  6.2 1.0 %copy-done.3 = f32[16,16,512]{2,1,0:T(8,128)S(1)} copy-done((f32[16,16,512]{2,1,0:T(8,128)S(1)}, f32[16,16,512]{2,1,0:T(8,128)}, u32[]{:S(2)}) %copy-start.3) | copy-done | bytes 524312
  9.3 3.0 %shard_map.73 = (f32[3,16,16,512]{3,2,1,0:T(8,128)S(1)}, f32[16,16,512]{2,1,0:T(8,128)S(1)}, f32[16,16,512]{2,1,0:T(8,128)S(1)}, f32[16,16,512]{2,1,0:T(8,128)S(...) custom-call(s32[3,100]{1,0:T(4,128)S(1)} %copy-done.5, s32[100]{0:T(128)S(1)} %copy-done.7, ...), custom_call_target="tpu_custom_call" | custom-call | tf_op jit(solution)/shard_map/pallas_call | solution.py:22
  12.3 1.1 %copy-done = f32[3,16,16,512]{3,2,1,0:T(8,128)} copy-done((f32[3,16,16,512]{3,2,1,0:T(8,128)}, f32[3,16,16,512]{3,2,1,0:T(8,128)S(1)}, u32[]{:S(2)}) %copy-start) | copy-done | bytes 1572888
  13.5 1.4 %copy-done.2 = f32[3,16,16,512]{3,2,1,0:T(8,128)S(1)} copy-done((f32[3,16,16,512]{3,2,1,0:T(8,128)S(1)}, f32[3,16,16,512]{3,2,1,0:T(8,128)}, u32[]{:S(2)}) %copy-start.2) | copy-done | bytes 1572888
  14.9 3.0 %shard_map.74 = (f32[3,16,16,512]{3,2,1,0:T(8,128)S(1)}, f32[6,8,512]{2,1,0:T(8,128)S(1)}, f32[6,8,512]{2,1,0:T(8,128)S(1)}) custom-call(f32[3,16,16,512]{3,2,1,0:T(8,128)S(1)} %copy-done.2, f32[2,16,16,512]{3,2,1,0:T(8,128)S(1)} %copy-done.1, f32[3,16,16,512]{3,2,1,0:T(8,128)} %copy-done, f32[16,16,512]{2,1,0:T(8,128)S(1)} %get-tuple-element.35.ratio_ref, ...), custom_call_target="tpu_custom_call" | custom-call | tf_op jit(solution)/shard_map/pallas_call | solution.py:22
  18.5 0.9 %collective-permute-done.2.coef_recv = f32[3,8,512]{2,1,0:T(8,128)S(1)} collective-permute-done((f32[3,8,512]{2,1,0:T(8,128)S(1)}, f32[3,8,512]{2,1,0:T(8,128)S(1)}, u32[]{:S(2)}, u32[]{:S(2)}) %collective-permute-start.2) | collective-permute-done | bytes 49184 | tf_op jit(solution)/shard_map/ppermute | solution.py:346
  19.4 3.6 %collective-permute-start.6 = (f32[9,8,512]{2,1,0:T(8,128)S(1)}, f32[9,8,512]{2,1,0:T(8,128)S(1)}, u32[]{:S(2)}, u32[]{:S(2)}) collective-permute-start(f32[9,8,512]{2,1,0:T(8,128)S(1)} %get-tuple-element.44.refs_0_), channel_id=1, source_target_pairs={{0,6},{1,7},{2,4},{3,5},{4,2},{5,3},{6,0},{7,1},{8,14},{9,15},{10,... | collective-permute-start | bytes 442376 | tf_op jit(solution)/shard_map/ppermute | solution.py:332
  23.8 4.2 %collective-permute-done.6.refs_3_ = f32[9,8,512]{2,1,0:T(8,128)S(1)} collective-permute-done((f32[9,8,512]{2,1,0:T(8,128)S(1)}, f32[9,8,512]{2,1,0:T(8,128)S(1)}, u32[]{:S(2)}, u32[]{:S(2)}) %collective-permute-start.6) | collective-permute-done | bytes 147488 | tf_op jit(solution)/shard_map/ppermute | solution.py:332
  28.0 8.0 %collective-permute-done.5.refs_2_ = f32[9,8,512]{2,1,0:T(8,128)S(1)} collective-permute-done((f32[9,8,512]{2,1,0:T(8,128)S(1)}, f32[9,8,512]{2,1,0:T(8,128)S(1)}, u32[]{:S(2)}, u32[]{:S(2)}) %collective-permute-start.5) | collective-permute-done | bytes 147488 | tf_op jit(solution)/shard_map/ppermute | solution.py:332
  36.3 1.3 %collective-permute-done.7.recv_ref = f32[6,8,512]{2,1,0:T(8,128)S(1)} collective-permute-done((f32[6,8,512]{2,1,0:T(8,128)S(1)}, f32[6,8,512]{2,1,0:T(8,128)S(1)}, u32[]{:S(2)}, u32[]{:S(2)}) %collective-permute-start.7) | collective-permute-done | bytes 98336 | tf_op jit(solution)/shard_map/ppermute | solution.py:379
  38.0 1.5 %collective-permute-start.8 = (f32[3,16,512]{2,1,0:T(8,128)S(1)}, f32[3,16,512]{2,1,0:T(8,128)S(1)}, u32[]{:S(2)}, u32[]{:S(2)}) collective-permute-start(f32[3,16,512]{2,1,0:T(8,128)S(1)} %get-tuple-element.49), channel_id=1, source_target_pairs={{0,8},{8,0},{16,24},{24,16},{1,9},{9,1},{17,25},{25,17},{2,10},{10... | collective-permute-start | bytes 294920 | tf_op jit(solution)/shard_map/ppermute | solution.py:349
  40.1 3.6 %collective-permute-done.8.halo_a_ref = f32[3,16,512]{2,1,0:T(8,128)S(1)} collective-permute-done((f32[3,16,512]{2,1,0:T(8,128)S(1)}, f32[3,16,512]{2,1,0:T(8,128)S(1)}, u32[]{:S(2)}, u32[]{:S(2)}) %collective-permute-start.8) | collective-permute-done | bytes 98336 | tf_op jit(solution)/shard_map/ppermute | solution.py:349
  43.7 1.4 %collective-permute-done.9.halo_b_ref = f32[3,16,512]{2,1,0:T(8,128)S(1)} collective-permute-done((f32[3,16,512]{2,1,0:T(8,128)S(1)}, f32[3,16,512]{2,1,0:T(8,128)S(1)}, u32[]{:S(2)}, u32[]{:S(2)}) %collective-permute-start.9) | collective-permute-done | bytes 98336 | tf_op jit(solution)/shard_map/ppermute | solution.py:350
  45.1 3.0 %shard_map.78 = (f32[3,16,16,512]{3,2,1,0:T(8,128)S(1)}, f32[6,8,512]{2,1,0:T(8,128)S(1)}, f32[6,8,512]{2,1,0:T(8,128)S(1)}) custom-call(f32[3,16,16,512]{3,2,1,0:T(8,128)S(1)} %get-tuple-element.48.state_ref, f32[2,16,16,512]{3,2,1,0:T(8,128)S(1)} %copy-done.1, f32[3,16,16,512]{3,2,1,0:T(8,128)} %copy-done, f32[16,16,512]{2,1,0:T(8,128)S(1)} %get-tuple-element.35.ratio_ref, ...), custom_call_target="tpu_custom_call" | custom-call | tf_op jit(solution)/shard_map/pallas_call | solution.py:22
  48.2 1.3 %collective-permute-done.10.recv = f32[6,8,512]{2,1,0:T(8,128)S(1)} collective-permute-done((f32[6,8,512]{2,1,0:T(8,128)S(1)}, f32[6,8,512]{2,1,0:T(8,128)S(1)}, u32[]{:S(2)}, u32[]{:S(2)}) %collective-permute-start.10) | collective-permute-done | bytes 98336 | tf_op jit(solution)/shard_map/ppermute | solution.py:356
  49.6 3.0 %collective-permute-start.12 = (f32[3,8,512]{2,1,0:T(8,128)S(1)}, f32[3,8,512]{2,1,0:T(8,128)S(1)}, u32[]{:S(2)}, u32[]{:S(2)}) collective-permute-start(f32[3,8,512]{2,1,0:T(8,128)S(1)} %get-tuple-element.56), channel_id=1, source_target_pairs={{0,4},{1,5},{2,6},{3,7},{4,0},{5,1},{6,2},{7,3},{8,12},{9,13},{10,... | collective-permute-start | bytes 147464 | tf_op jit(solution)/shard_map/ppermute | solution.py:332
  52.6 1.3 %collective-permute-start.13 = (f32[3,8,512]{2,1,0:T(8,128)S(1)}, f32[3,8,512]{2,1,0:T(8,128)S(1)}, u32[]{:S(2)}, u32[]{:S(2)}) collective-permute-start(f32[3,8,512]{2,1,0:T(8,128)S(1)} %get-tuple-element.57), channel_id=1, source_target_pairs={{0,6},{1,7},{2,4},{3,5},{4,2},{5,3},{6,0},{7,1},{8,14},{9,15},{10,... | collective-permute-start | bytes 147464 | tf_op jit(solution)/shard_map/ppermute | solution.py:332
  54.3 1.1 %collective-permute-done.12.refs_1_ = f32[3,8,512]{2,1,0:T(8,128)S(1)} collective-permute-done((f32[3,8,512]{2,1,0:T(8,128)S(1)}, f32[3,8,512]{2,1,0:T(8,128)S(1)}, u32[]{:S(2)}, u32[]{:S(2)}) %collective-permute-start.12) | collective-permute-done | bytes 49184 | tf_op jit(solution)/shard_map/ppermute | solution.py:332
  55.4 3.1 %collective-permute-done.13.refs_2_ = f32[3,8,512]{2,1,0:T(8,128)S(1)} collective-permute-done((f32[3,8,512]{2,1,0:T(8,128)S(1)}, f32[3,8,512]{2,1,0:T(8,128)S(1)}, u32[]{:S(2)}, u32[]{:S(2)}) %collective-permute-start.13) | collective-permute-done | bytes 49184 | tf_op jit(solution)/shard_map/ppermute | solution.py:332
  58.7 1.3 %collective-permute-done.14.recv_ref = f32[6,8,512]{2,1,0:T(8,128)S(1)} collective-permute-done((f32[6,8,512]{2,1,0:T(8,128)S(1)}, f32[6,8,512]{2,1,0:T(8,128)S(1)}, u32[]{:S(2)}, u32[]{:S(2)}) %collective-permute-start.14) | collective-permute-done | bytes 98336 | tf_op jit(solution)/shard_map/ppermute | solution.py:379
  60.0 1.4 %shard_map.81 = f32[3,16,16,512]{3,2,1,0:T(8,128)} custom-call(f32[3,16,16,512]{3,2,1,0:T(8,128)S(1)} %get-tuple-element.51.solved_ref, f32[16,16,512]{2,1,0:T(8,128)S(1)} %get-tuple-element.38.bottom_ref, f32[16,16,512]{2,1,0:T(8,128)S(1)} %get-tuple-element.39.top_ref, f32[6,8,512]{2,1,0:T(8,128)S(1)} %get-tuple-element.61.keep_ref, ...), custom_call_target="tpu_custom_call" | custom-call | tf_op jit(solution)/shard_map/pallas_call | solution.py:22
  (34 shorter events, 5.4 us)
Async XLA Ops:
  0.0 13.4 %copy-start.1 = (f32[2,16,16,512]{3,2,1,0:T(8,128)S(1)}, f32[2,16,16,512]{3,2,1,0:T(8,128)}, u32[]{:S(2)}) copy-start(f32[2,16,16,512]{3,2,1,0:T(8,128)} %flow_ref.3) | copy-start | bytes 3145732
  1.7 11.8 %collective-permute-start = (f32[3,16,512]{2,1,0:T(8,128)S(1)}, f32[3,16,512]{2,1,0:T(8,128)S(1)}, u32[]{:S(2)}, u32[]{:S(2)}) collective-permute-start(f32[3,16,512]{2,1,0:T(8,128)S(1)} %bitcast.6), channel_id=1, source_target_pairs={{0,8},{8,0},{16,24},{24,16},{1,9},{9,1},{17,25},{25,17},{2,10},{10... | collective-permute-start | bytes 294920 | tf_op jit(solution)/shard_map/ppermute | solution.py:349
  4.7 8.8 %collective-permute-start.1 = (f32[3,16,512]{2,1,0:T(8,128)S(1)}, f32[3,16,512]{2,1,0:T(8,128)S(1)}, u32[]{:S(2)}, u32[]{:S(2)}) collective-permute-start(f32[3,16,512]{2,1,0:T(8,128)S(1)} %bitcast.7), channel_id=1, source_target_pairs={{8,16},{16,8},{24,0},{0,24},{9,17},{17,9},{25,1},{1,25},{10,18},{1... | collective-permute-start | bytes 294920 | tf_op jit(solution)/shard_map/ppermute | solution.py:350
  6.2 1.0 %copy-start.3 = (f32[16,16,512]{2,1,0:T(8,128)S(1)}, f32[16,16,512]{2,1,0:T(8,128)}, u32[]{:S(2)}) copy-start(f32[16,16,512]{2,1,0:T(8,128)} %cond_ref.1) | copy-start | bytes 1572868
  7.3 0.7 %copy-start.5 = (s32[3,100]{1,0:T(4,128)S(1)}, s32[3,100]{1,0:T(4,128)}, u32[]{:S(2)}) copy-start(s32[3,100]{1,0:T(4,128)} %cells_ref.1) | copy-start | bytes 3604
  7.9 0.7 %copy-start.6 = (f32[3,12]{1,0:T(4,128)S(1)}, f32[3,12]{1,0:T(4,128)}, u32[]{:S(2)}) copy-start(f32[3,12]{1,0:T(4,128)} %table_ref.1) | copy-start | bytes 436
  8.6 0.7 %copy-start.7 = (s32[100]{0:T(128)S(1)}, s32[100]{0:T(128)}, u32[]{:S(2)}) copy-start(s32[100]{0:T(128)} %bin_ref.1) | copy-start | bytes 1204
  12.3 1.1 %copy-start = (f32[3,16,16,512]{3,2,1,0:T(8,128)}, f32[3,16,16,512]{3,2,1,0:T(8,128)S(1)}, u32[]{:S(2)}) copy-start(f32[3,16,16,512]{3,2,1,0:T(8,128)S(1)} %get-tuple-element.34.source_ref) | copy-start | bytes 4718596
  13.4 1.4 %copy-start.2 = (f32[3,16,16,512]{3,2,1,0:T(8,128)S(1)}, f32[3,16,16,512]{3,2,1,0:T(8,128)}, u32[]{:S(2)}) copy-start(f32[3,16,16,512]{3,2,1,0:T(8,128)} %state_ref.1) | copy-start | bytes 4718596
  14.9 21.2 %copy-start.4 = (s32[16,512]{1,0:T(8,128)S(1)}, s32[16,512]{1,0:T(8,128)}, u32[]{:S(2)}) copy-start(s32[16,512]{1,0:T(8,128)} %refs_5_.1) | copy-start | bytes 98308
  17.9 1.5 %collective-permute-start.3 = (f32[6,8,512]{2,1,0:T(8,128)S(1)}, f32[6,8,512]{2,1,0:T(8,128)S(1)}, u32[]{:S(2)}, u32[]{:S(2)}) collective-permute-start(f32[6,8,512]{2,1,0:T(8,128)S(1)} %get-tuple-element.43), channel_id=1, source_target_pairs={{0,1},{1,0},{2,3},{3,2},{4,5},{5,4},{6,7},{7,6},{8,9},{9,8},{10,11... | collective-permute-start | bytes 294920 | tf_op jit(solution)/shard_map/ppermute | solution.py:356
  18.0 1.4 %collective-permute-start.2 = (f32[3,8,512]{2,1,0:T(8,128)S(1)}, f32[3,8,512]{2,1,0:T(8,128)S(1)}, u32[]{:S(2)}, u32[]{:S(2)}) collective-permute-start(f32[3,8,512]{2,1,0:T(8,128)S(1)} %get-tuple-element.41), channel_id=1, source_target_pairs={{0,1},{1,0},{2,3},{3,2},{4,5},{5,4},{6,7},{7,6},{8,9},{9,8},{10,11... | collective-permute-start | bytes 147464 | tf_op jit(solution)/shard_map/ppermute | solution.py:346
  19.4 8.6 %collective-permute-start.6 = (f32[9,8,512]{2,1,0:T(8,128)S(1)}, f32[9,8,512]{2,1,0:T(8,128)S(1)}, u32[]{:S(2)}, u32[]{:S(2)}) collective-permute-start(f32[9,8,512]{2,1,0:T(8,128)S(1)} %get-tuple-element.44.refs_0_), channel_id=1, source_target_pairs={{0,6},{1,7},{2,4},{3,5},{4,2},{5,3},{6,0},{7,1},{8,14},{9,15},{10,... | collective-permute-start | bytes 442376 | tf_op jit(solution)/shard_map/ppermute | solution.py:332
  23.0 13.0 %collective-permute-start.5 = (f32[9,8,512]{2,1,0:T(8,128)S(1)}, f32[9,8,512]{2,1,0:T(8,128)S(1)}, u32[]{:S(2)}, u32[]{:S(2)}) collective-permute-start(f32[9,8,512]{2,1,0:T(8,128)S(1)} %get-tuple-element.44.refs_0_), channel_id=1, source_target_pairs={{0,4},{1,5},{2,6},{3,7},{4,0},{5,1},{6,2},{7,3},{8,12},{9,13},{10,... | collective-permute-start | bytes 442376 | tf_op jit(solution)/shard_map/ppermute | solution.py:332
  23.0 13.0 %collective-permute-start.4 = (f32[9,8,512]{2,1,0:T(8,128)S(1)}, f32[9,8,512]{2,1,0:T(8,128)S(1)}, u32[]{:S(2)}, u32[]{:S(2)}) collective-permute-start(f32[9,8,512]{2,1,0:T(8,128)S(1)} %get-tuple-element.44.refs_0_), channel_id=1, source_target_pairs={{0,2},{1,3},{2,0},{3,1},{4,6},{5,7},{6,4},{7,5},{8,10},{9,11},{10,... | collective-permute-start | bytes 442376 | tf_op jit(solution)/shard_map/ppermute | solution.py:332
  36.2 1.4 %collective-permute-start.7 = (f32[6,8,512]{2,1,0:T(8,128)S(1)}, f32[6,8,512]{2,1,0:T(8,128)S(1)}, u32[]{:S(2)}, u32[]{:S(2)}) collective-permute-start(f32[6,8,512]{2,1,0:T(8,128)S(1)} %get-tuple-element.47), channel_id=1, source_target_pairs={{0,1},{1,0},{2,3},{3,2},{4,5},{5,4},{6,7},{7,6},{8,9},{9,8},{10,11... | collective-permute-start | bytes 294920 | tf_op jit(solution)/shard_map/ppermute | solution.py:379
  38.0 5.7 %collective-permute-start.8 = (f32[3,16,512]{2,1,0:T(8,128)S(1)}, f32[3,16,512]{2,1,0:T(8,128)S(1)}, u32[]{:S(2)}, u32[]{:S(2)}) collective-permute-start(f32[3,16,512]{2,1,0:T(8,128)S(1)} %get-tuple-element.49), channel_id=1, source_target_pairs={{0,8},{8,0},{16,24},{24,16},{1,9},{9,1},{17,25},{25,17},{2,10},{10... | collective-permute-start | bytes 294920 | tf_op jit(solution)/shard_map/ppermute | solution.py:349
  39.5 5.5 %collective-permute-start.9 = (f32[3,16,512]{2,1,0:T(8,128)S(1)}, f32[3,16,512]{2,1,0:T(8,128)S(1)}, u32[]{:S(2)}, u32[]{:S(2)}) collective-permute-start(f32[3,16,512]{2,1,0:T(8,128)S(1)} %get-tuple-element.50), channel_id=1, source_target_pairs={{8,16},{16,8},{24,0},{0,24},{9,17},{17,9},{25,1},{1,25},{10,18},{1... | collective-permute-start | bytes 294920 | tf_op jit(solution)/shard_map/ppermute | solution.py:350
  48.1 1.4 %collective-permute-start.10 = (f32[6,8,512]{2,1,0:T(8,128)S(1)}, f32[6,8,512]{2,1,0:T(8,128)S(1)}, u32[]{:S(2)}, u32[]{:S(2)}) collective-permute-start(f32[6,8,512]{2,1,0:T(8,128)S(1)} %get-tuple-element.53), channel_id=1, source_target_pairs={{0,1},{1,0},{2,3},{3,2},{4,5},{5,4},{6,7},{7,6},{8,9},{9,8},{10,11... | collective-permute-start | bytes 294920 | tf_op jit(solution)/shard_map/ppermute | solution.py:356
  49.5 4.8 %collective-permute-start.11 = (f32[3,8,512]{2,1,0:T(8,128)S(1)}, f32[3,8,512]{2,1,0:T(8,128)S(1)}, u32[]{:S(2)}, u32[]{:S(2)}) collective-permute-start(f32[3,8,512]{2,1,0:T(8,128)S(1)} %get-tuple-element.55), channel_id=1, source_target_pairs={{0,2},{1,3},{2,0},{3,1},{4,6},{5,7},{6,4},{7,5},{8,10},{9,11},{10,... | collective-permute-start | bytes 147464 | tf_op jit(solution)/shard_map/ppermute | solution.py:332
  49.6 5.8 %collective-permute-start.12 = (f32[3,8,512]{2,1,0:T(8,128)S(1)}, f32[3,8,512]{2,1,0:T(8,128)S(1)}, u32[]{:S(2)}, u32[]{:S(2)}) collective-permute-start(f32[3,8,512]{2,1,0:T(8,128)S(1)} %get-tuple-element.56), channel_id=1, source_target_pairs={{0,4},{1,5},{2,6},{3,7},{4,0},{5,1},{6,2},{7,3},{8,12},{9,13},{10,... | collective-permute-start | bytes 147464 | tf_op jit(solution)/shard_map/ppermute | solution.py:332
  52.6 5.9 %collective-permute-start.13 = (f32[3,8,512]{2,1,0:T(8,128)S(1)}, f32[3,8,512]{2,1,0:T(8,128)S(1)}, u32[]{:S(2)}, u32[]{:S(2)}) collective-permute-start(f32[3,8,512]{2,1,0:T(8,128)S(1)} %get-tuple-element.57), channel_id=1, source_target_pairs={{0,6},{1,7},{2,4},{3,5},{4,2},{5,3},{6,0},{7,1},{8,14},{9,15},{10,... | collective-permute-start | bytes 147464 | tf_op jit(solution)/shard_map/ppermute | solution.py:332
  58.6 1.4 %collective-permute-start.14 = (f32[6,8,512]{2,1,0:T(8,128)S(1)}, f32[6,8,512]{2,1,0:T(8,128)S(1)}, u32[]{:S(2)}, u32[]{:S(2)}) collective-permute-start(f32[6,8,512]{2,1,0:T(8,128)S(1)} %get-tuple-element.62), channel_id=1, source_target_pairs={{0,1},{1,0},{2,3},{3,2},{4,5},{5,4},{6,7},{7,6},{8,9},{9,8},{10,11... | collective-permute-start | bytes 294920 | tf_op jit(solution)/shard_map/ppermute | solution.py:379

commit v2 on v1

v2 whole, which is shorter than its diff:
```python
import functools

import jax
import jax.numpy as jnp
from jax import lax
from jax.experimental import pallas as pl
from jax.experimental.pallas import tpu as pltpu
from jax.sharding import PartitionSpec as P

SWEEPS = 2
PSEUDO_STEP = 0.2
LATERAL_VISC = 1.0


F32 = jnp.float32
EARLY = True
AFTER_EDGE = lambda x: [x]
AFTER_SOURCE = lambda x: [x]
VMEM = pl.BlockSpec(memory_space=pltpu.VMEM)
SMEM = pl.BlockSpec(memory_space=pltpu.SMEM)
ANY = pl.BlockSpec(memory_space=pl.ANY)
PARAMS = pltpu.CompilerParams(vmem_limit_bytes=12 * 1024 * 1024)


def call(body, outs, ins, cost_us, specs=None, scratch=(), after=()):
    def run(*refs):
        body(*refs[: len(ins)], *refs[len(ins) + len(after) :])

    return pl.pallas_call(
        run,
        out_shape=[jax.ShapeDtypeStruct(s, F32) for s in outs],
        in_specs=(specs or [VMEM] * len(ins)) + [ANY] * len(after),
        out_specs=[VMEM] * len(outs),
        scratch_shapes=list(scratch),
        compiler_params=PARAMS,
        cost_estimate=pl.CostEstimate(
            flops=0, bytes_accessed=int(cost_us * 3.0e6), transcendentals=0
        ),
    )(*ins, *after)


def edge_kernel(state_ref, edge_a_ref, edge_b_ref):
    _, nz, nx, _ = state_ref.shape
    even = lax.rem(lax.axis_index("gx"), 2) == 0
    for c in range(3):
        for k in range(nz):
            first, last = state_ref[c, k, 0:1, :], state_ref[c, k, nx - 1 : nx, :]
            edge_a_ref[c, k : k + 1, :] = jnp.where(even, last, first)
            edge_b_ref[c, k : k + 1, :] = jnp.where(even, first, last)


def source_kernel(cells_ref, bin_ref, table_ref, source_ref):
    _, nz, nx, ny = source_ref.shape
    z0 = lax.axis_index("gz") * nz
    x0 = lax.axis_index("gx") * nx
    source_ref[...] = jnp.zeros(source_ref.shape, F32)
    lanes = lax.broadcasted_iota(jnp.int32, (1, ny), 1)

    def place(t, carry):
        lz = cells_ref[0, t] - z0
        lx = cells_ref[1, t] - x0
        inside = (lz >= 0) & (lz < nz) & (lx >= 0) & (lx < nx)

        @pl.when(inside)
        def _():
            here = lanes == cells_ref[2, t]
            for c in range(3):
                row = source_ref[c, lz, pl.ds(lx, 1), :]
                source_ref[c, lz, pl.ds(lx, 1), :] = row + jnp.where(
                    here, table_ref[c, bin_ref[t]], 0.0
                )

        return carry

    lax.fori_loop(0, cells_ref.shape[1], place, 0)


def slab_kernel(cond_ref, ratio_ref, recip_ref, bottom_ref, top_ref, keep_ref, send_ref):
    nz, nx, ny = cond_ref.shape
    half = lax.rem(lax.axis_index("gz"), 2)
    ends = []
    for tile in range(2):
        rows = pl.ds(tile * 8, 8)
        sigma = jnp.ones((8, ny), F32)
        tau = jnp.ones((8, ny), F32)
        for k in range(nz - 1):
            face = cond_ref[k + 1, rows, :]
            recip = 1.0 / (sigma + face)
            ratio = face * recip
            recip_ref[k, rows, :] = recip
            ratio_ref[k + 1, rows, :] = ratio
            sigma = 1.0 + sigma * ratio
            face = cond_ref[nz - 1 - k, rows, :]
            ratio = face / (tau + face)
            bottom_ref[nz - 1 - k, rows, :] = ratio
            tau = 1.0 + tau * ratio
        weight = 1.0 / sigma
        recip_ref[nz - 1, rows, :] = weight
        ratio_ref[0, rows, :] = jnp.zeros((8, ny), F32)
        top = weight
        top_ref[nz - 1, rows, :] = weight
        for k in range(nz - 2, -1, -1):
            weight = weight * ratio_ref[k + 1, rows, :]
            top_ref[k, rows, :] = weight
        cross = weight
        weight = 1.0 / tau
        bottom = weight
        bottom_ref[0, rows, :] = weight
        for k in range(1, nz):
            weight = weight * bottom_ref[k, rows, :]
            bottom_ref[k, rows, :] = weight
        ends.append((bottom + 1.0 / cond_ref[0, rows, :], cross, top))
    for i in range(3):
        keep_ref[i] = jnp.where(half == 0, ends[0][i], ends[1][i])
        send_ref[i] = jnp.where(half == 0, ends[1][i], ends[0][i])


def right_kernel(
    state_ref, flow_ref, source_ref, ratio_ref, recip_ref, bottom_ref, top_ref,
    solved_ref, ends_ref, *edge_refs,
):
    _, nz, nx, ny = state_ref.shape
    lanes = lax.broadcasted_iota(jnp.int32, (nx, ny), 1)
    rows = lax.broadcasted_iota(jnp.int32, (nx, ny), 0)
    visc = PSEUDO_STEP * LATERAL_VISC
    values = [None] * 3
    for k in range(nz):
        u = 0.5 * PSEUDO_STEP * flow_ref[0, k]
        v = 0.5 * PSEUDO_STEP * flow_ref[1, k]
        x_plus_w = visc + u
        x_minus_w = visc - u
        if edge_refs:
            edge_w, end_w = edge_refs
            for side, weight in ((0, x_minus_w[0:1]), (1, x_plus_w[nx - 1 : nx])):
                row = pl.ds(side * (nx - 1), 1)
                edge_w[side, k : k + 1, :] = weight
                end_w[side, 0, k : k + 1, :] = weight * bottom_ref[k, row, :]
                end_w[side, 1, k : k + 1, :] = weight * top_ref[k, row, :]
        x_plus_w = jnp.where(rows == nx - 1, 0.0, x_plus_w)
        x_minus_w = jnp.where(rows == 0, 0.0, x_minus_w)
        y_plus_w = jnp.where(lanes == ny - 1, 0.0, visc + v)
        y_minus_w = jnp.where(lanes == 0, 0.0, visc - v)
        ratio = ratio_ref[k]
        for c in range(3):
            a = state_ref[c, k]
            value = (
                (1.0 - 4.0 * visc) * a
                + x_plus_w * pltpu.roll(a, nx - 1, 0)
                + x_minus_w * pltpu.roll(a, 1, 0)
                + y_plus_w * pltpu.roll(a, ny - 1, 1)
                + y_minus_w * pltpu.roll(a, 1, 1)
                + source_ref[c, k]
            )
            if k:
                value = value + ratio * values[c]
            values[c] = value
            solved_ref[c, k] = value
    for k in range(nz - 1, -1, -1):
        recip = recip_ref[k]
        for c in range(3):
            value = solved_ref[c, k] * recip
            if k < nz - 1:
                value = value + ratio_ref[k + 1] * values[c]
            else:
                ends_ref[3 + c] = value
            values[c] = value
            solved_ref[c, k] = value
    for c in range(3):
        ends_ref[c] = values[c]


def halo_sides(halo_a_ref, halo_b_ref, c):
    strip = lax.axis_index("gx")
    even = lax.rem(strip, 2) == 0
    inner = ((strip > 0) & (strip < lax.axis_size("gx") - 1)).astype(F32)
    halo_a, halo_b = halo_a_ref[c], halo_b_ref[c] * inner
    return jnp.where(even, halo_b, halo_a), jnp.where(even, halo_a, halo_b)


def ends_kernel(ends_ref, halo_a_ref, halo_b_ref, end_w, keep_ref, send_ref):
    half = lax.rem(lax.axis_index("gz"), 2)
    rows = lax.broadcasted_iota(jnp.int32, (8, ends_ref.shape[2]), 0)
    for c in range(3):
        left, right = halo_sides(halo_a_ref, halo_b_ref, c)
        for e in range(2):
            low = jnp.sum(left * end_w[0, e], 0, keepdims=True)
            high = jnp.sum(right * end_w[1, e], 0, keepdims=True)
            i = 3 * e + c
            low = ends_ref[i, 0:8, :] + jnp.where(rows == 0, low, 0.0)
            high = ends_ref[i, 8:16, :] + jnp.where(rows == 7, high, 0.0)
            keep_ref[i] = jnp.where(half == 0, low, high)
            send_ref[i] = jnp.where(half == 0, high, low)


def halo_kernel(solved_ref, halo_a_ref, halo_b_ref, edge_w, ratio_ref, recip_ref, out_ref, right_ref):
    _, nz, nx, ny = solved_ref.shape
    rows = lax.broadcasted_iota(jnp.int32, (8, ny), 0)
    for c in range(3):
        for side, halo in enumerate(halo_sides(halo_a_ref, halo_b_ref, c)):
            right_ref[c, side] = halo * edge_w[side]
    for side in range(2):
        tile = pl.ds(8 * side, 8)
        here = rows == 7 * side
        values = [None] * 3
        for k in range(nz):
            ratio = ratio_ref[k, tile, :]
            for c in range(3):
                value = jnp.where(here, right_ref[c, side, k : k + 1, :], 0.0)
                if k:
                    value = value + ratio * values[c]
                values[c] = value
                out_ref[c, k, tile, :] = value
        for k in range(nz - 1, -1, -1):
            recip = recip_ref[k, tile, :]
            for c in range(3):
                value = out_ref[c, k, tile, :] * recip
                if k < nz - 1:
                    value = value + ratio_ref[k + 1, tile, :] * values[c]
                values[c] = value
                out_ref[c, k, tile, :] = value + solved_ref[c, k, tile, :]


def own_pair(half, keep_ref, recv_ref, i):
    mine, other = keep_ref[i], recv_ref[i]
    return jnp.where(half == 0, mine, other), jnp.where(half == 0, other, mine)


def chip_coef_kernel(keep, recv, out_ref, mid_ref):
    half = lax.rem(lax.axis_index("gz"), 2)
    a0, a1 = own_pair(half, keep, recv, 0)
    c0, c1 = own_pair(half, keep, recv, 1)
    d0, d1 = own_pair(half, keep, recv, 2)
    inv = 1.0 / (d0 + a1)
    out_ref[0] = a0 - c0 * c0 * inv
    out_ref[1] = c0 * c1 * inv
    out_ref[2] = d1 - c1 * c1 * inv
    mid_ref[0] = inv
    mid_ref[1] = c0
    mid_ref[2] = c1


def join_coef_kernel(chips, *refs):
    own_ref, others, mask_ref = refs[0], refs[1:chips], refs[chips]
    below_ref, above_ref, own_out, all_ref = refs[chips + 1 :]
    index = lax.axis_index("gz")
    chip, half = lax.div(index, 2), lax.rem(index, 2)
    all_ref[chip] = own_ref[...]
    for j in range(1, chips):
        all_ref[chip ^ j] = others[j - 1][...]
    mask = mask_ref[...].astype(F32)
    mask = jnp.where(half == 0, mask[:8], mask[8:])
    zero = jnp.zeros(mask.shape, F32)

    low = zero
    for t in range(chips - 1):
        cross = all_ref[t, 1]
        kappa = cross / (all_ref[t, 0] + low)
        if t == 0:
            kappa = kappa * mask
        below_ref[t] = kappa
        low = jnp.where(t < chip, all_ref[t, 2] - kappa * cross, low)
    below_ref[chips - 1] = zero

    high = zero
    above_ref[chips - 1] = zero
    above_ref[0] = zero
    for t in range(chips - 1, 0, -1):
        cross = all_ref[t, 1]
        kappa = zero if t == chips - 1 else cross / (all_ref[t, 2] + high)
        above_ref[t] = kappa
        high = jnp.where(t > chip, all_ref[t, 0] - kappa * cross, high)

    near, cross, far = own_ref[0], own_ref[1], own_ref[2]
    bottom_on = jnp.where(chip == 0, mask, 1.0)
    top_on = jnp.where(chip == chips - 1, 0.0, 1.0)
    up = cross * bottom_on / (near + low)
    down = cross * top_on / (far + high)
    own_out[0] = up
    own_out[1] = down
    own_out[2] = bottom_on / (low + near - down * cross)
    own_out[3] = top_on / (high + far - up * cross)


def chip_values(half, keep, recv, mid_ref, volt_ref, c):
    inv, c0, c1 = mid_ref[0], mid_ref[1], mid_ref[2]
    first0, first1 = own_pair(half, keep, recv, c)
    last0, last1 = own_pair(half, keep, recv, 3 + c)
    current = (last0 - first1) * inv
    first = first0 - c0 * current
    last = last1 + c1 * current
    volt_ref[c] = first
    volt_ref[3 + c] = last
    volt_ref[6 + c] = current
    return first, last


def chip_kernel(keep, recv, mid_ref, volt_ref, own_ref):
    half = lax.rem(lax.axis_index("gz"), 2)
    for c in range(3):
        own_ref[c], own_ref[3 + c] = chip_values(half, keep, recv, mid_ref, volt_ref, c)


def chip_again_kernel(chips, keep, recv, mid_ref, own_coef, volt_ref, *parts):
    index = lax.axis_index("gz")
    chip, half = lax.div(index, 2), lax.rem(index, 2)
    up, down = own_coef[0], own_coef[1]
    for c in range(3):
        first, last = chip_values(half, keep, recv, mid_ref, volt_ref, c)
        to_above = last - up * first
        to_below = first - down * last
        for j in range(1, chips):
            parts[j - 1][c] = jnp.where((chip ^ j) > chip, to_above, to_below)


def join_kernel(chips, scaled, *refs):
    others = refs[: chips - 1]
    volt_ref, mid_ref, below_ref, above_ref, own_coef = refs[chips - 1 : chips + 4]
    keep_ref, send_ref, all_ref = refs[chips + 4 :]
    index = lax.axis_index("gz")
    chip, half = lax.div(index, 2), lax.rem(index, 2)
    for j in range(1, chips):
        all_ref[chip ^ j] = others[j - 1][...]
    all_ref[chip] = jnp.zeros(all_ref.shape[1:], F32)
    inv, c0, c1 = mid_ref[0], mid_ref[1], mid_ref[2]
    up, down, bottom_g, top_g = (own_coef[i] for i in range(4))
    for c in range(3):
        low = jnp.zeros(inv.shape, F32)
        for t in range(chips - 1):
            if scaled:
                value = all_ref[t, c] + below_ref[t] * low
            else:
                value = all_ref[t, 3 + c] + below_ref[t] * (low - all_ref[t, c])
            low = jnp.where(t < chip, value, low)
        high = jnp.zeros(inv.shape, F32)
        for t in range(chips - 1, 0, -1):
            if scaled:
                value = all_ref[t, c] + above_ref[t] * high
            else:
                value = all_ref[t, c] + above_ref[t] * (high - all_ref[t, 3 + c])
            high = jnp.where(t > chip, value, high)
        first, last = volt_ref[c], volt_ref[3 + c]
        j_bottom = (low - first - down * (high - last)) * bottom_g
        j_top = (last + up * (low - first) - high) * top_g
        j_mid = volt_ref[6 + c] + (c0 * j_bottom + c1 * j_top) * inv
        keep_ref[c] = jnp.where(half == 0, j_bottom, j_mid)
        keep_ref[3 + c] = jnp.where(half == 0, j_mid, j_top)
        send_ref[c] = jnp.where(half == 0, j_mid, j_bottom)
        send_ref[3 + c] = jnp.where(half == 0, j_top, j_mid)


def update_kernel(solved_ref, bottom_ref, top_ref, keep_ref, recv_ref, *outs):
    out_ref = outs[0]
    _, nz, nx, ny = solved_ref.shape
    half = lax.rem(lax.axis_index("gz"), 2)
    even = lax.rem(lax.axis_index("gx"), 2) == 0
    for c in range(3):
        j_bottom = jnp.concatenate(own_pair(half, keep_ref, recv_ref, c), 0)
        j_top = jnp.concatenate(own_pair(half, keep_ref, recv_ref, 3 + c), 0)
        for k in range(nz):
            value = solved_ref[c, k] + bottom_ref[k] * j_bottom - top_ref[k] * j_top
            out_ref[c, k] = value
            if len(outs) > 1:
                first, last = value[0:1], value[nx - 1 : nx]
                outs[1][c, k : k + 1, :] = jnp.where(even, last, first)
                outs[2][c, k : k + 1, :] = jnp.where(even, first, last)


def per_device(strips, slabs, adjoint, base_flow, conductance, ground_mask, turbine_cells, yaw_bin, yaw_table):
    _, nz, nx, ny = adjoint.shape
    chips = slabs // 2
    cube, field, plane = (nz, nx, ny), adjoint.shape, (3, nz, ny)
    pair_a = [(i, i ^ 1) for i in range(strips)]
    pair_b = [((i + 1) % strips, ((i ^ 1) + 1) % strips) for i in range(strips)]
    cores = [(i, i ^ 1) for i in range(slabs)]

    def across(parts):
        return [
            lax.ppermute(part, "gz", [(i, i ^ (2 * (j + 1))) for i in range(slabs)])
            for j, part in enumerate(parts)
        ]

    part = lambda n: (n, 8, ny)
    ratio, recip, bottom_w, top_w, keep, send = call(
        slab_kernel, [cube, cube, cube, cube, part(3), part(3)], (conductance,), 0.3
    )
    edge_a, edge_b = call(edge_kernel, [plane, plane], (adjoint,), 0.2, after=AFTER_EDGE(keep))
    recv = lax.ppermute(send, "gz", cores)
    own, mid = call(chip_coef_kernel, [part(3), part(3)], (keep, recv), 0.2)
    coefs = across([own] * (chips - 1))
    (source,) = call(
        source_kernel,
        [field],
        (turbine_cells, yaw_bin, yaw_table),
        3.5,
        [SMEM, SMEM, SMEM],
        after=AFTER_SOURCE(own),
    )
    state = adjoint
    for sweep_index in range(SWEEPS):
        halo_a = lax.ppermute(edge_a, "gx", pair_a)
        halo_b = lax.ppermute(edge_b, "gx", pair_b)
        first = sweep_index == 0
        extra = [(2, nz, ny), (2, 2, nz, ny)] if first else []
        solved, ends, *extra = call(
            right_kernel,
            [field, (6, nx, ny), *extra],
            (state, base_flow, source, ratio, recip, bottom_w, top_w),
            3.0,
        )
        if first:
            edge_w, end_w = extra
        keep, send = call(ends_kernel, [part(6), part(6)], (ends, halo_a, halo_b, end_w), 0.3)
        recv = lax.ppermute(send, "gz", cores)
        if first and not EARLY:
            volts, mine = call(chip_kernel, [part(9), part(6)], (keep, recv, mid), 0.2)
            others = across([mine] * (chips - 1))
        if first:
            below, above, own_coef = call(
                functools.partial(join_coef_kernel, chips),
                [(chips, 8, ny), (chips, 8, ny), part(4)],
                (own, *coefs, ground_mask),
                0.2,
                scratch=[pltpu.VMEM((chips, 3, 8, ny), F32)],
            )
        if not first or EARLY:
            volts, *parts = call(
                functools.partial(chip_again_kernel, chips),
                [part(9)] + [part(3)] * (chips - 1),
                (keep, recv, mid, own_coef),
                0.2,
            )
            others = across(parts)
        (solved,) = call(
            halo_kernel,
            [field],
            (solved, halo_a, halo_b, edge_w, ratio, recip),
            1.0,
            scratch=[pltpu.VMEM((3, 2, nz, ny), F32)],
        )
        scaled = not first or EARLY
        j_keep, j_send = call(
            functools.partial(join_kernel, chips, scaled),
            [part(6), part(6)],
            (*others, volts, mid, below, above, own_coef),
            0.2,
            scratch=[pltpu.VMEM((chips, 3 if scaled else 6, 8, ny), F32)],
        )
        j_recv = lax.ppermute(j_send, "gz", cores)
        last = sweep_index == SWEEPS - 1
        edges = [] if last else [plane] * 2
        state, *edges = call(
            update_kernel, [field, *edges], (solved, bottom_w, top_w, j_keep, j_recv), 0.5
        )
        if not last:
            edge_a, edge_b = edges
    return state


def solution(mesh):
    in_specs = (
        P(None, "gz", "gx", None),
        P(None, "gz", "gx", None),
        P("gz", "gx", None),
        P("gx", None),
        P(),
        P(),
        P(),
    )
    out_specs = P(None, "gz", "gx", None)
    body = functools.partial(per_device, mesh.shape["gx"], mesh.shape["gz"])
    return jax.shard_map(body, mesh=mesh, in_specs=in_specs, out_specs=out_specs, check_vma=False)
```

time: 61.6 us -> 52.5 us (0.85)
  waiting for transfers between devices: 26.5 us -> 20.4 us
  local copies, waits for them, and re-layouts: 7.26 us -> 2.47 us
  starting transfers between devices: 16.3 us -> 20.1 us
  Pallas kernels: 11.1 us -> 9.15 us
    ppermute x6 -> x9, starting transfers between devices: 8.9 us -> 13.3 us  [across(): lax.ppermute(part, 'gz', [(i, i ^ 2 * (j + 1)) for i in range(slabs)])]
    ppermute x6 -> x9, waiting for transfers between devices: 16.8 us -> 12.4 us  [across(): lax.ppermute(part, 'gz', [(i, i ^ 2 * (j + 1)) for i in range(slabs)])]
    unnamed x18 -> x16, local copies, waits for them, and re-layouts: 5.62 us -> 2.47 us
    pallas_call x9 -> x17, Pallas kernels: 11.1 us -> 9.15 us  [call(): pl.pallas_call(run, out_shape=[jax.ShapeDtypeStruct(s, F32) for s in outs...]
    dynamic_slice x1 -> x0, local copies, waits for them, and re-layouts: 1.64 us -> none  [per_device(): lax.dynamic_index_in_dim(adjoint, odd * (nx - 1), 2, keepdims=False)]
    ppermute x2, waiting for transfers between devices: 3.65 us -> 2.4 us  [per_device(): halo_a = lax.ppermute(edge_a, 'gx', pair_a)]
    ppermute x2 -> x3, waiting for transfers between devices: 1.29 us -> 2.52 us  [per_device(): recv = lax.ppermute(send, 'gz', cores)]
    ppermute x1 -> x0, waiting for transfers between devices: 0.88 us -> none  [per_device(): coef_recv = lax.ppermute(coef_send, 'gz', cores)]
  transfers between devices with their start and end apart: 15 -> 18, of which waited for: 11 -> 13; matrix products, arithmetic and copies ran while one was open for 0% -> 0% of each run, Pallas kernels for 5% -> 13%
where the time goes in v2:
time: 52.5 us; the launch traced here: 52.3 us
  waiting for transfers between devices  20.4 us (39%)
  starting transfers between devices  20.1 us (38%)
  Pallas kernels  9.15 us (17%)
  local copies, waits for them, and re-layouts  2.47 us (5%)
    ppermute x9, starting transfers between devices, across(): lax.ppermute(part, 'gz', [(i, i ^ 2 * (j + 1)) for i in range(slabs)])  13.3 us
    ppermute x9, waiting for transfers between devices, across(): lax.ppermute(part, 'gz', [(i, i ^ 2 * (j + 1)) for i in range(slabs)])  12.4 us
    pallas_call x17, Pallas kernels, call(): pl.pallas_call(run, out_shape=[jax.ShapeDtypeStruct(s, F32) for s in outs...  9.15 us
    ppermute x2, starting transfers between devices, per_device(): halo_a = lax.ppermute(edge_a, 'gx', pair_a)  4.5 us
    ppermute x3, waiting for transfers between devices, per_device(): recv = lax.ppermute(send, 'gz', cores)  2.52 us
    unnamed x16, local copies, waits for them, and re-layouts  2.47 us
    ppermute x2, waiting for transfers between devices, per_device(): halo_a = lax.ppermute(edge_a, 'gx', pair_a)  2.4 us
    ppermute x2, starting transfers between devices, per_device(): halo_b = lax.ppermute(edge_b, 'gx', pair_b)  1.81 us
  transfers between devices with their start and end apart: 18, of which 13 were waited for; matrix products, arithmetic and copies ran while one was open for 0% of the time, Pallas kernels for 13%

profile of v2, /device:TPU:0, one launch (start us, length us, event | category | flops | bytes accessed | tf_op | source)
XLA Modules:
  0.0 52.3 jit_solution(17350607414728217253)
XLA Ops:
  0.0 1.0 %copy-done.3 = f32[16,16,512]{2,1,0:T(8,128)S(1)} copy-done((f32[16,16,512]{2,1,0:T(8,128)S(1)}, f32[16,16,512]{2,1,0:T(8,128)}, u32[]{:S(2)}) %copy-start.3) | copy-done | bytes 524312
  1.3 1.4 %copy-done = f32[3,16,16,512]{3,2,1,0:T(8,128)S(1)} copy-done((f32[3,16,16,512]{3,2,1,0:T(8,128)S(1)}, f32[3,16,16,512]{3,2,1,0:T(8,128)}, u32[]{:S(2)}) %copy-start) | copy-done | bytes 1572888
  2.8 3.0 %collective-permute-start.1 = (f32[3,16,512]{2,1,0:T(8,128)S(1)}, f32[3,16,512]{2,1,0:T(8,128)S(1)}, u32[]{:S(2)}, u32[]{:S(2)}) collective-permute-start(f32[3,16,512]{2,1,0:T(8,128)S(1)} %get-tuple-element.51), channel_id=1, source_target_pairs={{0,8},{8,0},{16,24},{24,16},{1,9},{9,1},{17,25},{25,17},{2,10},{10... | collective-permute-start | bytes 294920 | tf_op jit(solution)/shard_map/ppermute | solution.py:400
  5.8 1.5 %collective-permute-start.2 = (f32[3,16,512]{2,1,0:T(8,128)S(1)}, f32[3,16,512]{2,1,0:T(8,128)S(1)}, u32[]{:S(2)}, u32[]{:S(2)}) collective-permute-start(f32[3,16,512]{2,1,0:T(8,128)S(1)} %get-tuple-element.52), channel_id=1, source_target_pairs={{8,16},{16,8},{24,0},{0,24},{9,17},{17,9},{25,1},{1,25},{10,18},{1... | collective-permute-start | bytes 294920 | tf_op jit(solution)/shard_map/ppermute | solution.py:401
  7.3 1.2 %collective-permute-done.refs_1_ = f32[3,8,512]{2,1,0:T(8,128)S(1)} collective-permute-done((f32[3,8,512]{2,1,0:T(8,128)S(1)}, f32[3,8,512]{2,1,0:T(8,128)S(1)}, u32[]{:S(2)}, u32[]{:S(2)}) %collective-permute-start) | collective-permute-done | bytes 49184 | tf_op jit(solution)/shard_map/ppermute | solution.py:387
  8.6 2.6 %shard_map.75.refs_2_ = f32[3,16,16,512]{3,2,1,0:T(8,128)S(1)} custom-call(s32[3,100]{1,0:T(4,128)S(1)} %copy-done.5, s32[100]{0:T(128)S(1)} %copy-done.7, f32[3,12]{1,0:T(4,128)S(1)} %copy-done.6, f32[3,8,512]{2,1,0:T(8,128)S(1)} %get-tuple-element.45.refs_3_.refs_0_), custom_call_target="tpu_custom_call" | custom-call | bytes 10500000 | tf_op jit(solution)/shard_map/pallas_call | solution.py:29
  11.2 1.6 %shard_map.76 = (f32[3,16,16,512]{3,2,1,0:T(8,128)S(1)}, f32[6,16,512]{2,1,0:T(8,128)S(1)}, f32[2,16,512]{2,1,0:T(8,128)S(1)}, f32[2,2,16,512]{3,2,1,0:T(8,128)S(1)}) custom-call(f32[3,16,16,512]{3,2,1,0:T(8,128)S(1)} %copy-done.1, f32[2,16,16,512]{3,2,1,0:T(8,128)S(1)} %copy-done.2, f32[3,16,16,512]{3,2,1,0:T(8,128)S(1)} %shard_map.75.refs_2_, ...), custom_call_target="tpu_custom_call" | custom-call | bytes 9000000 | tf_op jit(solution)/shard_map/pallas_call | solution.py:29
  13.2 3.6 %collective-permute-start.6 = (f32[3,8,512]{2,1,0:T(8,128)S(1)}, f32[3,8,512]{2,1,0:T(8,128)S(1)}, u32[]{:S(2)}, u32[]{:S(2)}) collective-permute-start(f32[3,8,512]{2,1,0:T(8,128)S(1)} %get-tuple-element.45.refs_3_.refs_0_), channel_id=1, source_target_pairs={{0,6},{1,7},{2,4},{3,5},{4,2},{5,3},{6,0},{7,1},{8,14},{9,15},{10,... | collective-permute-start | bytes 147464 | tf_op jit(solution)/shard_map/ppermute | solution.py:378
  17.6 1.6 %collective-permute-done.6.refs_3_ = f32[3,8,512]{2,1,0:T(8,128)S(1)} collective-permute-done((f32[3,8,512]{2,1,0:T(8,128)S(1)}, f32[3,8,512]{2,1,0:T(8,128)S(1)}, u32[]{:S(2)}, u32[]{:S(2)}) %collective-permute-start.6) | collective-permute-done | bytes 49184 | tf_op jit(solution)/shard_map/ppermute | solution.py:378
  19.2 2.7 %collective-permute-done.5.refs_2_ = f32[3,8,512]{2,1,0:T(8,128)S(1)} collective-permute-done((f32[3,8,512]{2,1,0:T(8,128)S(1)}, f32[3,8,512]{2,1,0:T(8,128)S(1)}, u32[]{:S(2)}, u32[]{:S(2)}) %collective-permute-start.5) | collective-permute-done | bytes 49184 | tf_op jit(solution)/shard_map/ppermute | solution.py:378
  23.1 1.8 %collective-permute-start.8 = (f32[3,8,512]{2,1,0:T(8,128)S(1)}, f32[3,8,512]{2,1,0:T(8,128)S(1)}, u32[]{:S(2)}, u32[]{:S(2)}) collective-permute-start(f32[3,8,512]{2,1,0:T(8,128)S(1)} %get-tuple-element.61), channel_id=1, source_target_pairs={{0,4},{1,5},{2,6},{3,7},{4,0},{5,1},{6,2},{7,3},{8,12},{9,13},{10,... | collective-permute-start | bytes 147464 | tf_op jit(solution)/shard_map/ppermute | solution.py:378
  24.9 1.6 %collective-permute-start.9 = (f32[3,8,512]{2,1,0:T(8,128)S(1)}, f32[3,8,512]{2,1,0:T(8,128)S(1)}, u32[]{:S(2)}, u32[]{:S(2)}) collective-permute-start(f32[3,8,512]{2,1,0:T(8,128)S(1)} %get-tuple-element.62), channel_id=1, source_target_pairs={{0,6},{1,7},{2,4},{3,5},{4,2},{5,3},{6,0},{7,1},{8,14},{9,15},{10,... | collective-permute-start | bytes 147464 | tf_op jit(solution)/shard_map/ppermute | solution.py:378
  26.5 1.5 %collective-permute-done.8.refs_1_ = f32[3,8,512]{2,1,0:T(8,128)S(1)} collective-permute-done((f32[3,8,512]{2,1,0:T(8,128)S(1)}, f32[3,8,512]{2,1,0:T(8,128)S(1)}, u32[]{:S(2)}, u32[]{:S(2)}) %collective-permute-start.8) | collective-permute-done | bytes 49184 | tf_op jit(solution)/shard_map/ppermute | solution.py:378
  28.0 2.7 %collective-permute-done.9.refs_2_ = f32[3,8,512]{2,1,0:T(8,128)S(1)} collective-permute-done((f32[3,8,512]{2,1,0:T(8,128)S(1)}, f32[3,8,512]{2,1,0:T(8,128)S(1)}, u32[]{:S(2)}, u32[]{:S(2)}) %collective-permute-start.9) | collective-permute-done | bytes 49184 | tf_op jit(solution)/shard_map/ppermute | solution.py:378
  32.7 1.5 %collective-permute-start.11 = (f32[3,16,512]{2,1,0:T(8,128)S(1)}, f32[3,16,512]{2,1,0:T(8,128)S(1)}, u32[]{:S(2)}, u32[]{:S(2)}) collective-permute-start(f32[3,16,512]{2,1,0:T(8,128)S(1)} %get-tuple-element.70), channel_id=1, source_target_pairs={{0,8},{8,0},{16,24},{24,16},{1,9},{9,1},{17,25},{25,17},{2,10},{10... | collective-permute-start | bytes 294920 | tf_op jit(solution)/shard_map/ppermute | solution.py:400
  34.5 1.5 %shard_map.84 = (f32[3,16,16,512]{3,2,1,0:T(8,128)S(1)}, f32[6,16,512]{2,1,0:T(8,128)S(1)}) custom-call(f32[3,16,16,512]{3,2,1,0:T(8,128)S(1)} %get-tuple-element.68.refs_0_, f32[2,16,16,512]{3,2,1,0:T(8,128)S(1)} %copy-done.2, f32[3,16,16,512]{3,2,1,0:T(8,128)S(1)} %shard_map.75.refs_2_, f32[16,16,512]{2,1,0:T(8,128)S(1)} %get-tuple-element.46.refs_3_.refs_4_, ...), custom_call_target="tpu_custom_call" | custom-call | bytes 9000000 | tf_op jit(solution)/shard_map/pallas_call | solution.py:29
  36.0 2.4 %collective-permute-done.11.refs_1_ = f32[3,16,512]{2,1,0:T(8,128)S(1)} collective-permute-done((f32[3,16,512]{2,1,0:T(8,128)S(1)}, f32[3,16,512]{2,1,0:T(8,128)S(1)}, u32[]{:S(2)}, u32[]{:S(2)}) %collective-permute-start.11) | collective-permute-done | bytes 98336 | tf_op jit(solution)/shard_map/ppermute | solution.py:400
  38.4 1.3 %collective-permute-done.12.refs_2_ = f32[3,16,512]{2,1,0:T(8,128)S(1)} collective-permute-done((f32[3,16,512]{2,1,0:T(8,128)S(1)}, f32[3,16,512]{2,1,0:T(8,128)S(1)}, u32[]{:S(2)}, u32[]{:S(2)}) %collective-permute-start.12) | collective-permute-done | bytes 98336 | tf_op jit(solution)/shard_map/ppermute | solution.py:401
  39.9 1.3 %collective-permute-done.13.refs_1_ = f32[6,8,512]{2,1,0:T(8,128)S(1)} collective-permute-done((f32[6,8,512]{2,1,0:T(8,128)S(1)}, f32[6,8,512]{2,1,0:T(8,128)S(1)}, u32[]{:S(2)}, u32[]{:S(2)}) %collective-permute-start.13) | collective-permute-done | bytes 98336 | tf_op jit(solution)/shard_map/ppermute | solution.py:413
  41.3 2.3 %collective-permute-start.15 = (f32[3,8,512]{2,1,0:T(8,128)S(1)}, f32[3,8,512]{2,1,0:T(8,128)S(1)}, u32[]{:S(2)}, u32[]{:S(2)}) collective-permute-start(f32[3,8,512]{2,1,0:T(8,128)S(1)} %get-tuple-element.76), channel_id=1, source_target_pairs={{0,4},{1,5},{2,6},{3,7},{4,0},{5,1},{6,2},{7,3},{8,12},{9,13},{10,... | collective-permute-start | bytes 147464 | tf_op jit(solution)/shard_map/ppermute | solution.py:378
  43.6 2.0 %collective-permute-start.16 = (f32[3,8,512]{2,1,0:T(8,128)S(1)}, f32[3,8,512]{2,1,0:T(8,128)S(1)}, u32[]{:S(2)}, u32[]{:S(2)}) collective-permute-start(f32[3,8,512]{2,1,0:T(8,128)S(1)} %get-tuple-element.77), channel_id=1, source_target_pairs={{0,6},{1,7},{2,4},{3,5},{4,2},{5,3},{6,0},{7,1},{8,14},{9,15},{10,... | collective-permute-start | bytes 147464 | tf_op jit(solution)/shard_map/ppermute | solution.py:378
  45.9 2.5 %collective-permute-done.15.refs_1_ = f32[3,8,512]{2,1,0:T(8,128)S(1)} collective-permute-done((f32[3,8,512]{2,1,0:T(8,128)S(1)}, f32[3,8,512]{2,1,0:T(8,128)S(1)}, u32[]{:S(2)}, u32[]{:S(2)}) %collective-permute-start.15) | collective-permute-done | bytes 49184 | tf_op jit(solution)/shard_map/ppermute | solution.py:378
  48.4 1.1 %collective-permute-done.16.refs_2_ = f32[3,8,512]{2,1,0:T(8,128)S(1)} collective-permute-done((f32[3,8,512]{2,1,0:T(8,128)S(1)}, f32[3,8,512]{2,1,0:T(8,128)S(1)}, u32[]{:S(2)}, u32[]{:S(2)}) %collective-permute-start.16) | collective-permute-done | bytes 49184 | tf_op jit(solution)/shard_map/ppermute | solution.py:378
  51.0 1.4 %shard_map.89 = f32[3,16,16,512]{3,2,1,0:T(8,128)} custom-call(f32[3,16,16,512]{3,2,1,0:T(8,128)S(1)} %shard_map.85.refs_0_, f32[16,16,512]{2,1,0:T(8,128)S(1)} %get-tuple-element.48.refs_5_.refs_1_, f32[16,16,512]{2,1,0:T(8,128)S(1)} %get-tuple-element.49.refs_6_.refs_2_, f32[6,8,512]{2,1,0:T(8,128)S(1)} %get-tuple-element.79.refs_3_, ...), custom_call_target="tpu_custom_call" | custom-call | bytes 1500000 | tf_op jit(solution)/shard_map/pallas_call | solution.py:29
  (45 shorter events, 6.9 us)
Async XLA Ops:
  1.0 7.5 %copy-start.5 = (s32[3,100]{1,0:T(4,128)S(1)}, s32[3,100]{1,0:T(4,128)}, u32[]{:S(2)}) copy-start(s32[3,100]{1,0:T(4,128)} %refs_0_.5) | copy-start | bytes 3604
  1.0 7.5 %copy-start.6 = (f32[3,12]{1,0:T(4,128)S(1)}, f32[3,12]{1,0:T(4,128)}, u32[]{:S(2)}) copy-start(f32[3,12]{1,0:T(4,128)} %refs_2_.1) | copy-start | bytes 436
  1.0 7.5 %copy-start.7 = (s32[100]{0:T(128)S(1)}, s32[100]{0:T(128)}, u32[]{:S(2)}) copy-start(s32[100]{0:T(128)} %refs_1_.3) | copy-start | bytes 1204
  2.7 8.4 %copy-start.1 = (f32[3,16,16,512]{3,2,1,0:T(8,128)S(1)}, f32[3,16,16,512]{3,2,1,0:T(8,128)}, u32[]{:S(2)}) copy-start(f32[3,16,16,512]{3,2,1,0:T(8,128)} %refs_0_.7) | copy-start | bytes 4718596
  2.7 8.5 %copy-start.2 = (f32[2,16,16,512]{3,2,1,0:T(8,128)S(1)}, f32[2,16,16,512]{3,2,1,0:T(8,128)}, u32[]{:S(2)}) copy-start(f32[2,16,16,512]{3,2,1,0:T(8,128)} %refs_1_.5) | copy-start | bytes 3145732
  2.8 10.0 %collective-permute-start.1 = (f32[3,16,512]{2,1,0:T(8,128)S(1)}, f32[3,16,512]{2,1,0:T(8,128)S(1)}, u32[]{:S(2)}, u32[]{:S(2)}) collective-permute-start(f32[3,16,512]{2,1,0:T(8,128)S(1)} %get-tuple-element.51), channel_id=1, source_target_pairs={{0,8},{8,0},{16,24},{24,16},{1,9},{9,1},{17,25},{25,17},{2,10},{10... | collective-permute-start | bytes 294920 | tf_op jit(solution)/shard_map/ppermute | solution.py:400
  5.8 7.0 %collective-permute-start.2 = (f32[3,16,512]{2,1,0:T(8,128)S(1)}, f32[3,16,512]{2,1,0:T(8,128)S(1)}, u32[]{:S(2)}, u32[]{:S(2)}) collective-permute-start(f32[3,16,512]{2,1,0:T(8,128)S(1)} %get-tuple-element.52), channel_id=1, source_target_pairs={{8,16},{16,8},{24,0},{0,24},{9,17},{17,9},{25,1},{1,25},{10,18},{1... | collective-permute-start | bytes 294920 | tf_op jit(solution)/shard_map/ppermute | solution.py:401
  7.3 1.2 %collective-permute-start = (f32[3,8,512]{2,1,0:T(8,128)S(1)}, f32[3,8,512]{2,1,0:T(8,128)S(1)}, u32[]{:S(2)}, u32[]{:S(2)}) collective-permute-start(f32[3,8,512]{2,1,0:T(8,128)S(1)} %get-tuple-element.44), channel_id=1, source_target_pairs={{0,1},{1,0},{2,3},{3,2},{4,5},{5,4},{6,7},{7,6},{8,9},{9,8},{10,11... | collective-permute-start | bytes 147464 | tf_op jit(solution)/shard_map/ppermute | solution.py:387
  11.2 10.7 %copy-start.4 = (s32[16,512]{1,0:T(8,128)S(1)}, s32[16,512]{1,0:T(8,128)}, u32[]{:S(2)}) copy-start(s32[16,512]{1,0:T(8,128)} %refs_4_.1) | copy-start | bytes 98308
  12.9 9.1 %collective-permute-start.3 = (f32[6,8,512]{2,1,0:T(8,128)S(1)}, f32[6,8,512]{2,1,0:T(8,128)S(1)}, u32[]{:S(2)}, u32[]{:S(2)}) collective-permute-start(f32[6,8,512]{2,1,0:T(8,128)S(1)} %get-tuple-element.57), channel_id=1, source_target_pairs={{0,1},{1,0},{2,3},{3,2},{4,5},{5,4},{6,7},{7,6},{8,9},{9,8},{10,11... | collective-permute-start | bytes 294920 | tf_op jit(solution)/shard_map/ppermute | solution.py:413
  13.2 5.9 %collective-permute-start.6 = (f32[3,8,512]{2,1,0:T(8,128)S(1)}, f32[3,8,512]{2,1,0:T(8,128)S(1)}, u32[]{:S(2)}, u32[]{:S(2)}) collective-permute-start(f32[3,8,512]{2,1,0:T(8,128)S(1)} %get-tuple-element.45.refs_3_.refs_0_), channel_id=1, source_target_pairs={{0,6},{1,7},{2,4},{3,5},{4,2},{5,3},{6,0},{7,1},{8,14},{9,15},{10,... | collective-permute-start | bytes 147464 | tf_op jit(solution)/shard_map/ppermute | solution.py:378
  16.8 5.1 %collective-permute-start.5 = (f32[3,8,512]{2,1,0:T(8,128)S(1)}, f32[3,8,512]{2,1,0:T(8,128)S(1)}, u32[]{:S(2)}, u32[]{:S(2)}) collective-permute-start(f32[3,8,512]{2,1,0:T(8,128)S(1)} %get-tuple-element.45.refs_3_.refs_0_), channel_id=1, source_target_pairs={{0,4},{1,5},{2,6},{3,7},{4,0},{5,1},{6,2},{7,3},{8,12},{9,13},{10,... | collective-permute-start | bytes 147464 | tf_op jit(solution)/shard_map/ppermute | solution.py:378
  16.8 5.1 %collective-permute-start.4 = (f32[3,8,512]{2,1,0:T(8,128)S(1)}, f32[3,8,512]{2,1,0:T(8,128)S(1)}, u32[]{:S(2)}, u32[]{:S(2)}) collective-permute-start(f32[3,8,512]{2,1,0:T(8,128)S(1)} %get-tuple-element.45.refs_3_.refs_0_), channel_id=1, source_target_pairs={{0,2},{1,3},{2,0},{3,1},{4,6},{5,7},{6,4},{7,5},{8,10},{9,11},{10,... | collective-permute-start | bytes 147464 | tf_op jit(solution)/shard_map/ppermute | solution.py:378
  22.1 4.5 %collective-permute-start.7 = (f32[3,8,512]{2,1,0:T(8,128)S(1)}, f32[3,8,512]{2,1,0:T(8,128)S(1)}, u32[]{:S(2)}, u32[]{:S(2)}) collective-permute-start(f32[3,8,512]{2,1,0:T(8,128)S(1)} %get-tuple-element.60), channel_id=1, source_target_pairs={{0,2},{1,3},{2,0},{3,1},{4,6},{5,7},{6,4},{7,5},{8,10},{9,11},{10,... | collective-permute-start | bytes 147464 | tf_op jit(solution)/shard_map/ppermute | solution.py:378
  23.1 5.0 %collective-permute-start.8 = (f32[3,8,512]{2,1,0:T(8,128)S(1)}, f32[3,8,512]{2,1,0:T(8,128)S(1)}, u32[]{:S(2)}, u32[]{:S(2)}) collective-permute-start(f32[3,8,512]{2,1,0:T(8,128)S(1)} %get-tuple-element.61), channel_id=1, source_target_pairs={{0,4},{1,5},{2,6},{3,7},{4,0},{5,1},{6,2},{7,3},{8,12},{9,13},{10,... | collective-permute-start | bytes 147464 | tf_op jit(solution)/shard_map/ppermute | solution.py:378
  24.9 5.9 %collective-permute-start.9 = (f32[3,8,512]{2,1,0:T(8,128)S(1)}, f32[3,8,512]{2,1,0:T(8,128)S(1)}, u32[]{:S(2)}, u32[]{:S(2)}) collective-permute-start(f32[3,8,512]{2,1,0:T(8,128)S(1)} %get-tuple-element.62), channel_id=1, source_target_pairs={{0,6},{1,7},{2,4},{3,5},{4,2},{5,3},{6,0},{7,1},{8,14},{9,15},{10,... | collective-permute-start | bytes 147464 | tf_op jit(solution)/shard_map/ppermute | solution.py:378
  30.9 1.4 %collective-permute-start.10 = (f32[6,8,512]{2,1,0:T(8,128)S(1)}, f32[6,8,512]{2,1,0:T(8,128)S(1)}, u32[]{:S(2)}, u32[]{:S(2)}) collective-permute-start(f32[6,8,512]{2,1,0:T(8,128)S(1)} %get-tuple-element.67), channel_id=1, source_target_pairs={{0,1},{1,0},{2,3},{3,2},{4,5},{5,4},{6,7},{7,6},{8,9},{9,8},{10,11... | collective-permute-start | bytes 294920 | tf_op jit(solution)/shard_map/ppermute | solution.py:448
  32.7 5.7 %collective-permute-start.11 = (f32[3,16,512]{2,1,0:T(8,128)S(1)}, f32[3,16,512]{2,1,0:T(8,128)S(1)}, u32[]{:S(2)}, u32[]{:S(2)}) collective-permute-start(f32[3,16,512]{2,1,0:T(8,128)S(1)} %get-tuple-element.70), channel_id=1, source_target_pairs={{0,8},{8,0},{16,24},{24,16},{1,9},{9,1},{17,25},{25,17},{2,10},{10... | collective-permute-start | bytes 294920 | tf_op jit(solution)/shard_map/ppermute | solution.py:400
  34.2 5.5 %collective-permute-start.12 = (f32[3,16,512]{2,1,0:T(8,128)S(1)}, f32[3,16,512]{2,1,0:T(8,128)S(1)}, u32[]{:S(2)}, u32[]{:S(2)}) collective-permute-start(f32[3,16,512]{2,1,0:T(8,128)S(1)} %get-tuple-element.71), channel_id=1, source_target_pairs={{8,16},{16,8},{24,0},{0,24},{9,17},{17,9},{25,1},{1,25},{10,18},{1... | collective-permute-start | bytes 294920 | tf_op jit(solution)/shard_map/ppermute | solution.py:401
  39.8 1.4 %collective-permute-start.13 = (f32[6,8,512]{2,1,0:T(8,128)S(1)}, f32[6,8,512]{2,1,0:T(8,128)S(1)}, u32[]{:S(2)}, u32[]{:S(2)}) collective-permute-start(f32[6,8,512]{2,1,0:T(8,128)S(1)} %get-tuple-element.74), channel_id=1, source_target_pairs={{0,1},{1,0},{2,3},{3,2},{4,5},{5,4},{6,7},{7,6},{8,9},{9,8},{10,11... | collective-permute-start | bytes 294920 | tf_op jit(solution)/shard_map/ppermute | solution.py:413
  41.2 4.8 %collective-permute-start.14 = (f32[3,8,512]{2,1,0:T(8,128)S(1)}, f32[3,8,512]{2,1,0:T(8,128)S(1)}, u32[]{:S(2)}, u32[]{:S(2)}) collective-permute-start(f32[3,8,512]{2,1,0:T(8,128)S(1)} %get-tuple-element.75), channel_id=1, source_target_pairs={{0,2},{1,3},{2,0},{3,1},{4,6},{5,7},{6,4},{7,5},{8,10},{9,11},{10,... | collective-permute-start | bytes 147464 | tf_op jit(solution)/shard_map/ppermute | solution.py:378
  41.3 7.2 %collective-permute-start.15 = (f32[3,8,512]{2,1,0:T(8,128)S(1)}, f32[3,8,512]{2,1,0:T(8,128)S(1)}, u32[]{:S(2)}, u32[]{:S(2)}) collective-permute-start(f32[3,8,512]{2,1,0:T(8,128)S(1)} %get-tuple-element.76), channel_id=1, source_target_pairs={{0,4},{1,5},{2,6},{3,7},{4,0},{5,1},{6,2},{7,3},{8,12},{9,13},{10,... | collective-permute-start | bytes 147464 | tf_op jit(solution)/shard_map/ppermute | solution.py:378
  43.6 5.9 %collective-permute-start.16 = (f32[3,8,512]{2,1,0:T(8,128)S(1)}, f32[3,8,512]{2,1,0:T(8,128)S(1)}, u32[]{:S(2)}, u32[]{:S(2)}) collective-permute-start(f32[3,8,512]{2,1,0:T(8,128)S(1)} %get-tuple-element.77), channel_id=1, source_target_pairs={{0,6},{1,7},{2,4},{3,5},{4,2},{5,3},{6,0},{7,1},{8,14},{9,15},{10,... | collective-permute-start | bytes 147464 | tf_op jit(solution)/shard_map/ppermute | solution.py:378
  49.6 1.4 %collective-permute-start.17 = (f32[6,8,512]{2,1,0:T(8,128)S(1)}, f32[6,8,512]{2,1,0:T(8,128)S(1)}, u32[]{:S(2)}, u32[]{:S(2)}) collective-permute-start(f32[6,8,512]{2,1,0:T(8,128)S(1)} %get-tuple-element.80), channel_id=1, source_target_pairs={{0,1},{1,0},{2,3},{3,2},{4,5},{5,4},{6,7},{7,6},{8,9},{9,8},{10,11... | collective-permute-start | bytes 294920 | tf_op jit(solution)/shard_map/ppermute | solution.py:448
  (2 other events, 2.5 us)

commit v3 on v2

v3 whole, which is shorter than its diff:
```python
import functools

import jax
import jax.numpy as jnp
from jax import lax
from jax.experimental import pallas as pl
from jax.experimental.pallas import tpu as pltpu
from jax.sharding import PartitionSpec as P

SWEEPS = 2
PSEUDO_STEP = 0.2
LATERAL_VISC = 1.0


F32 = jnp.float32
VMEM = pl.BlockSpec(memory_space=pltpu.VMEM)
SMEM = pl.BlockSpec(memory_space=pltpu.SMEM)
ANY = pl.BlockSpec(memory_space=pl.ANY)
PARAMS = pltpu.CompilerParams(vmem_limit_bytes=12 * 1024 * 1024)


def call(body, outs, ins, cost_us, specs=None, scratch=(), after=()):
    def run(*refs):
        body(*refs[: len(ins)], *refs[len(ins) + len(after) :])

    return pl.pallas_call(
        run,
        out_shape=[jax.ShapeDtypeStruct(s, F32) for s in outs],
        in_specs=(specs or [VMEM] * len(ins)) + [ANY] * len(after),
        out_specs=[VMEM] * len(outs),
        scratch_shapes=list(scratch),
        compiler_params=PARAMS,
        cost_estimate=pl.CostEstimate(
            flops=0, bytes_accessed=int(cost_us * 3.0e6), transcendentals=0
        ),
    )(*ins, *after)


def chip_and_core():
    index = lax.axis_index("gz")
    return lax.div(index, 2), lax.rem(index, 2)


def share_kernel(whole_ref, keep_ref, send_ref, *inner_refs):
    parts, nz, nx, _ = whole_ref.shape
    half = nx // 2
    _, core = chip_and_core()
    mine = pl.ds(pl.multiple_of(core * half, half), half)
    other = pl.ds(pl.multiple_of((1 - core) * half, half), half)
    for c in range(parts):
        for k in range(nz):
            keep_ref[c, k] = whole_ref[c, k, mine, :]
            send_ref[c, k] = whole_ref[c, k, other, :]
            if inner_refs:
                before = whole_ref[c, k, half - 1 : half, :]
                behind = whole_ref[c, k, half : half + 1, :]
                at = nz + k // half, slice(k % half, k % half + 1)
                inner_refs[0][c, k : k + 1, :] = jnp.where(core == 0, behind, before)
                send_ref[c, at[0], at[1], :] = jnp.where(core == 0, before, behind)


def store_edges(core, c, k, first, last, outer_ref, inner_ref):
    outer_ref[c, k : k + 1, :] = jnp.where(core == 0, first, last)
    inner_ref[c, k : k + 1, :] = jnp.where(core == 0, last, first)


def gather_kernel(keep_ref, recv_ref, out_ref):
    parts, nz, _, _ = keep_ref.shape
    _, core = chip_and_core()
    for c in range(parts):
        for k in range(nz):
            out_ref[c, core * nz + k] = keep_ref[c, k]
            out_ref[c, (1 - core) * nz + k] = recv_ref[c, k]


def gather_state_kernel(keep_ref, recv_ref, row_ref, out_ref, outer_ref, inner_ref):
    parts, nz, nx, _ = keep_ref.shape
    gather_kernel(keep_ref, recv_ref, out_ref)
    _, core = chip_and_core()
    for c in range(parts):
        inner_ref[c, pl.ds(pl.multiple_of(core * nz, nz), nz), :] = row_ref[c]
        for i in range(nz // nx):
            at = pl.ds(pl.multiple_of((1 - core) * nz + i * nx, nx), nx)
            inner_ref[c, at, :] = recv_ref[c, nz + i]
        for k in range(2 * nz):
            first, last = out_ref[c, k, 0:1, :], out_ref[c, k, nx - 1 : nx, :]
            outer_ref[c, k : k + 1, :] = jnp.where(core == 0, first, last)


def source_kernel(cells_ref, bin_ref, table_ref, source_ref):
    parts, nz, nx, ny = source_ref.shape
    count = cells_ref.shape[1]
    chip, core = chip_and_core()
    lz = cells_ref[0:1, :] - chip * nz
    lx = cells_ref[1:2, :] - (lax.axis_index("gx") * 2 + core) * nx
    inside = (lz >= 0) & (lz < nz) & (lx >= 0) & (lx < nx)
    row = jnp.where(inside, lz * nx + lx, -1)
    at_row = lax.broadcasted_iota(jnp.int32, (nz * nx, count), 0) == row
    at_lane = lax.broadcasted_iota(jnp.int32, (ny, count), 0) == cells_ref[2:3, :]
    at_lane = jnp.where(at_lane, 1.0, 0.0)
    bins = [bin_ref[...] == b for b in range(table_ref.shape[1])]
    for c in range(parts):
        strength = jnp.zeros((1, count), F32)
        for b, here in enumerate(bins):
            strength = jnp.where(here, table_ref[c : c + 1, b : b + 1], strength)
        placed = lax.dot_general(
            jnp.where(at_row, strength, 0.0),
            at_lane,
            (((1,), (1,)), ((), ())),
            precision=lax.Precision.HIGHEST,
            preferred_element_type=F32,
        )
        source_ref[c] = placed.reshape(nz, nx, ny)


def slab_kernel(keep_ref, recv_ref, ratio_ref, recip_ref, bottom_ref, top_ref, own_ref, w_ref, cond_ref):
    nz, nx, ny = cond_ref.shape
    half = nz // 2
    _, core = chip_and_core()
    for k in range(half):
        cond_ref[core * half + k] = keep_ref[0, k]
        cond_ref[(1 - core) * half + k] = recv_ref[0, k]
    sigma = jnp.ones((nx, ny), F32)
    tau = jnp.ones((nx, ny), F32)
    for k in range(nz - 1):
        face = cond_ref[k + 1]
        recip = 1.0 / (sigma + face)
        ratio = face * recip
        recip_ref[k] = recip
        ratio_ref[k + 1] = ratio
        sigma = 1.0 + sigma * ratio
        face = cond_ref[nz - 1 - k]
        ratio = face / (tau + face)
        bottom_ref[nz - 1 - k] = ratio
        tau = 1.0 + tau * ratio
    weight = 1.0 / sigma
    recip_ref[nz - 1] = weight
    ratio_ref[0] = jnp.zeros((nx, ny), F32)
    own_ref[2] = weight
    top_ref[nz - 1] = weight
    for k in range(nz - 2, -1, -1):
        weight = weight * ratio_ref[k + 1]
        top_ref[k] = weight
    own_ref[1] = weight
    weight = 1.0 / tau
    own_ref[0] = weight + 1.0 / cond_ref[0]
    bottom_ref[0] = weight
    for k in range(1, nz):
        weight = weight * bottom_ref[k]
        bottom_ref[k] = weight
    for k in range(half):
        w_ref[0, k] = bottom_ref[(1 - core) * half + k]
        w_ref[1, k] = top_ref[(1 - core) * half + k]


def right_kernel(
    state_ref, flow_ref, source_ref, ratio_ref, recip_ref, bottom_ref, top_ref,
    solved_ref, ends_ref, *edge_refs,
):
    _, nz, nx, ny = state_ref.shape
    lanes = lax.broadcasted_iota(jnp.int32, (nx, ny), 1)
    rows = lax.broadcasted_iota(jnp.int32, (nx, ny), 0)
    visc = PSEUDO_STEP * LATERAL_VISC
    values = [None] * 3
    for k in range(nz):
        u = 0.5 * PSEUDO_STEP * flow_ref[0, k]
        v = 0.5 * PSEUDO_STEP * flow_ref[1, k]
        x_plus_w = visc + u
        x_minus_w = visc - u
        if edge_refs:
            edge_w, end_w = edge_refs
            for side, weight in ((0, x_minus_w[0:1]), (1, x_plus_w[nx - 1 : nx])):
                row = pl.ds(side * (nx - 1), 1)
                edge_w[side, k : k + 1, :] = weight
                end_w[side, 0, k : k + 1, :] = weight * bottom_ref[k, row, :]
                end_w[side, 1, k : k + 1, :] = weight * top_ref[k, row, :]
        x_plus_w = jnp.where(rows == nx - 1, 0.0, x_plus_w)
        x_minus_w = jnp.where(rows == 0, 0.0, x_minus_w)
        y_plus_w = jnp.where(lanes == ny - 1, 0.0, visc + v)
        y_minus_w = jnp.where(lanes == 0, 0.0, visc - v)
        ratio = ratio_ref[k]
        for c in range(3):
            a = state_ref[c, k]
            value = (
                (1.0 - 4.0 * visc) * a
                + x_plus_w * pltpu.roll(a, nx - 1, 0)
                + x_minus_w * pltpu.roll(a, 1, 0)
                + y_plus_w * pltpu.roll(a, ny - 1, 1)
                + y_minus_w * pltpu.roll(a, 1, 1)
                + source_ref[c, k]
            )
            if k:
                value = value + ratio * values[c]
            values[c] = value
            solved_ref[c, k] = value
    for k in range(nz - 1, -1, -1):
        recip = recip_ref[k]
        for c in range(3):
            value = solved_ref[c, k] * recip
            if k < nz - 1:
                value = value + ratio_ref[k + 1] * values[c]
            else:
                ends_ref[3 + c] = value
            values[c] = value
            solved_ref[c, k] = value
    for c in range(3):
        ends_ref[c] = values[c]


def halo_sides(outer_ref, inner_ref, c):
    _, core = chip_and_core()
    strip = lax.axis_index("gx")
    wall = jnp.where(core == 0, strip == 0, strip == lax.axis_size("gx") - 1)
    outer = outer_ref[c] * jnp.where(wall, 0.0, 1.0)
    inner = inner_ref[c]
    return jnp.where(core == 0, outer, inner), jnp.where(core == 0, inner, outer)


def ends_kernel(chips, ends_ref, outer_ref, inner_ref, end_w, own_coef, volt_ref, *parts):
    chip, _ = chip_and_core()
    nx = ends_ref.shape[1]
    rows = lax.broadcasted_iota(jnp.int32, ends_ref.shape[1:], 0)
    up, down = own_coef[0], own_coef[1]
    for c in range(3):
        left, right = halo_sides(outer_ref, inner_ref, c)
        both = []
        for e in range(2):
            low = jnp.sum(left * end_w[0, e], 0, keepdims=True)
            high = jnp.sum(right * end_w[1, e], 0, keepdims=True)
            value = ends_ref[3 * e + c] + jnp.where(rows == 0, low, 0.0)
            value = value + jnp.where(rows == nx - 1, high, 0.0)
            volt_ref[3 * e + c] = value
            both.append(value)
        first, last = both
        to_above = last - up * first
        to_below = first - down * last
        for j in range(1, chips):
            parts[j - 1][c] = jnp.where((chip ^ j) > chip, to_above, to_below)


def halo_kernel(solved_ref, outer_ref, inner_ref, edge_w, ratio_ref, recip_ref, out_ref, *refs):
    _, nz, nx, ny = solved_ref.shape
    right_ref = refs[-1]
    rows = lax.broadcasted_iota(jnp.int32, (nx, ny), 0)
    for c in range(3):
        for side, halo in enumerate(halo_sides(outer_ref, inner_ref, c)):
            right_ref[c, side] = halo * edge_w[side]
    values = [None] * 3
    for k in range(nz):
        ratio = ratio_ref[k]
        for c in range(3):
            value = jnp.where(rows == 0, right_ref[c, 0, k : k + 1, :], 0.0)
            value = jnp.where(rows == nx - 1, right_ref[c, 1, k : k + 1, :], value)
            if k:
                value = value + ratio * values[c]
            values[c] = value
            out_ref[c, k] = value
    for k in range(nz - 1, -1, -1):
        recip = recip_ref[k]
        for c in range(3):
            value = out_ref[c, k] * recip
            if k < nz - 1:
                value = value + ratio_ref[k + 1] * values[c]
            values[c] = value
            out_ref[c, k] = value + solved_ref[c, k]
    if len(refs) > 1:
        half = nz // 2
        _, core = chip_and_core()
        for c in range(3):
            for k in range(half):
                refs[0][c, k] = out_ref[c, (1 - core) * half + k]


def join_coef_kernel(chips, *refs):
    own_ref, others, mask_ref = refs[0], refs[1:chips], refs[chips]
    below_ref, above_ref, own_out, all_ref = refs[chips + 1 :]
    chip, core = chip_and_core()
    nx = own_ref.shape[1]
    all_ref[chip] = own_ref[...]
    for j in range(1, chips):
        all_ref[chip ^ j] = others[j - 1][...]
    mask = mask_ref[pl.ds(pl.multiple_of(core * nx, nx), nx), :].astype(F32)
    zero = jnp.zeros(mask.shape, F32)

    low = zero
    for t in range(chips - 1):
        cross = all_ref[t, 1]
        kappa = cross / (all_ref[t, 0] + low)
        if t == 0:
            kappa = kappa * mask
        below_ref[t] = kappa
        low = jnp.where(t < chip, all_ref[t, 2] - kappa * cross, low)
    below_ref[chips - 1] = zero

    high = zero
    above_ref[chips - 1] = zero
    above_ref[0] = zero
    for t in range(chips - 1, 0, -1):
        cross = all_ref[t, 1]
        kappa = zero if t == chips - 1 else cross / (all_ref[t, 2] + high)
        above_ref[t] = kappa
        high = jnp.where(t > chip, all_ref[t, 0] - kappa * cross, high)

    near, cross, far = own_ref[0], own_ref[1], own_ref[2]
    bottom_on = jnp.where(chip == 0, mask, 1.0)
    top_on = jnp.where(chip == chips - 1, 0.0, 1.0)
    up = cross * bottom_on / (near + low)
    down = cross * top_on / (far + high)
    own_out[0] = up
    own_out[1] = down
    own_out[2] = bottom_on / (low + near - down * cross)
    own_out[3] = top_on / (high + far - up * cross)


def join_kernel(chips, whole, *refs):
    others = refs[: chips - 1]
    volt_ref, below_ref, above_ref, own_coef = refs[chips - 1 : chips + 3]
    rest, all_ref = refs[chips + 3 : -1], refs[-1]
    chip, core = chip_and_core()
    for j in range(1, chips):
        all_ref[chip ^ j] = others[j - 1][...]
    all_ref[chip] = jnp.zeros(all_ref.shape[1:], F32)
    up, down, bottom_g, top_g = (own_coef[i] for i in range(4))
    for c in range(3):
        low = jnp.zeros(up.shape, F32)
        for t in range(chips - 1):
            low = jnp.where(t < chip, all_ref[t, c] + below_ref[t] * low, low)
        high = jnp.zeros(up.shape, F32)
        for t in range(chips - 1, 0, -1):
            high = jnp.where(t > chip, all_ref[t, c] + above_ref[t] * high, high)
        first, last = volt_ref[c], volt_ref[3 + c]
        j_bottom = (low - first - down * (high - last)) * bottom_g
        j_top = (last + up * (low - first) - high) * top_g
        if not whole:
            rest[0][c] = j_bottom
            rest[0][3 + c] = j_top
            continue
        solved_ref, bottom_ref, top_ref, out_ref, outer_ref, inner_ref = rest
        nz, nx, _ = bottom_ref.shape
        for k in range(nz):
            value = solved_ref[c, k] + bottom_ref[k] * j_bottom - top_ref[k] * j_top
            out_ref[c, k] = value
            store_edges(core, c, k, value[0:1], value[nx - 1 : nx], outer_ref, inner_ref)


def last_kernel(
    solved_ref, bottom_ref, top_ref, j_ref, solved_other, w_other, j_other, out_ref
):
    half = solved_other.shape[1]
    nx = solved_ref.shape[2]
    _, core = chip_and_core()
    mine = pl.ds(pl.multiple_of(core * nx, nx), nx)
    other = pl.ds(pl.multiple_of((1 - core) * nx, nx), nx)
    for c in range(3):
        for k in range(half):
            at = core * half + k
            out_ref[c, k, mine, :] = (
                solved_ref[c, at] + bottom_ref[at] * j_ref[c] - top_ref[at] * j_ref[3 + c]
            )
            out_ref[c, k, other, :] = (
                solved_other[c, k] + w_other[0, k] * j_other[c] - w_other[1, k] * j_other[3 + c]
            )


def per_device(strips, slabs, adjoint, base_flow, conductance, ground_mask, turbine_cells, yaw_bin, yaw_table):
    _, nz, nx, ny = adjoint.shape
    half, chips, levels = nx // 2, slabs // 2, 2 * nz
    cube, field, plane = (levels, half, ny), (3, levels, half, ny), (3, levels, ny)
    cores = [(i, i ^ 1) for i in range(slabs)]
    facing = []
    for strip in range(strips):
        for slab in range(slabs):
            other = strip + (1 if slab % 2 else -1)
            there = other * slabs + (slab ^ 1) if 0 <= other < strips else strip * slabs + (slab ^ 2)
            facing.append((strip * slabs + slab, there))

    def swap(part):
        return lax.ppermute(part, "gz", cores)

    def face(outer):
        return lax.ppermute(outer, ("gx", "gz"), facing)

    def across(parts):
        return [
            lax.ppermute(part, "gz", [(i, i ^ (2 * (j + 1))) for i in range(slabs)])
            for j, part in enumerate(parts)
        ]

    def share(whole, after=()):
        shape = (whole.shape[0], nz, half, ny)
        keep, send = call(share_kernel, [shape, shape], (whole,), 0.3, after=after)
        return keep, swap(send)

    part = lambda n: (n, half, ny)
    keep, recv = share(conductance[None])
    ratio, recip, bottom_w, top_w, own, w_send = call(
        slab_kernel,
        [cube, cube, cube, cube, part(3), (2, nz, half, ny)],
        (keep, recv),
        0.5,
        scratch=[pltpu.VMEM(cube, F32)],
    )
    coefs = across([own] * (chips - 1))
    extra = -(-nz // half)
    keep, send, row = call(
        share_kernel,
        [(3, nz, half, ny), (3, nz + extra, half, ny), (3, nz, ny)],
        (adjoint,),
        0.3,
        after=[recv],
    )
    flow_parts = share(base_flow, [keep])
    state, outer, inner = call(
        gather_state_kernel, [field, plane, plane], (keep, swap(send), row), 0.5, after=[own]
    )
    (flow,) = call(gather_kernel, [(2, *cube)], flow_parts, 0.3)
    (source,) = call(
        source_kernel, [field], (turbine_cells, yaw_bin[None], yaw_table), 1.0, after=[own]
    )
    for sweep_index in range(SWEEPS):
        first, last = sweep_index == 0, sweep_index == SWEEPS - 1
        outer = face(outer)
        if not first:
            inner = swap(inner)
        extra = [(2, levels, ny), (2, 2, levels, ny)] if first else []
        solved, ends, *extra = call(
            right_kernel,
            [field, part(6), *extra],
            (state, flow, source, ratio, recip, bottom_w, top_w),
            1.5,
        )
        if first:
            edge_w, end_w = extra
            below, above, own_coef = call(
                functools.partial(join_coef_kernel, chips),
                [(chips, half, ny), (chips, half, ny), part(4)],
                (own, *coefs, ground_mask),
                0.1,
                after=[ends],
                scratch=[pltpu.VMEM((chips, 3, half, ny), F32)],
            )
        volts, *parts = call(
            functools.partial(ends_kernel, chips),
            [part(6)] + [part(3)] * (chips - 1),
            (ends, outer, inner, end_w, own_coef),
            0.2,
        )
        others = across(parts)
        solved, *send = call(
            halo_kernel,
            [field] + ([(3, nz, half, ny)] if last else []),
            (solved, outer, inner, edge_w, ratio, recip),
            0.4,
            scratch=[pltpu.VMEM((3, 2, levels, ny), F32)],
        )
        more = () if last else (solved, bottom_w, top_w)
        outs = call(
            functools.partial(join_kernel, chips, not last),
            [part(6)] if last else [field, plane, plane],
            (*others, volts, below, above, own_coef, *more),
            0.4,
            scratch=[pltpu.VMEM((chips, 3, half, ny), F32)],
        )
        if not last:
            state, outer, inner = outs
    solved_other, w_other = swap(send[0]), swap(w_send)
    (currents,) = outs
    (out,) = call(
        last_kernel,
        [adjoint.shape],
        (solved, bottom_w, top_w, currents, solved_other, w_other, swap(currents)),
        1.0,
    )
    return out


def solution(mesh):
    in_specs = (
        P(None, "gz", "gx", None),
        P(None, "gz", "gx", None),
        P("gz", "gx", None),
        P("gx", None),
        P(),
        P(),
        P(),
    )
    out_specs = P(None, "gz", "gx", None)
    body = functools.partial(per_device, mesh.shape["gx"], mesh.shape["gz"])
    return jax.shard_map(body, mesh=mesh, in_specs=in_specs, out_specs=out_specs, check_vma=False)
```

time: 52.5 us -> 46.9 us (0.89)
  waiting for transfers between devices: 20.4 us -> 15.3 us
  starting transfers between devices: 20.1 us -> 19.2 us
  local copies, waits for them, and re-layouts: 2.47 us -> 3.1 us
    ppermute x9, waiting for transfers between devices: 12.4 us -> 8.94 us  [across(): lax.ppermute(part, 'gz', [(i, i ^ 2 * (j + 1)) for i in range(slabs)])]
    ppermute x9, waiting for transfers between devices: 7.98 us -> 6.38 us  [the longest x2 3.55 us: face(): return lax.ppermute(outer, ('gx', 'gz'), facing)]
    ppermute x9, starting transfers between devices: 6.79 us -> 5.94 us  [the longest x2 3.08 us: face(): return lax.ppermute(outer, ('gx', 'gz'), facing)]
    unnamed x16 -> x14, local copies, waits for them, and re-layouts: 2.47 us -> 3.1 us
  transfers between devices with their start and end apart: 18 -> 18, of which waited for: 13 -> 10; matrix products, arithmetic and copies ran while one was open for 0% -> 0% of each run, Pallas kernels for 13% -> 13%
where the time goes in v3:
time: 46.9 us; the launch traced here: 46.7 us
  starting transfers between devices  19.2 us (41%)
  waiting for transfers between devices  15.3 us (33%)
  Pallas kernels  8.83 us (19%)
  local copies, waits for them, and re-layouts  3.1 us (7%)
    ppermute x9, starting transfers between devices, across(): lax.ppermute(part, 'gz', [(i, i ^ 2 * (j + 1)) for i in range(slabs)])  13.3 us
    ppermute x9, waiting for transfers between devices, across(): lax.ppermute(part, 'gz', [(i, i ^ 2 * (j + 1)) for i in range(slabs)])  8.94 us
    pallas_call x17, Pallas kernels, call(): pl.pallas_call(run, out_shape=[jax.ShapeDtypeStruct(s, F32) for s in outs...  8.83 us
    ppermute x2, waiting for transfers between devices, face(): return lax.ppermute(outer, ('gx', 'gz'), facing)  3.55 us
    unnamed x14, local copies, waits for them, and re-layouts  3.1 us
    ppermute x2, starting transfers between devices, face(): return lax.ppermute(outer, ('gx', 'gz'), facing)  3.08 us
    ppermute x7, starting transfers between devices, swap(): return lax.ppermute(part, 'gz', cores)  2.86 us
    ppermute x7, waiting for transfers between devices, swap(): return lax.ppermute(part, 'gz', cores)  2.83 us
  transfers between devices with their start and end apart: 18, of which 10 were waited for; matrix products, arithmetic and copies ran while one was open for 0% of the time, Pallas kernels for 13%

profile of v3, /device:TPU:0, one launch (start us, length us, event | category | flops | bytes accessed | tf_op | source)
XLA Modules:
  0.0 46.7 jit_solution(4621184527298539277)
XLA Ops:
  0.0 1.0 %copy-done.2 = f32[16,16,512]{2,1,0:T(8,128)S(1)} copy-done((f32[16,16,512]{2,1,0:T(8,128)S(1)}, f32[16,16,512]{2,1,0:T(8,128)}, u32[]{:S(2)}) %copy-start.2) | copy-done | bytes 524312
  1.6 1.2 %collective-permute-done.refs_1_ = f32[1,16,8,512]{3,2,1,0:T(8,128)S(1)} collective-permute-done((f32[1,16,8,512]{3,2,1,0:T(8,128)S(1)}, f32[1,16,8,512]{3,2,1,0:T(8,128)S(1)}, u32[]{:S(2)}, u32[]{:S(2)}) %collective-permute-start) | collective-permute-done | bytes 262176 | tf_op jit(solution)/shard_map/ppermute | solution.py:378
  2.8 1.4 %copy-done = f32[3,16,16,512]{3,2,1,0:T(8,128)S(1)} copy-done((f32[3,16,16,512]{3,2,1,0:T(8,128)S(1)}, f32[3,16,16,512]{3,2,1,0:T(8,128)}, u32[]{:S(2)}) %copy-start) | copy-done | bytes 1572888
  4.8 0.6 %copy-done.1 = f32[2,16,16,512]{3,2,1,0:T(8,128)S(1)} copy-done((f32[2,16,16,512]{3,2,1,0:T(8,128)S(1)}, f32[2,16,16,512]{3,2,1,0:T(8,128)}, u32[]{:S(2)}) %copy-start.1) | copy-done | bytes 1048600
  7.0 3.0 %collective-permute-start.3 = (f32[3,32,512]{2,1,0:T(8,128)S(1)}, f32[3,32,512]{2,1,0:T(8,128)S(1)}, u32[]{:S(2)}, u32[]{:S(2)}) collective-permute-start(f32[3,32,512]{2,1,0:T(8,128)S(1)} %get-tuple-element.57), channel_id=1, source_target_pairs={{0,2},{1,8},{2,0},{3,10},{4,6},{5,12},{6,4},{7,14},{8,1},{9,16},{1... | collective-permute-start | bytes 589832 | tf_op jit(solution)/shard_map/ppermute | solution.py:381
  10.0 2.5 %collective-permute-start.6 = (f32[3,8,512]{2,1,0:T(8,128)S(1)}, f32[3,8,512]{2,1,0:T(8,128)S(1)}, u32[]{:S(2)}, u32[]{:S(2)}) collective-permute-start(f32[3,8,512]{2,1,0:T(8,128)S(1)} %get-tuple-element.48.refs_3_.refs_0_), channel_id=1, source_target_pairs={{0,6},{1,7},{2,4},{3,5},{4,2},{5,3},{6,0},{7,1},{8,14},{9,15},{10,... | collective-permute-start | bytes 147464 | tf_op jit(solution)/shard_map/ppermute | solution.py:385
  12.6 1.8 %collective-permute-start.4 = (f32[3,8,512]{2,1,0:T(8,128)S(1)}, f32[3,8,512]{2,1,0:T(8,128)S(1)}, u32[]{:S(2)}, u32[]{:S(2)}) collective-permute-start(f32[3,8,512]{2,1,0:T(8,128)S(1)} %get-tuple-element.48.refs_3_.refs_0_), channel_id=1, source_target_pairs={{0,2},{1,3},{2,0},{3,1},{4,6},{5,7},{6,4},{7,5},{8,10},{9,11},{10,... | collective-permute-start | bytes 147464 | tf_op jit(solution)/shard_map/ppermute | solution.py:385
  14.4 1.4 %shard_map.79.refs_2_ = f32[3,32,8,512]{3,2,1,0:T(8,128)S(1)} custom-call(s32[3,100]{1,0:T(4,128)S(1)} %copy-done.4, s32[1,100]{1,0:T(1,128)S(1)} %bitcast.3, f32[3,12]{1,0:T(4,128)S(1)} %copy-done.5, f32[3,8,512]{2,1,0:T(8,128)S(1)} %get-tuple-element.48.refs_3_.refs_0_), custom_call_target="tpu_custom_call" | custom-call | bytes 3000000 | tf_op jit(solution)/shard_map/pallas_call | solution.py:26
  16.0 1.5 %shard_map.80 = (f32[3,32,8,512]{3,2,1,0:T(8,128)S(1)}, f32[6,8,512]{2,1,0:T(8,128)S(1)}, f32[2,32,512]{2,1,0:T(8,128)S(1)}, f32[2,2,32,512]{3,2,1,0:T(8,128)S(1)}) custom-call(f32[3,32,8,512]{3,2,1,0:T(8,128)S(1)} %get-tuple-element.49.refs_0_, f32[2,32,8,512]{3,2,1,0:T(8,128)S(1)} %shard_map.78.refs_1_, f32[3,32,8,512]{3,2,1,0:T(8,128)S(1)} %shard_map.79.refs_2_, ...), custom_call_target="tpu_custom_call" | custom-call | bytes 4500000 | tf_op jit(solution)/shard_map/pallas_call | solution.py:26
  17.9 1.1 %collective-permute-done.5.refs_2_ = f32[3,8,512]{2,1,0:T(8,128)S(1)} collective-permute-done((f32[3,8,512]{2,1,0:T(8,128)S(1)}, f32[3,8,512]{2,1,0:T(8,128)S(1)}, u32[]{:S(2)}, u32[]{:S(2)}) %collective-permute-start.5) | collective-permute-done | bytes 49184 | tf_op jit(solution)/shard_map/ppermute | solution.py:385
  19.4 2.4 %collective-permute-start.8 = (f32[3,8,512]{2,1,0:T(8,128)S(1)}, f32[3,8,512]{2,1,0:T(8,128)S(1)}, u32[]{:S(2)}, u32[]{:S(2)}) collective-permute-start(f32[3,8,512]{2,1,0:T(8,128)S(1)} %get-tuple-element.62), channel_id=1, source_target_pairs={{0,4},{1,5},{2,6},{3,7},{4,0},{5,1},{6,2},{7,3},{8,12},{9,13},{10,... | collective-permute-start | bytes 147464 | tf_op jit(solution)/shard_map/ppermute | solution.py:385
  21.8 2.0 %collective-permute-start.9 = (f32[3,8,512]{2,1,0:T(8,128)S(1)}, f32[3,8,512]{2,1,0:T(8,128)S(1)}, u32[]{:S(2)}, u32[]{:S(2)}) collective-permute-start(f32[3,8,512]{2,1,0:T(8,128)S(1)} %get-tuple-element.63), channel_id=1, source_target_pairs={{0,6},{1,7},{2,4},{3,5},{4,2},{5,3},{6,0},{7,1},{8,14},{9,15},{10,... | collective-permute-start | bytes 147464 | tf_op jit(solution)/shard_map/ppermute | solution.py:385
  24.3 2.0 %collective-permute-done.8.refs_1_ = f32[3,8,512]{2,1,0:T(8,128)S(1)} collective-permute-done((f32[3,8,512]{2,1,0:T(8,128)S(1)}, f32[3,8,512]{2,1,0:T(8,128)S(1)}, u32[]{:S(2)}, u32[]{:S(2)}) %collective-permute-start.8) | collective-permute-done | bytes 49184 | tf_op jit(solution)/shard_map/ppermute | solution.py:385
  26.3 1.4 %collective-permute-done.9.refs_2_ = f32[3,8,512]{2,1,0:T(8,128)S(1)} collective-permute-done((f32[3,8,512]{2,1,0:T(8,128)S(1)}, f32[3,8,512]{2,1,0:T(8,128)S(1)}, u32[]{:S(2)}, u32[]{:S(2)}) %collective-permute-start.9) | collective-permute-done | bytes 49184 | tf_op jit(solution)/shard_map/ppermute | solution.py:385
  27.7 0.6 %shard_map.84 = (f32[3,32,8,512]{3,2,1,0:T(8,128)S(1)}, f32[3,32,512]{2,1,0:T(8,128)S(1)}, f32[3,32,512]{2,1,0:T(8,128)S(1)}) custom-call(f32[3,8,512]{2,1,0:T(8,128)S(1)} %collective-permute-done.7.refs_0_, f32[3,8,512]{2,1,0:T(8,128)S(1)} %collective-permute-done.8.refs_1_, f32[3,8,512]{2,1,0:T(8,128)S(1)} %collective-permute-done.9.refs_2_, ...), custom_call_target="tpu_custom_call" | custom-call | bytes 1200000 | tf_op jit(solution)/shard_map/pallas_call | solution.py:26
  28.4 0.8 %collective-permute-start.11 = (f32[3,32,512]{2,1,0:T(8,128)S(1)}, f32[3,32,512]{2,1,0:T(8,128)S(1)}, u32[]{:S(2)}, u32[]{:S(2)}) collective-permute-start(f32[3,32,512]{2,1,0:T(8,128)S(1)} %get-tuple-element.72), channel_id=1, source_target_pairs={{0,1},{1,0},{2,3},{3,2},{4,5},{5,4},{6,7},{7,6},{8,9},{9,8},{10,11... | collective-permute-start | bytes 589832 | tf_op jit(solution)/shard_map/ppermute | solution.py:378
  29.2 1.3 %shard_map.85 = (f32[3,32,8,512]{3,2,1,0:T(8,128)S(1)}, f32[6,8,512]{2,1,0:T(8,128)S(1)}) custom-call(f32[3,32,8,512]{3,2,1,0:T(8,128)S(1)} %get-tuple-element.69.refs_0_, f32[2,32,8,512]{3,2,1,0:T(8,128)S(1)} %shard_map.78.refs_1_, f32[3,32,8,512]{3,2,1,0:T(8,128)S(1)} %shard_map.79.refs_2_, f32[32,8,512]{2,1,0:T(8,128)S(1)} %get-tuple-element.52.refs_3_.refs_4_, ...), custom_call_target="tpu_custom_call" | custom-call | bytes 4500000 | tf_op jit(solution)/shard_map/pallas_call | solution.py:26
  30.5 3.5 %collective-permute-done.10.refs_1_ = f32[3,32,512]{2,1,0:T(8,128)S(1)} collective-permute-done((f32[3,32,512]{2,1,0:T(8,128)S(1)}, f32[3,32,512]{2,1,0:T(8,128)S(1)}, u32[]{:S(2)}, u32[]{:S(2)}) %collective-permute-start.10) | collective-permute-done | bytes 196640 | tf_op jit(solution)/shard_map/ppermute | solution.py:381
  35.9 2.1 %collective-permute-start.13 = (f32[3,8,512]{2,1,0:T(8,128)S(1)}, f32[3,8,512]{2,1,0:T(8,128)S(1)}, u32[]{:S(2)}, u32[]{:S(2)}) collective-permute-start(f32[3,8,512]{2,1,0:T(8,128)S(1)} %get-tuple-element.76), channel_id=1, source_target_pairs={{0,4},{1,5},{2,6},{3,7},{4,0},{5,1},{6,2},{7,3},{8,12},{9,13},{10,... | collective-permute-start | bytes 147464 | tf_op jit(solution)/shard_map/ppermute | solution.py:385
  38.0 1.8 %collective-permute-start.14 = (f32[3,8,512]{2,1,0:T(8,128)S(1)}, f32[3,8,512]{2,1,0:T(8,128)S(1)}, u32[]{:S(2)}, u32[]{:S(2)}) collective-permute-start(f32[3,8,512]{2,1,0:T(8,128)S(1)} %get-tuple-element.77), channel_id=1, source_target_pairs={{0,6},{1,7},{2,4},{3,5},{4,2},{5,3},{6,0},{7,1},{8,14},{9,15},{10,... | collective-permute-start | bytes 147464 | tf_op jit(solution)/shard_map/ppermute | solution.py:385
  39.8 2.9 %collective-permute-done.13.refs_1_ = f32[3,8,512]{2,1,0:T(8,128)S(1)} collective-permute-done((f32[3,8,512]{2,1,0:T(8,128)S(1)}, f32[3,8,512]{2,1,0:T(8,128)S(1)}, u32[]{:S(2)}, u32[]{:S(2)}) %collective-permute-start.13) | collective-permute-done | bytes 49184 | tf_op jit(solution)/shard_map/ppermute | solution.py:385
  42.7 1.2 %collective-permute-done.14.refs_2_ = f32[3,8,512]{2,1,0:T(8,128)S(1)} collective-permute-done((f32[3,8,512]{2,1,0:T(8,128)S(1)}, f32[3,8,512]{2,1,0:T(8,128)S(1)}, u32[]{:S(2)}, u32[]{:S(2)}) %collective-permute-start.14) | collective-permute-done | bytes 49184 | tf_op jit(solution)/shard_map/ppermute | solution.py:385
  44.0 1.3 %collective-permute-done.17.refs_6_ = f32[6,8,512]{2,1,0:T(8,128)S(1)} collective-permute-done((f32[6,8,512]{2,1,0:T(8,128)S(1)}, f32[6,8,512]{2,1,0:T(8,128)S(1)}, u32[]{:S(2)}, u32[]{:S(2)}) %collective-permute-start.17) | collective-permute-done | bytes 98336 | tf_op jit(solution)/shard_map/ppermute | solution.py:378
  45.3 1.4 %shard_map.89 = f32[3,16,16,512]{3,2,1,0:T(8,128)} custom-call(f32[3,32,8,512]{3,2,1,0:T(8,128)S(1)} %get-tuple-element.73.refs_0_, f32[32,8,512]{2,1,0:T(8,128)S(1)} %get-tuple-element.54.refs_5_.refs_8_.refs_1_, f32[32,8,512]{2,1,0:T(8,128)S(1)} %get-tuple-element.55.refs_6_.refs_9_.refs_2_, f32[6,8,512]{2,1,0:T(8,128)S(1)} %shard_map.88.refs_3_, ...), custom_call_target="tpu_custom_call" | custom-call | bytes 3000000 | tf_op jit(solution)/shard_map/pallas_call | solution.py:26
  (43 shorter events, 6.2 us)
Async XLA Ops:
  1.1 1.7 %collective-permute-start = (f32[1,16,8,512]{3,2,1,0:T(8,128)S(1)}, f32[1,16,8,512]{3,2,1,0:T(8,128)S(1)}, u32[]{:S(2)}, u32[]{:S(2)}) collective-permute-start(f32[1,16,8,512]{3,2,1,0:T(8,128)S(1)} %get-tuple-element.43), channel_id=1, source_target_pairs={{0,1},{1,0},{2,3},{3,2},{4,5},{5,4},{6,7},{7,6},{8,9},{9,8},{10,11... | collective-permute-start | bytes 786440 | tf_op jit(solution)/shard_map/ppermute | solution.py:378
  2.8 1.4 %copy-start = (f32[3,16,16,512]{3,2,1,0:T(8,128)S(1)}, f32[3,16,16,512]{3,2,1,0:T(8,128)}, u32[]{:S(2)}) copy-start(f32[3,16,16,512]{3,2,1,0:T(8,128)} %refs_0_.3) | copy-start | bytes 4718596
  4.2 1.2 %copy-start.1 = (f32[2,16,16,512]{3,2,1,0:T(8,128)S(1)}, f32[2,16,16,512]{3,2,1,0:T(8,128)}, u32[]{:S(2)}) copy-start(f32[2,16,16,512]{3,2,1,0:T(8,128)} %refs_0_.4) | copy-start | bytes 3145732
  4.3 2.5 %collective-permute-start.1 = (f32[3,18,8,512]{3,2,1,0:T(8,128)S(1)}, f32[3,18,8,512]{3,2,1,0:T(8,128)S(1)}, u32[]{:S(2)}, u32[]{:S(2)}) collective-permute-start(f32[3,18,8,512]{3,2,1,0:T(8,128)S(1)} %get-tuple-element.45), channel_id=1, source_target_pairs={{0,1},{1,0},{2,3},{3,2},{4,5},{5,4},{6,7},{7,6},{8,9},{9,8},{10,11... | collective-permute-start | bytes 2654216 | tf_op jit(solution)/shard_map/ppermute | solution.py:378
  5.5 9.0 %copy-start.4 = (s32[3,100]{1,0:T(4,128)S(1)}, s32[3,100]{1,0:T(4,128)}, u32[]{:S(2)}) copy-start(s32[3,100]{1,0:T(4,128)} %refs_0_.5) | copy-start | bytes 3604
  5.5 9.0 %copy-start.5 = (f32[3,12]{1,0:T(4,128)S(1)}, f32[3,12]{1,0:T(4,128)}, u32[]{:S(2)}) copy-start(f32[3,12]{1,0:T(4,128)} %refs_2_.1) | copy-start | bytes 436
  5.5 8.9 %copy-start.6 = (s32[100]{0:T(128)S(1)}, s32[100]{0:T(128)}, u32[]{:S(2)}) copy-start(s32[100]{0:T(128)} %param.12) | copy-start | bytes 1204
  5.5 10.4 %collective-permute-start.2 = (f32[2,16,8,512]{3,2,1,0:T(8,128)S(1)}, f32[2,16,8,512]{3,2,1,0:T(8,128)S(1)}, u32[]{:S(2)}, u32[]{:S(2)}) collective-permute-start(f32[2,16,8,512]{3,2,1,0:T(8,128)S(1)} %get-tuple-element.51), channel_id=1, source_target_pairs={{0,1},{1,0},{2,3},{3,2},{4,5},{5,4},{6,7},{7,6},{8,9},{9,8},{10,11... | collective-permute-start | bytes 1572872 | tf_op jit(solution)/shard_map/ppermute | solution.py:378
  7.0 12.1 %collective-permute-start.3 = (f32[3,32,512]{2,1,0:T(8,128)S(1)}, f32[3,32,512]{2,1,0:T(8,128)S(1)}, u32[]{:S(2)}, u32[]{:S(2)}) collective-permute-start(f32[3,32,512]{2,1,0:T(8,128)S(1)} %get-tuple-element.57), channel_id=1, source_target_pairs={{0,2},{1,8},{2,0},{3,10},{4,6},{5,12},{6,4},{7,14},{8,1},{9,16},{1... | collective-permute-start | bytes 589832 | tf_op jit(solution)/shard_map/ppermute | solution.py:381
  10.0 7.9 %collective-permute-start.6 = (f32[3,8,512]{2,1,0:T(8,128)S(1)}, f32[3,8,512]{2,1,0:T(8,128)S(1)}, u32[]{:S(2)}, u32[]{:S(2)}) collective-permute-start(f32[3,8,512]{2,1,0:T(8,128)S(1)} %get-tuple-element.48.refs_3_.refs_0_), channel_id=1, source_target_pairs={{0,6},{1,7},{2,4},{3,5},{4,2},{5,3},{6,0},{7,1},{8,14},{9,15},{10,... | collective-permute-start | bytes 147464 | tf_op jit(solution)/shard_map/ppermute | solution.py:385
  12.5 6.5 %collective-permute-start.5 = (f32[3,8,512]{2,1,0:T(8,128)S(1)}, f32[3,8,512]{2,1,0:T(8,128)S(1)}, u32[]{:S(2)}, u32[]{:S(2)}) collective-permute-start(f32[3,8,512]{2,1,0:T(8,128)S(1)} %get-tuple-element.48.refs_3_.refs_0_), channel_id=1, source_target_pairs={{0,4},{1,5},{2,6},{3,7},{4,0},{5,1},{6,2},{7,3},{8,12},{9,13},{10,... | collective-permute-start | bytes 147464 | tf_op jit(solution)/shard_map/ppermute | solution.py:385
  12.6 6.4 %collective-permute-start.4 = (f32[3,8,512]{2,1,0:T(8,128)S(1)}, f32[3,8,512]{2,1,0:T(8,128)S(1)}, u32[]{:S(2)}, u32[]{:S(2)}) collective-permute-start(f32[3,8,512]{2,1,0:T(8,128)S(1)} %get-tuple-element.48.refs_3_.refs_0_), channel_id=1, source_target_pairs={{0,2},{1,3},{2,0},{3,1},{4,6},{5,7},{6,4},{7,5},{8,10},{9,11},{10,... | collective-permute-start | bytes 147464 | tf_op jit(solution)/shard_map/ppermute | solution.py:385
  16.0 3.1 %copy-start.3 = (s32[16,512]{1,0:T(8,128)S(1)}, s32[16,512]{1,0:T(8,128)}, u32[]{:S(2)}) copy-start(s32[16,512]{1,0:T(8,128)} %refs_4_.1) | copy-start | bytes 98308
  19.3 5.0 %collective-permute-start.7 = (f32[3,8,512]{2,1,0:T(8,128)S(1)}, f32[3,8,512]{2,1,0:T(8,128)S(1)}, u32[]{:S(2)}, u32[]{:S(2)}) collective-permute-start(f32[3,8,512]{2,1,0:T(8,128)S(1)} %get-tuple-element.61), channel_id=1, source_target_pairs={{0,2},{1,3},{2,0},{3,1},{4,6},{5,7},{6,4},{7,5},{8,10},{9,11},{10,... | collective-permute-start | bytes 147464 | tf_op jit(solution)/shard_map/ppermute | solution.py:385
  19.4 6.9 %collective-permute-start.8 = (f32[3,8,512]{2,1,0:T(8,128)S(1)}, f32[3,8,512]{2,1,0:T(8,128)S(1)}, u32[]{:S(2)}, u32[]{:S(2)}) collective-permute-start(f32[3,8,512]{2,1,0:T(8,128)S(1)} %get-tuple-element.62), channel_id=1, source_target_pairs={{0,4},{1,5},{2,6},{3,7},{4,0},{5,1},{6,2},{7,3},{8,12},{9,13},{10,... | collective-permute-start | bytes 147464 | tf_op jit(solution)/shard_map/ppermute | solution.py:385
  21.8 5.9 %collective-permute-start.9 = (f32[3,8,512]{2,1,0:T(8,128)S(1)}, f32[3,8,512]{2,1,0:T(8,128)S(1)}, u32[]{:S(2)}, u32[]{:S(2)}) collective-permute-start(f32[3,8,512]{2,1,0:T(8,128)S(1)} %get-tuple-element.63), channel_id=1, source_target_pairs={{0,6},{1,7},{2,4},{3,5},{4,2},{5,3},{6,0},{7,1},{8,14},{9,15},{10,... | collective-permute-start | bytes 147464 | tf_op jit(solution)/shard_map/ppermute | solution.py:385
  28.3 5.7 %collective-permute-start.10 = (f32[3,32,512]{2,1,0:T(8,128)S(1)}, f32[3,32,512]{2,1,0:T(8,128)S(1)}, u32[]{:S(2)}, u32[]{:S(2)}) collective-permute-start(f32[3,32,512]{2,1,0:T(8,128)S(1)} %get-tuple-element.71), channel_id=1, source_target_pairs={{0,2},{1,8},{2,0},{3,10},{4,6},{5,12},{6,4},{7,14},{8,1},{9,16},{1... | collective-permute-start | bytes 589832 | tf_op jit(solution)/shard_map/ppermute | solution.py:381
  28.4 5.7 %collective-permute-start.11 = (f32[3,32,512]{2,1,0:T(8,128)S(1)}, f32[3,32,512]{2,1,0:T(8,128)S(1)}, u32[]{:S(2)}, u32[]{:S(2)}) collective-permute-start(f32[3,32,512]{2,1,0:T(8,128)S(1)} %get-tuple-element.72), channel_id=1, source_target_pairs={{0,1},{1,0},{2,3},{3,2},{4,5},{5,4},{6,7},{7,6},{8,9},{9,8},{10,11... | collective-permute-start | bytes 589832 | tf_op jit(solution)/shard_map/ppermute | solution.py:378
  34.6 10.7 %collective-permute-start.15 = (f32[3,16,8,512]{3,2,1,0:T(8,128)S(1)}, f32[3,16,8,512]{3,2,1,0:T(8,128)S(1)}, u32[]{:S(2)}, u32[]{:S(2)}) collective-permute-start(f32[3,16,8,512]{3,2,1,0:T(8,128)S(1)} %get-tuple-element.79), channel_id=1, source_target_pairs={{0,1},{1,0},{2,3},{3,2},{4,5},{5,4},{6,7},{7,6},{8,9},{9,8},{10,11... | collective-permute-start | bytes 2359304 | tf_op jit(solution)/shard_map/ppermute | solution.py:378
  34.7 9.3 %collective-permute-start.16 = (f32[2,16,8,512]{3,2,1,0:T(8,128)S(1)}, f32[2,16,8,512]{3,2,1,0:T(8,128)S(1)}, u32[]{:S(2)}, u32[]{:S(2)}) collective-permute-start(f32[2,16,8,512]{3,2,1,0:T(8,128)S(1)} %get-tuple-element.80), channel_id=1, source_target_pairs={{0,1},{1,0},{2,3},{3,2},{4,5},{5,4},{6,7},{7,6},{8,9},{9,8},{10,11... | collective-permute-start | bytes 1572872 | tf_op jit(solution)/shard_map/ppermute | solution.py:378
  35.4 4.5 %collective-permute-start.12 = (f32[3,8,512]{2,1,0:T(8,128)S(1)}, f32[3,8,512]{2,1,0:T(8,128)S(1)}, u32[]{:S(2)}, u32[]{:S(2)}) collective-permute-start(f32[3,8,512]{2,1,0:T(8,128)S(1)} %get-tuple-element.75), channel_id=1, source_target_pairs={{0,2},{1,3},{2,0},{3,1},{4,6},{5,7},{6,4},{7,5},{8,10},{9,11},{10,... | collective-permute-start | bytes 147464 | tf_op jit(solution)/shard_map/ppermute | solution.py:385
  35.9 6.8 %collective-permute-start.13 = (f32[3,8,512]{2,1,0:T(8,128)S(1)}, f32[3,8,512]{2,1,0:T(8,128)S(1)}, u32[]{:S(2)}, u32[]{:S(2)}) collective-permute-start(f32[3,8,512]{2,1,0:T(8,128)S(1)} %get-tuple-element.76), channel_id=1, source_target_pairs={{0,4},{1,5},{2,6},{3,7},{4,0},{5,1},{6,2},{7,3},{8,12},{9,13},{10,... | collective-permute-start | bytes 147464 | tf_op jit(solution)/shard_map/ppermute | solution.py:385
  38.0 5.9 %collective-permute-start.14 = (f32[3,8,512]{2,1,0:T(8,128)S(1)}, f32[3,8,512]{2,1,0:T(8,128)S(1)}, u32[]{:S(2)}, u32[]{:S(2)}) collective-permute-start(f32[3,8,512]{2,1,0:T(8,128)S(1)} %get-tuple-element.77), channel_id=1, source_target_pairs={{0,6},{1,7},{2,4},{3,5},{4,2},{5,3},{6,0},{7,1},{8,14},{9,15},{10,... | collective-permute-start | bytes 147464 | tf_op jit(solution)/shard_map/ppermute | solution.py:385
  43.9 1.4 %collective-permute-start.17 = (f32[6,8,512]{2,1,0:T(8,128)S(1)}, f32[6,8,512]{2,1,0:T(8,128)S(1)}, u32[]{:S(2)}, u32[]{:S(2)}) collective-permute-start(f32[6,8,512]{2,1,0:T(8,128)S(1)} %shard_map.88.refs_3_), channel_id=1, source_target_pairs={{0,1},{1,0},{2,3},{3,2},{4,5},{5,4},{6,7},{7,6},{8,9},{9,8},{10,11... | collective-permute-start | bytes 294920 | tf_op jit(solution)/shard_map/ppermute | solution.py:378
  (1 other events, 1.0 us)

commit v4 on v3

--- a/solution.py
+++ b/solution.py
@@ -14,26 +14,28 @@
 
 F32 = jnp.float32
 VMEM = pl.BlockSpec(memory_space=pltpu.VMEM)
-SMEM = pl.BlockSpec(memory_space=pltpu.SMEM)
 ANY = pl.BlockSpec(memory_space=pl.ANY)
-PARAMS = pltpu.CompilerParams(vmem_limit_bytes=12 * 1024 * 1024)
-
-
-def call(body, outs, ins, cost_us, specs=None, scratch=(), after=()):
+
+
+def call(body, outs, ins, cost_us, specs=None, scratch=(), after=(), through=()):
+    n, m, k = len(ins), len(ins) + len(after) + len(through), len(through)
+
     def run(*refs):
-        body(*refs[: len(ins)], *refs[len(ins) + len(after) :])
+        body(*refs[:n], *refs[m : m + len(outs)], *refs[m + len(outs) + k :])
 
     return pl.pallas_call(
         run,
-        out_shape=[jax.ShapeDtypeStruct(s, F32) for s in outs],
-        in_specs=(specs or [VMEM] * len(ins)) + [ANY] * len(after),
-        out_specs=[VMEM] * len(outs),
+        out_shape=[jax.ShapeDtypeStruct(s, F32) for s in outs]
+        + [jax.ShapeDtypeStruct(t.shape, F32) for t in through],
+        in_specs=(specs or [VMEM] * n) + [ANY] * (m - n),
+        out_specs=[VMEM] * len(outs) + [ANY] * k,
+        input_output_aliases={m - k + i: len(outs) + i for i in range(k)},
         scratch_shapes=list(scratch),
-        compiler_params=PARAMS,
+        compiler_params=pltpu.CompilerParams(vmem_limit_bytes=12 * 1024 * 1024),
         cost_estimate=pl.CostEstimate(
             flops=0, bytes_accessed=int(cost_us * 3.0e6), transcendentals=0
         ),
-    )(*ins, *after)
+    )(*ins, *after, *through)
 
 
 def chip_and_core():
@@ -381,10 +383,11 @@
         return lax.ppermute(outer, ("gx", "gz"), facing)
 
     def across(parts):
-        return [
-            lax.ppermute(part, "gz", [(i, i ^ (2 * (j + 1))) for i in range(slabs)])
-            for j, part in enumerate(parts)
-        ]
+        there = [None] * len(parts)
+        for j in range(len(parts), 0, -1):
+            pairs = [(i, i ^ (2 * j)) for i in range(slabs)]
+            there[j - 1] = lax.ppermute(parts[j - 1], "gz", pairs)
+        return there
 
     def share(whole, after=()):
         shape = (whole.shape[0], nz, half, ny)
@@ -392,31 +395,34 @@
         return keep, swap(send)
 
     part = lambda n: (n, half, ny)
-    keep, recv = share(conductance[None])
-    ratio, recip, bottom_w, top_w, own, w_send = call(
+    shape = (nz, half, ny)
+    keep, send = call(share_kernel, [(1, *shape)] * 2, (conductance[None],), 0.1)
+    extra = -(-nz // half)
+    state_keep, state_send, row = call(
+        share_kernel,
+        [(3, *shape), (3, nz + extra, half, ny), (3, nz, ny)],
+        (adjoint,),
+        0.3,
+        after=[keep],
+    )
+    ratio, recip, bottom_w, top_w, own, w_send, state_send = call(
         slab_kernel,
         [cube, cube, cube, cube, part(3), (2, nz, half, ny)],
-        (keep, recv),
+        (keep, swap(send)),
         0.5,
         scratch=[pltpu.VMEM(cube, F32)],
+        through=[state_send],
     )
     coefs = across([own] * (chips - 1))
-    extra = -(-nz // half)
-    keep, send, row = call(
-        share_kernel,
-        [(3, nz, half, ny), (3, nz + extra, half, ny), (3, nz, ny)],
-        (adjoint,),
-        0.3,
-        after=[recv],
-    )
-    flow_parts = share(base_flow, [keep])
-    state, outer, inner = call(
-        gather_state_kernel, [field, plane, plane], (keep, swap(send), row), 0.5, after=[own]
-    )
-    (flow,) = call(gather_kernel, [(2, *cube)], flow_parts, 0.3)
     (source,) = call(
         source_kernel, [field], (turbine_cells, yaw_bin[None], yaw_table), 1.0, after=[own]
     )
+    state_recv = swap(state_send)
+    state, outer, inner = call(
+        gather_state_kernel, [field, plane, plane], (state_keep, state_recv, row), 0.3, after=[source]
+    )
+    flow_keep, flow_recv = share(base_flow, [own])
+    (flow,) = call(gather_kernel, [(2, *cube)], (flow_keep, flow_recv), 0.1)
     for sweep_index in range(SWEEPS):
         first, last = sweep_index == 0, sweep_index == SWEEPS - 1
         outer = face(outer)
@@ -436,8 +442,8 @@
                 [(chips, half, ny), (chips, half, ny), part(4)],
                 (own, *coefs, ground_mask),
                 0.1,
+                scratch=[pltpu.VMEM((chips, 3, half, ny), F32)],
                 after=[ends],
-                scratch=[pltpu.VMEM((chips, 3, half, ny), F32)],
             )
         volts, *parts = call(
             functools.partial(ends_kernel, chips),
@@ -451,6 +457,7 @@
             [field] + ([(3, nz, half, ny)] if last else []),
             (solved, outer, inner, edge_w, ratio, recip),
             0.4,
+            after=parts[:1],
             scratch=[pltpu.VMEM((3, 2, levels, ny), F32)],
         )
         more = () if last else (solved, bottom_w, top_w)

time: 46.9 us -> 44.7 us (0.953)
  starting transfers between devices: 19.2 us -> 17.1 us
    ppermute x9, waiting for transfers between devices: 8.94 us -> 10.9 us  [across(): there[j - 1] = lax.ppermute(parts[j - 1], 'gz', pairs)]
    ppermute x9, starting transfers between devices: 13.3 us -> 11.4 us  [across(): there[j - 1] = lax.ppermute(parts[j - 1], 'gz', pairs)]
    ppermute x7, waiting for transfers between devices: 2.83 us -> 1.61 us  [swap(): return lax.ppermute(part, 'gz', cores)]
    ppermute x2, waiting for transfers between devices: 3.55 us -> 2.94 us  [face(): return lax.ppermute(outer, ('gx', 'gz'), facing)]
    ppermute x7, starting transfers between devices: 2.86 us -> 2.3 us  [swap(): return lax.ppermute(part, 'gz', cores)]
  transfers between devices with their start and end apart: 18 -> 18, of which waited for: 10 -> 10; matrix products, arithmetic and copies ran while one was open for 0% -> 0% of each run, Pallas kernels for 13% -> 12%
where the time goes in v4:
time: 44.7 us; the launch traced here: 44.5 us
  starting transfers between devices  17.1 us (38%)
  waiting for transfers between devices  15.5 us (35%)
  Pallas kernels  8.84 us (20%)
  local copies, waits for them, and re-layouts  2.86 us (6%)
    ppermute x9, starting transfers between devices, across(): there[j - 1] = lax.ppermute(parts[j - 1], 'gz', pairs)  11.4 us
    ppermute x9, waiting for transfers between devices, across(): there[j - 1] = lax.ppermute(parts[j - 1], 'gz', pairs)  10.9 us
    pallas_call x17, Pallas kernels, call(): pl.pallas_call(run, out_shape=[jax.ShapeDtypeStruct(s, F32) for s in outs...  8.84 us
    ppermute x2, starting transfers between devices, face(): return lax.ppermute(outer, ('gx', 'gz'), facing)  3.41 us
    ppermute x2, waiting for transfers between devices, face(): return lax.ppermute(outer, ('gx', 'gz'), facing)  2.94 us
    unnamed x14, local copies, waits for them, and re-layouts  2.86 us
    ppermute x7, starting transfers between devices, swap(): return lax.ppermute(part, 'gz', cores)  2.3 us
    ppermute x7, waiting for transfers between devices, swap(): return lax.ppermute(part, 'gz', cores)  1.61 us
  transfers between devices with their start and end apart: 18, of which 10 were waited for; matrix products, arithmetic and copies ran while one was open for 0% of the time, Pallas kernels for 12%

profile of v4, /device:TPU:0, one launch (start us, length us, event | category | flops | bytes accessed | tf_op | source)
XLA Modules:
  0.0 44.5 jit_solution(15962552651899118941)
XLA Ops:
  0.0 1.0 %copy-done.2 = f32[16,16,512]{2,1,0:T(8,128)S(1)} copy-done((f32[16,16,512]{2,1,0:T(8,128)S(1)}, f32[16,16,512]{2,1,0:T(8,128)}, u32[]{:S(2)}) %copy-start.2) | copy-done | bytes 524312
  1.6 1.4 %copy-done = f32[3,16,16,512]{3,2,1,0:T(8,128)S(1)} copy-done((f32[3,16,16,512]{3,2,1,0:T(8,128)S(1)}, f32[3,16,16,512]{3,2,1,0:T(8,128)}, u32[]{:S(2)}) %copy-start) | copy-done | bytes 1572888
  4.4 1.4 %shard_map.76.refs_3_.refs_2_ = f32[3,32,8,512]{3,2,1,0:T(8,128)S(1)} custom-call(s32[3,100]{1,0:T(4,128)S(1)} %copy-done.4, s32[1,100]{1,0:T(1,128)S(1)} %bitcast.3, f32[3,12]{1,0:T(4,128)S(1)} %copy-done.5, f32[3,8,512]{2,1,0:T(8,128)S(1)} %get-tuple-element.50.refs_3_.refs_1_.refs_0_), custom_call_target="tpu_custom_call" | custom-call | bytes 3000000 | tf_op jit(solution)/shard_map/pallas_call | solution.py:26
  6.4 2.8 %collective-permute-start.3 = (f32[3,32,512]{2,1,0:T(8,128)S(1)}, f32[3,32,512]{2,1,0:T(8,128)S(1)}, u32[]{:S(2)}, u32[]{:S(2)}) collective-permute-start(f32[3,32,512]{2,1,0:T(8,128)S(1)} %get-tuple-element.59), channel_id=1, source_target_pairs={{0,2},{1,8},{2,0},{3,10},{4,6},{5,12},{6,4},{7,14},{8,1},{9,16},{1... | collective-permute-start | bytes 589832 | tf_op jit(solution)/shard_map/ppermute | solution.py:383
  9.2 2.5 %collective-permute-start.6 = (f32[3,8,512]{2,1,0:T(8,128)S(1)}, f32[3,8,512]{2,1,0:T(8,128)S(1)}, u32[]{:S(2)}, u32[]{:S(2)}) collective-permute-start(f32[3,8,512]{2,1,0:T(8,128)S(1)} %get-tuple-element.50.refs_3_.refs_1_.refs_0_), channel_id=1, source_target_pairs={{0,6},{1,7},{2,4},{3,5},{4,2},{5,3},{6,0},{7,1},{8,14},{9,15},{10,... | collective-permute-start | bytes 147464 | tf_op jit(solution)/shard_map/ppermute | solution.py:389
  11.8 1.8 %collective-permute-start.4 = (f32[3,8,512]{2,1,0:T(8,128)S(1)}, f32[3,8,512]{2,1,0:T(8,128)S(1)}, u32[]{:S(2)}, u32[]{:S(2)}) collective-permute-start(f32[3,8,512]{2,1,0:T(8,128)S(1)} %get-tuple-element.50.refs_3_.refs_1_.refs_0_), channel_id=1, source_target_pairs={{0,2},{1,3},{2,0},{3,1},{4,6},{5,7},{6,4},{7,5},{8,10},{9,11},{10,... | collective-permute-start | bytes 147464 | tf_op jit(solution)/shard_map/ppermute | solution.py:389
  13.7 1.5 %shard_map.80 = (f32[3,32,8,512]{3,2,1,0:T(8,128)S(1)}, f32[6,8,512]{2,1,0:T(8,128)S(1)}, f32[2,32,512]{2,1,0:T(8,128)S(1)}, f32[2,2,32,512]{3,2,1,0:T(8,128)S(1)}) custom-call(f32[3,32,8,512]{3,2,1,0:T(8,128)S(1)} %get-tuple-element.51.refs_0_, f32[2,32,8,512]{3,2,1,0:T(8,128)S(1)} %shard_map.79.refs_1_, f32[3,32,8,512]{3,2,1,0:T(8,128)S(1)} %shard_map.76.refs_3_.refs_2_, ...), custom_call_target="tpu_custom_call" | custom-call | bytes 4500000 | tf_op jit(solution)/shard_map/pallas_call | solution.py:26
  15.2 1.9 %collective-permute-done.6.refs_3_ = f32[3,8,512]{2,1,0:T(8,128)S(1)} collective-permute-done((f32[3,8,512]{2,1,0:T(8,128)S(1)}, f32[3,8,512]{2,1,0:T(8,128)S(1)}, u32[]{:S(2)}, u32[]{:S(2)}) %collective-permute-start.6) | collective-permute-done | bytes 49184 | tf_op jit(solution)/shard_map/ppermute | solution.py:389
  17.1 1.1 %collective-permute-done.5.refs_2_ = f32[3,8,512]{2,1,0:T(8,128)S(1)} collective-permute-done((f32[3,8,512]{2,1,0:T(8,128)S(1)}, f32[3,8,512]{2,1,0:T(8,128)S(1)}, u32[]{:S(2)}, u32[]{:S(2)}) %collective-permute-start.5) | collective-permute-done | bytes 49184 | tf_op jit(solution)/shard_map/ppermute | solution.py:389
  18.5 0.9 %collective-permute-start.8 = (f32[3,8,512]{2,1,0:T(8,128)S(1)}, f32[3,8,512]{2,1,0:T(8,128)S(1)}, u32[]{:S(2)}, u32[]{:S(2)}) collective-permute-start(f32[3,8,512]{2,1,0:T(8,128)S(1)} %get-tuple-element.64), channel_id=1, source_target_pairs={{0,4},{1,5},{2,6},{3,7},{4,0},{5,1},{6,2},{7,3},{8,12},{9,13},{10,... | collective-permute-start | bytes 147464 | tf_op jit(solution)/shard_map/ppermute | solution.py:389
  19.4 1.6 %collective-permute-start.9 = (f32[3,8,512]{2,1,0:T(8,128)S(1)}, f32[3,8,512]{2,1,0:T(8,128)S(1)}, u32[]{:S(2)}, u32[]{:S(2)}) collective-permute-start(f32[3,8,512]{2,1,0:T(8,128)S(1)} %get-tuple-element.65), channel_id=1, source_target_pairs={{0,6},{1,7},{2,4},{3,5},{4,2},{5,3},{6,0},{7,1},{8,14},{9,15},{10,... | collective-permute-start | bytes 147464 | tf_op jit(solution)/shard_map/ppermute | solution.py:389
  20.9 1.1 %collective-permute-start.7 = (f32[3,8,512]{2,1,0:T(8,128)S(1)}, f32[3,8,512]{2,1,0:T(8,128)S(1)}, u32[]{:S(2)}, u32[]{:S(2)}) collective-permute-start(f32[3,8,512]{2,1,0:T(8,128)S(1)} %get-tuple-element.63.refs_6_), channel_id=1, source_target_pairs={{0,2},{1,3},{2,0},{3,1},{4,6},{5,7},{6,4},{7,5},{8,10},{9,11},{10,... | collective-permute-start | bytes 147464 | tf_op jit(solution)/shard_map/ppermute | solution.py:389
  22.5 2.1 %collective-permute-done.8.refs_1_ = f32[3,8,512]{2,1,0:T(8,128)S(1)} collective-permute-done((f32[3,8,512]{2,1,0:T(8,128)S(1)}, f32[3,8,512]{2,1,0:T(8,128)S(1)}, u32[]{:S(2)}, u32[]{:S(2)}) %collective-permute-start.8) | collective-permute-done | bytes 49184 | tf_op jit(solution)/shard_map/ppermute | solution.py:389
  24.6 0.8 %collective-permute-done.9.refs_2_ = f32[3,8,512]{2,1,0:T(8,128)S(1)} collective-permute-done((f32[3,8,512]{2,1,0:T(8,128)S(1)}, f32[3,8,512]{2,1,0:T(8,128)S(1)}, u32[]{:S(2)}, u32[]{:S(2)}) %collective-permute-start.9) | collective-permute-done | bytes 49184 | tf_op jit(solution)/shard_map/ppermute | solution.py:389
  25.8 0.6 %shard_map.84 = (f32[3,32,8,512]{3,2,1,0:T(8,128)S(1)}, f32[3,32,512]{2,1,0:T(8,128)S(1)}, f32[3,32,512]{2,1,0:T(8,128)S(1)}) custom-call(f32[3,8,512]{2,1,0:T(8,128)S(1)} %collective-permute-done.7.refs_0_, f32[3,8,512]{2,1,0:T(8,128)S(1)} %collective-permute-done.8.refs_1_, f32[3,8,512]{2,1,0:T(8,128)S(1)} %collective-permute-done.9.refs_2_, ...), custom_call_target="tpu_custom_call" | custom-call | bytes 1200000 | tf_op jit(solution)/shard_map/pallas_call | solution.py:26
  26.5 0.6 %collective-permute-start.10 = (f32[3,32,512]{2,1,0:T(8,128)S(1)}, f32[3,32,512]{2,1,0:T(8,128)S(1)}, u32[]{:S(2)}, u32[]{:S(2)}) collective-permute-start(f32[3,32,512]{2,1,0:T(8,128)S(1)} %get-tuple-element.73), channel_id=1, source_target_pairs={{0,2},{1,8},{2,0},{3,10},{4,6},{5,12},{6,4},{7,14},{8,1},{9,16},{1... | collective-permute-start | bytes 589832 | tf_op jit(solution)/shard_map/ppermute | solution.py:383
  27.1 0.9 %collective-permute-start.11 = (f32[3,32,512]{2,1,0:T(8,128)S(1)}, f32[3,32,512]{2,1,0:T(8,128)S(1)}, u32[]{:S(2)}, u32[]{:S(2)}) collective-permute-start(f32[3,32,512]{2,1,0:T(8,128)S(1)} %get-tuple-element.74), channel_id=1, source_target_pairs={{0,1},{1,0},{2,3},{3,2},{4,5},{5,4},{6,7},{7,6},{8,9},{9,8},{10,11... | collective-permute-start | bytes 589832 | tf_op jit(solution)/shard_map/ppermute | solution.py:380
  28.0 1.3 %shard_map.85 = (f32[3,32,8,512]{3,2,1,0:T(8,128)S(1)}, f32[6,8,512]{2,1,0:T(8,128)S(1)}) custom-call(f32[3,32,8,512]{3,2,1,0:T(8,128)S(1)} %get-tuple-element.71.refs_0_, f32[2,32,8,512]{3,2,1,0:T(8,128)S(1)} %shard_map.79.refs_1_, f32[3,32,8,512]{3,2,1,0:T(8,128)S(1)} %shard_map.76.refs_3_.refs_2_, f32[32,8,512]{2,1,0:T(8,128)S(1)} %get-tuple-element.54.refs_3_.refs_4_, ...), custom_call_target="tpu_custom_call" | custom-call | bytes 4500000 | tf_op jit(solution)/shard_map/pallas_call | solution.py:26
  29.3 2.9 %collective-permute-done.10.refs_1_ = f32[3,32,512]{2,1,0:T(8,128)S(1)} collective-permute-done((f32[3,32,512]{2,1,0:T(8,128)S(1)}, f32[3,32,512]{2,1,0:T(8,128)S(1)}, u32[]{:S(2)}, u32[]{:S(2)}) %collective-permute-start.10) | collective-permute-done | bytes 196640 | tf_op jit(solution)/shard_map/ppermute | solution.py:383
  33.5 1.2 %collective-permute-start.13 = (f32[3,8,512]{2,1,0:T(8,128)S(1)}, f32[3,8,512]{2,1,0:T(8,128)S(1)}, u32[]{:S(2)}, u32[]{:S(2)}) collective-permute-start(f32[3,8,512]{2,1,0:T(8,128)S(1)} %get-tuple-element.78), channel_id=1, source_target_pairs={{0,4},{1,5},{2,6},{3,7},{4,0},{5,1},{6,2},{7,3},{8,12},{9,13},{10,... | collective-permute-start | bytes 147464 | tf_op jit(solution)/shard_map/ppermute | solution.py:389
  34.7 2.2 %collective-permute-start.14 = (f32[3,8,512]{2,1,0:T(8,128)S(1)}, f32[3,8,512]{2,1,0:T(8,128)S(1)}, u32[]{:S(2)}, u32[]{:S(2)}) collective-permute-start(f32[3,8,512]{2,1,0:T(8,128)S(1)} %get-tuple-element.79), channel_id=1, source_target_pairs={{0,6},{1,7},{2,4},{3,5},{4,2},{5,3},{6,0},{7,1},{8,14},{9,15},{10,... | collective-permute-start | bytes 147464 | tf_op jit(solution)/shard_map/ppermute | solution.py:389
  37.0 4.1 %collective-permute-done.13.refs_1_ = f32[3,8,512]{2,1,0:T(8,128)S(1)} collective-permute-done((f32[3,8,512]{2,1,0:T(8,128)S(1)}, f32[3,8,512]{2,1,0:T(8,128)S(1)}, u32[]{:S(2)}, u32[]{:S(2)}) %collective-permute-start.13) | collective-permute-done | bytes 49184 | tf_op jit(solution)/shard_map/ppermute | solution.py:389
  41.8 1.3 %collective-permute-done.17.refs_6_ = f32[6,8,512]{2,1,0:T(8,128)S(1)} collective-permute-done((f32[6,8,512]{2,1,0:T(8,128)S(1)}, f32[6,8,512]{2,1,0:T(8,128)S(1)}, u32[]{:S(2)}, u32[]{:S(2)}) %collective-permute-start.17) | collective-permute-done | bytes 98336 | tf_op jit(solution)/shard_map/ppermute | solution.py:380
  43.1 1.4 %shard_map.89 = f32[3,16,16,512]{3,2,1,0:T(8,128)} custom-call(f32[3,32,8,512]{3,2,1,0:T(8,128)S(1)} %get-tuple-element.77.refs_0_, f32[32,8,512]{2,1,0:T(8,128)S(1)} %get-tuple-element.56.refs_5_.refs_8_.refs_1_, f32[32,8,512]{2,1,0:T(8,128)S(1)} %get-tuple-element.57.refs_6_.refs_9_.refs_2_, f32[6,8,512]{2,1,0:T(8,128)S(1)} %shard_map.88.refs_3_, ...), custom_call_target="tpu_custom_call" | custom-call | bytes 3000000 | tf_op jit(solution)/shard_map/pallas_call | solution.py:26
  (43 shorter events, 6.0 us)
Async XLA Ops:
  1.1 2.1 %collective-permute-start = (f32[1,16,8,512]{3,2,1,0:T(8,128)S(1)}, f32[1,16,8,512]{3,2,1,0:T(8,128)S(1)}, u32[]{:S(2)}, u32[]{:S(2)}) collective-permute-start(f32[1,16,8,512]{3,2,1,0:T(8,128)S(1)} %get-tuple-element.46), channel_id=1, source_target_pairs={{0,1},{1,0},{2,3},{3,2},{4,5},{5,4},{6,7},{7,6},{8,9},{9,8},{10,11... | collective-permute-start | bytes 786440 | tf_op jit(solution)/shard_map/ppermute | solution.py:380
  1.6 1.4 %copy-start = (f32[3,16,16,512]{3,2,1,0:T(8,128)S(1)}, f32[3,16,16,512]{3,2,1,0:T(8,128)}, u32[]{:S(2)}) copy-start(f32[3,16,16,512]{3,2,1,0:T(8,128)} %refs_0_.3) | copy-start | bytes 4718596
  3.0 1.2 %copy-start.1 = (f32[2,16,16,512]{3,2,1,0:T(8,128)S(1)}, f32[2,16,16,512]{3,2,1,0:T(8,128)}, u32[]{:S(2)}) copy-start(f32[2,16,16,512]{3,2,1,0:T(8,128)} %refs_0_.5) | copy-start | bytes 3145732
  3.2 1.3 %copy-start.4 = (s32[3,100]{1,0:T(4,128)S(1)}, s32[3,100]{1,0:T(4,128)}, u32[]{:S(2)}) copy-start(s32[3,100]{1,0:T(4,128)} %refs_0_.4) | copy-start | bytes 3604
  3.2 1.3 %copy-start.5 = (f32[3,12]{1,0:T(4,128)S(1)}, f32[3,12]{1,0:T(4,128)}, u32[]{:S(2)}) copy-start(f32[3,12]{1,0:T(4,128)} %refs_2_.1) | copy-start | bytes 436
  3.2 1.3 %copy-start.6 = (s32[100]{0:T(128)S(1)}, s32[100]{0:T(128)}, u32[]{:S(2)}) copy-start(s32[100]{0:T(128)} %param.12) | copy-start | bytes 1204
  3.7 2.5 %collective-permute-start.1 = (f32[3,18,8,512]{3,2,1,0:T(8,128)S(1)}, f32[3,18,8,512]{3,2,1,0:T(8,128)S(1)}, u32[]{:S(2)}, u32[]{:S(2)}) collective-permute-start(f32[3,18,8,512]{3,2,1,0:T(8,128)S(1)} %get-tuple-element.48), channel_id=1, source_target_pairs={{0,1},{1,0},{2,3},{3,2},{4,5},{5,4},{6,7},{7,6},{8,9},{9,8},{10,11... | collective-permute-start | bytes 2654216 | tf_op jit(solution)/shard_map/ppermute | solution.py:380
  4.3 9.3 %collective-permute-start.2 = (f32[2,16,8,512]{3,2,1,0:T(8,128)S(1)}, f32[2,16,8,512]{3,2,1,0:T(8,128)S(1)}, u32[]{:S(2)}, u32[]{:S(2)}) collective-permute-start(f32[2,16,8,512]{3,2,1,0:T(8,128)S(1)} %get-tuple-element.53), channel_id=1, source_target_pairs={{0,1},{1,0},{2,3},{3,2},{4,5},{5,4},{6,7},{7,6},{8,9},{9,8},{10,11... | collective-permute-start | bytes 1572872 | tf_op jit(solution)/shard_map/ppermute | solution.py:380
  6.4 11.9 %collective-permute-start.3 = (f32[3,32,512]{2,1,0:T(8,128)S(1)}, f32[3,32,512]{2,1,0:T(8,128)S(1)}, u32[]{:S(2)}, u32[]{:S(2)}) collective-permute-start(f32[3,32,512]{2,1,0:T(8,128)S(1)} %get-tuple-element.59), channel_id=1, source_target_pairs={{0,2},{1,8},{2,0},{3,10},{4,6},{5,12},{6,4},{7,14},{8,1},{9,16},{1... | collective-permute-start | bytes 589832 | tf_op jit(solution)/shard_map/ppermute | solution.py:383
  9.2 7.9 %collective-permute-start.6 = (f32[3,8,512]{2,1,0:T(8,128)S(1)}, f32[3,8,512]{2,1,0:T(8,128)S(1)}, u32[]{:S(2)}, u32[]{:S(2)}) collective-permute-start(f32[3,8,512]{2,1,0:T(8,128)S(1)} %get-tuple-element.50.refs_3_.refs_1_.refs_0_), channel_id=1, source_target_pairs={{0,6},{1,7},{2,4},{3,5},{4,2},{5,3},{6,0},{7,1},{8,14},{9,15},{10,... | collective-permute-start | bytes 147464 | tf_op jit(solution)/shard_map/ppermute | solution.py:389
  11.7 6.5 %collective-permute-start.5 = (f32[3,8,512]{2,1,0:T(8,128)S(1)}, f32[3,8,512]{2,1,0:T(8,128)S(1)}, u32[]{:S(2)}, u32[]{:S(2)}) collective-permute-start(f32[3,8,512]{2,1,0:T(8,128)S(1)} %get-tuple-element.50.refs_3_.refs_1_.refs_0_), channel_id=1, source_target_pairs={{0,4},{1,5},{2,6},{3,7},{4,0},{5,1},{6,2},{7,3},{8,12},{9,13},{10,... | collective-permute-start | bytes 147464 | tf_op jit(solution)/shard_map/ppermute | solution.py:389
  11.8 6.4 %collective-permute-start.4 = (f32[3,8,512]{2,1,0:T(8,128)S(1)}, f32[3,8,512]{2,1,0:T(8,128)S(1)}, u32[]{:S(2)}, u32[]{:S(2)}) collective-permute-start(f32[3,8,512]{2,1,0:T(8,128)S(1)} %get-tuple-element.50.refs_3_.refs_1_.refs_0_), channel_id=1, source_target_pairs={{0,2},{1,3},{2,0},{3,1},{4,6},{5,7},{6,4},{7,5},{8,10},{9,11},{10,... | collective-permute-start | bytes 147464 | tf_op jit(solution)/shard_map/ppermute | solution.py:389
  13.7 4.5 %copy-start.3 = (s32[16,512]{1,0:T(8,128)S(1)}, s32[16,512]{1,0:T(8,128)}, u32[]{:S(2)}) copy-start(s32[16,512]{1,0:T(8,128)} %refs_4_.1) | copy-start | bytes 98308
  18.5 6.1 %collective-permute-start.8 = (f32[3,8,512]{2,1,0:T(8,128)S(1)}, f32[3,8,512]{2,1,0:T(8,128)S(1)}, u32[]{:S(2)}, u32[]{:S(2)}) collective-permute-start(f32[3,8,512]{2,1,0:T(8,128)S(1)} %get-tuple-element.64), channel_id=1, source_target_pairs={{0,4},{1,5},{2,6},{3,7},{4,0},{5,1},{6,2},{7,3},{8,12},{9,13},{10,... | collective-permute-start | bytes 147464 | tf_op jit(solution)/shard_map/ppermute | solution.py:389
  19.4 6.0 %collective-permute-start.9 = (f32[3,8,512]{2,1,0:T(8,128)S(1)}, f32[3,8,512]{2,1,0:T(8,128)S(1)}, u32[]{:S(2)}, u32[]{:S(2)}) collective-permute-start(f32[3,8,512]{2,1,0:T(8,128)S(1)} %get-tuple-element.65), channel_id=1, source_target_pairs={{0,6},{1,7},{2,4},{3,5},{4,2},{5,3},{6,0},{7,1},{8,14},{9,15},{10,... | collective-permute-start | bytes 147464 | tf_op jit(solution)/shard_map/ppermute | solution.py:389
  20.9 4.9 %collective-permute-start.7 = (f32[3,8,512]{2,1,0:T(8,128)S(1)}, f32[3,8,512]{2,1,0:T(8,128)S(1)}, u32[]{:S(2)}, u32[]{:S(2)}) collective-permute-start(f32[3,8,512]{2,1,0:T(8,128)S(1)} %get-tuple-element.63.refs_6_), channel_id=1, source_target_pairs={{0,2},{1,3},{2,0},{3,1},{4,6},{5,7},{6,4},{7,5},{8,10},{9,11},{10,... | collective-permute-start | bytes 147464 | tf_op jit(solution)/shard_map/ppermute | solution.py:389
  26.5 5.7 %collective-permute-start.10 = (f32[3,32,512]{2,1,0:T(8,128)S(1)}, f32[3,32,512]{2,1,0:T(8,128)S(1)}, u32[]{:S(2)}, u32[]{:S(2)}) collective-permute-start(f32[3,32,512]{2,1,0:T(8,128)S(1)} %get-tuple-element.73), channel_id=1, source_target_pairs={{0,2},{1,8},{2,0},{3,10},{4,6},{5,12},{6,4},{7,14},{8,1},{9,16},{1... | collective-permute-start | bytes 589832 | tf_op jit(solution)/shard_map/ppermute | solution.py:383
  27.1 5.1 %collective-permute-start.11 = (f32[3,32,512]{2,1,0:T(8,128)S(1)}, f32[3,32,512]{2,1,0:T(8,128)S(1)}, u32[]{:S(2)}, u32[]{:S(2)}) collective-permute-start(f32[3,32,512]{2,1,0:T(8,128)S(1)} %get-tuple-element.74), channel_id=1, source_target_pairs={{0,1},{1,0},{2,3},{3,2},{4,5},{5,4},{6,7},{7,6},{8,9},{9,8},{10,11... | collective-permute-start | bytes 589832 | tf_op jit(solution)/shard_map/ppermute | solution.py:380
  32.9 10.2 %collective-permute-start.15 = (f32[3,16,8,512]{3,2,1,0:T(8,128)S(1)}, f32[3,16,8,512]{3,2,1,0:T(8,128)S(1)}, u32[]{:S(2)}, u32[]{:S(2)}) collective-permute-start(f32[3,16,8,512]{3,2,1,0:T(8,128)S(1)} %get-tuple-element.81), channel_id=1, source_target_pairs={{0,1},{1,0},{2,3},{3,2},{4,5},{5,4},{6,7},{7,6},{8,9},{9,8},{10,11... | collective-permute-start | bytes 2359304 | tf_op jit(solution)/shard_map/ppermute | solution.py:380
  33.3 8.5 %collective-permute-start.16 = (f32[2,16,8,512]{3,2,1,0:T(8,128)S(1)}, f32[2,16,8,512]{3,2,1,0:T(8,128)S(1)}, u32[]{:S(2)}, u32[]{:S(2)}) collective-permute-start(f32[2,16,8,512]{3,2,1,0:T(8,128)S(1)} %get-tuple-element.82), channel_id=1, source_target_pairs={{0,1},{1,0},{2,3},{3,2},{4,5},{5,4},{6,7},{7,6},{8,9},{9,8},{10,11... | collective-permute-start | bytes 1572872 | tf_op jit(solution)/shard_map/ppermute | solution.py:380
  33.5 7.6 %collective-permute-start.13 = (f32[3,8,512]{2,1,0:T(8,128)S(1)}, f32[3,8,512]{2,1,0:T(8,128)S(1)}, u32[]{:S(2)}, u32[]{:S(2)}) collective-permute-start(f32[3,8,512]{2,1,0:T(8,128)S(1)} %get-tuple-element.78), channel_id=1, source_target_pairs={{0,4},{1,5},{2,6},{3,7},{4,0},{5,1},{6,2},{7,3},{8,12},{9,13},{10,... | collective-permute-start | bytes 147464 | tf_op jit(solution)/shard_map/ppermute | solution.py:389
  34.7 6.4 %collective-permute-start.14 = (f32[3,8,512]{2,1,0:T(8,128)S(1)}, f32[3,8,512]{2,1,0:T(8,128)S(1)}, u32[]{:S(2)}, u32[]{:S(2)}) collective-permute-start(f32[3,8,512]{2,1,0:T(8,128)S(1)} %get-tuple-element.79), channel_id=1, source_target_pairs={{0,6},{1,7},{2,4},{3,5},{4,2},{5,3},{6,0},{7,1},{8,14},{9,15},{10,... | collective-permute-start | bytes 147464 | tf_op jit(solution)/shard_map/ppermute | solution.py:389
  36.9 4.8 %collective-permute-start.12 = (f32[3,8,512]{2,1,0:T(8,128)S(1)}, f32[3,8,512]{2,1,0:T(8,128)S(1)}, u32[]{:S(2)}, u32[]{:S(2)}) collective-permute-start(f32[3,8,512]{2,1,0:T(8,128)S(1)} %get-tuple-element.76.refs_6_), channel_id=1, source_target_pairs={{0,2},{1,3},{2,0},{3,1},{4,6},{5,7},{6,4},{7,5},{8,10},{9,11},{10,... | collective-permute-start | bytes 147464 | tf_op jit(solution)/shard_map/ppermute | solution.py:389
  41.8 1.4 %collective-permute-start.17 = (f32[6,8,512]{2,1,0:T(8,128)S(1)}, f32[6,8,512]{2,1,0:T(8,128)S(1)}, u32[]{:S(2)}, u32[]{:S(2)}) collective-permute-start(f32[6,8,512]{2,1,0:T(8,128)S(1)} %shard_map.88.refs_3_), channel_id=1, source_target_pairs={{0,1},{1,0},{2,3},{3,2},{4,5},{5,4},{6,7},{7,6},{8,9},{9,8},{10,11... | collective-permute-start | bytes 294920 | tf_op jit(solution)/shard_map/ppermute | solution.py:380
  (1 other events, 1.0 us)

commit v5 on v4

--- a/solution.py
+++ b/solution.py
@@ -396,32 +396,36 @@
 
     part = lambda n: (n, half, ny)
     shape = (nz, half, ny)
-    keep, send = call(share_kernel, [(1, *shape)] * 2, (conductance[None],), 0.1)
     extra = -(-nz // half)
     state_keep, state_send, row = call(
         share_kernel,
         [(3, *shape), (3, nz + extra, half, ny), (3, nz, ny)],
         (adjoint,),
         0.3,
-        after=[keep],
-    )
-    ratio, recip, bottom_w, top_w, own, w_send, state_send = call(
+    )
+    keep, send = call(
+        share_kernel, [(1, *shape)] * 2, (conductance[None],), 0.1, after=[state_keep]
+    )
+    ratio, recip, bottom_w, top_w, own, w_send = call(
         slab_kernel,
         [cube, cube, cube, cube, part(3), (2, nz, half, ny)],
         (keep, swap(send)),
         0.5,
         scratch=[pltpu.VMEM(cube, F32)],
-        through=[state_send],
     )
     coefs = across([own] * (chips - 1))
+    state_recv = swap(state_send)
+    state, outer, inner = call(
+        gather_state_kernel,
+        [field, plane, plane],
+        (state_keep, state_recv, row),
+        0.3,
+        after=[send],
+    )
     (source,) = call(
         source_kernel, [field], (turbine_cells, yaw_bin[None], yaw_table), 1.0, after=[own]
     )
-    state_recv = swap(state_send)
-    state, outer, inner = call(
-        gather_state_kernel, [field, plane, plane], (state_keep, state_recv, row), 0.3, after=[source]
-    )
-    flow_keep, flow_recv = share(base_flow, [own])
+    flow_keep, flow_recv = share(base_flow, [outer])
     (flow,) = call(gather_kernel, [(2, *cube)], (flow_keep, flow_recv), 0.1)
     for sweep_index in range(SWEEPS):
         first, last = sweep_index == 0, sweep_index == SWEEPS - 1

time: 44.7 us -> 43.9 us (0.982)
  local copies, waits for them, and re-layouts: 2.86 us -> 1.79 us
  starting transfers between devices: 17.1 us -> 18 us
  waiting for transfers between devices: 15.5 us -> 14.9 us
    ppermute x9, waiting for transfers between devices: 10.9 us -> 9.19 us  [across(): there[j - 1] = lax.ppermute(parts[j - 1], 'gz', pairs)]
    ppermute x7, waiting for transfers between devices: 1.61 us -> 2.94 us  [swap(): return lax.ppermute(part, 'gz', cores)]
    ppermute x7, starting transfers between devices: 2.3 us -> 3.41 us  [swap(): return lax.ppermute(part, 'gz', cores)]
    unnamed x14, local copies, waits for them, and re-layouts: 2.86 us -> 1.79 us
  transfers between devices with their start and end apart: 18 -> 18, of which waited for: 10 -> 9; matrix products, arithmetic and copies ran while one was open for 0% -> 0% of each run, Pallas kernels for 12% -> 13%
where the time goes in v5:
time: 43.9 us; the launch traced here: 43.7 us
  starting transfers between devices  18 us (41%)
  waiting for transfers between devices  14.9 us (34%)
  Pallas kernels  8.85 us (20%)
  local copies, waits for them, and re-layouts  1.79 us (4%)
    ppermute x9, starting transfers between devices, across(): there[j - 1] = lax.ppermute(parts[j - 1], 'gz', pairs)  11.5 us
    ppermute x9, waiting for transfers between devices, across(): there[j - 1] = lax.ppermute(parts[j - 1], 'gz', pairs)  9.19 us
    pallas_call x17, Pallas kernels, call(): pl.pallas_call(run, out_shape=[jax.ShapeDtypeStruct(s, F32) for s in outs...  8.85 us
    ppermute x7, starting transfers between devices, swap(): return lax.ppermute(part, 'gz', cores)  3.41 us
    ppermute x2, starting transfers between devices, face(): return lax.ppermute(outer, ('gx', 'gz'), facing)  3.02 us
    ppermute x7, waiting for transfers between devices, swap(): return lax.ppermute(part, 'gz', cores)  2.94 us
    ppermute x2, waiting for transfers between devices, face(): return lax.ppermute(outer, ('gx', 'gz'), facing)  2.78 us
    unnamed x14, local copies, waits for them, and re-layouts  1.79 us
  transfers between devices with their start and end apart: 18, of which 9 were waited for; matrix products, arithmetic and copies ran while one was open for 0% of the time, Pallas kernels for 13%

profile of v5, /device:TPU:0, one launch (start us, length us, event | category | flops | bytes accessed | tf_op | source)
XLA Modules:
  0.0 43.7 jit_solution(8591286747833401689)
XLA Ops:
  0.0 1.4 %copy-done = f32[3,16,16,512]{3,2,1,0:T(8,128)S(1)} copy-done((f32[3,16,16,512]{3,2,1,0:T(8,128)S(1)}, f32[3,16,16,512]{3,2,1,0:T(8,128)}, u32[]{:S(2)}) %copy-start) | copy-done | bytes 1572888
  2.5 1.6 %collective-permute-done.refs_1_ = f32[3,18,8,512]{3,2,1,0:T(8,128)S(1)} collective-permute-done((f32[3,18,8,512]{3,2,1,0:T(8,128)S(1)}, f32[3,18,8,512]{3,2,1,0:T(8,128)S(1)}, u32[]{:S(2)}, u32[]{:S(2)}) %collective-permute-start) | collective-permute-done | bytes 884768 | tf_op jit(solution)/shard_map/ppermute | solution.py:380
  5.0 2.9 %collective-permute-start.3 = (f32[3,32,512]{2,1,0:T(8,128)S(1)}, f32[3,32,512]{2,1,0:T(8,128)S(1)}, u32[]{:S(2)}, u32[]{:S(2)}) collective-permute-start(f32[3,32,512]{2,1,0:T(8,128)S(1)} %get-tuple-element.48.refs_1_), channel_id=1, source_target_pairs={{0,2},{1,8},{2,0},{3,10},{4,6},{5,12},{6,4},{7,14},{8,1},{9,16},{1... | collective-permute-start | bytes 589832 | tf_op jit(solution)/shard_map/ppermute | solution.py:383
  8.5 3.9 %collective-permute-start.6 = (f32[3,8,512]{2,1,0:T(8,128)S(1)}, f32[3,8,512]{2,1,0:T(8,128)S(1)}, u32[]{:S(2)}, u32[]{:S(2)}) collective-permute-start(f32[3,8,512]{2,1,0:T(8,128)S(1)} %get-tuple-element.52.refs_3_.refs_0_), channel_id=1, source_target_pairs={{0,6},{1,7},{2,4},{3,5},{4,2},{5,3},{6,0},{7,1},{8,14},{9,15},{10,... | collective-permute-start | bytes 147464 | tf_op jit(solution)/shard_map/ppermute | solution.py:389
  12.3 0.6 %collective-permute-start.4 = (f32[3,8,512]{2,1,0:T(8,128)S(1)}, f32[3,8,512]{2,1,0:T(8,128)S(1)}, u32[]{:S(2)}, u32[]{:S(2)}) collective-permute-start(f32[3,8,512]{2,1,0:T(8,128)S(1)} %get-tuple-element.52.refs_3_.refs_0_), channel_id=1, source_target_pairs={{0,2},{1,3},{2,0},{3,1},{4,6},{5,7},{6,4},{7,5},{8,10},{9,11},{10,... | collective-permute-start | bytes 147464 | tf_op jit(solution)/shard_map/ppermute | solution.py:389
  13.0 1.4 %shard_map.79.refs_2_ = f32[3,32,8,512]{3,2,1,0:T(8,128)S(1)} custom-call(s32[3,100]{1,0:T(4,128)S(1)} %copy-done.4, s32[1,100]{1,0:T(1,128)S(1)} %bitcast.3, f32[3,12]{1,0:T(4,128)S(1)} %copy-done.5, f32[3,8,512]{2,1,0:T(8,128)S(1)} %get-tuple-element.52.refs_3_.refs_0_), custom_call_target="tpu_custom_call" | custom-call | bytes 3000000 | tf_op jit(solution)/shard_map/pallas_call | solution.py:26
  14.6 1.5 %shard_map.80 = (f32[3,32,8,512]{3,2,1,0:T(8,128)S(1)}, f32[6,8,512]{2,1,0:T(8,128)S(1)}, f32[2,32,512]{2,1,0:T(8,128)S(1)}, f32[2,2,32,512]{3,2,1,0:T(8,128)S(1)}) custom-call(f32[3,32,8,512]{3,2,1,0:T(8,128)S(1)} %get-tuple-element.47.refs_0_, f32[2,32,8,512]{3,2,1,0:T(8,128)S(1)} %shard_map.77.refs_1_, f32[3,32,8,512]{3,2,1,0:T(8,128)S(1)} %shard_map.79.refs_2_, ...), custom_call_target="tpu_custom_call" | custom-call | bytes 4500000 | tf_op jit(solution)/shard_map/pallas_call | solution.py:26
  16.1 1.2 %collective-permute-done.5.refs_2_ = f32[3,8,512]{2,1,0:T(8,128)S(1)} collective-permute-done((f32[3,8,512]{2,1,0:T(8,128)S(1)}, f32[3,8,512]{2,1,0:T(8,128)S(1)}, u32[]{:S(2)}, u32[]{:S(2)}) %collective-permute-start.5) | collective-permute-done | bytes 49184 | tf_op jit(solution)/shard_map/ppermute | solution.py:389
  17.6 2.1 %collective-permute-start.8 = (f32[3,8,512]{2,1,0:T(8,128)S(1)}, f32[3,8,512]{2,1,0:T(8,128)S(1)}, u32[]{:S(2)}, u32[]{:S(2)}) collective-permute-start(f32[3,8,512]{2,1,0:T(8,128)S(1)} %get-tuple-element.62), channel_id=1, source_target_pairs={{0,4},{1,5},{2,6},{3,7},{4,0},{5,1},{6,2},{7,3},{8,12},{9,13},{10,... | collective-permute-start | bytes 147464 | tf_op jit(solution)/shard_map/ppermute | solution.py:389
  19.7 1.2 %collective-permute-start.9 = (f32[3,8,512]{2,1,0:T(8,128)S(1)}, f32[3,8,512]{2,1,0:T(8,128)S(1)}, u32[]{:S(2)}, u32[]{:S(2)}) collective-permute-start(f32[3,8,512]{2,1,0:T(8,128)S(1)} %get-tuple-element.63), channel_id=1, source_target_pairs={{0,6},{1,7},{2,4},{3,5},{4,2},{5,3},{6,0},{7,1},{8,14},{9,15},{10,... | collective-permute-start | bytes 147464 | tf_op jit(solution)/shard_map/ppermute | solution.py:389
  21.6 2.3 %collective-permute-done.8.refs_1_ = f32[3,8,512]{2,1,0:T(8,128)S(1)} collective-permute-done((f32[3,8,512]{2,1,0:T(8,128)S(1)}, f32[3,8,512]{2,1,0:T(8,128)S(1)}, u32[]{:S(2)}, u32[]{:S(2)}) %collective-permute-start.8) | collective-permute-done | bytes 49184 | tf_op jit(solution)/shard_map/ppermute | solution.py:389
  23.9 1.6 %collective-permute-done.9.refs_2_ = f32[3,8,512]{2,1,0:T(8,128)S(1)} collective-permute-done((f32[3,8,512]{2,1,0:T(8,128)S(1)}, f32[3,8,512]{2,1,0:T(8,128)S(1)}, u32[]{:S(2)}, u32[]{:S(2)}) %collective-permute-start.9) | collective-permute-done | bytes 49184 | tf_op jit(solution)/shard_map/ppermute | solution.py:389
  25.6 0.6 %shard_map.84 = (f32[3,32,8,512]{3,2,1,0:T(8,128)S(1)}, f32[3,32,512]{2,1,0:T(8,128)S(1)}, f32[3,32,512]{2,1,0:T(8,128)S(1)}) custom-call(f32[3,8,512]{2,1,0:T(8,128)S(1)} %collective-permute-done.7.refs_0_, f32[3,8,512]{2,1,0:T(8,128)S(1)} %collective-permute-done.8.refs_1_, f32[3,8,512]{2,1,0:T(8,128)S(1)} %collective-permute-done.9.refs_2_, ...), custom_call_target="tpu_custom_call" | custom-call | bytes 1200000 | tf_op jit(solution)/shard_map/pallas_call | solution.py:26
  26.3 1.6 %collective-permute-start.11 = (f32[3,32,512]{2,1,0:T(8,128)S(1)}, f32[3,32,512]{2,1,0:T(8,128)S(1)}, u32[]{:S(2)}, u32[]{:S(2)}) collective-permute-start(f32[3,32,512]{2,1,0:T(8,128)S(1)} %get-tuple-element.72), channel_id=1, source_target_pairs={{0,1},{1,0},{2,3},{3,2},{4,5},{5,4},{6,7},{7,6},{8,9},{9,8},{10,11... | collective-permute-start | bytes 589832 | tf_op jit(solution)/shard_map/ppermute | solution.py:380
  27.9 1.3 %shard_map.85 = (f32[3,32,8,512]{3,2,1,0:T(8,128)S(1)}, f32[6,8,512]{2,1,0:T(8,128)S(1)}) custom-call(f32[3,32,8,512]{3,2,1,0:T(8,128)S(1)} %get-tuple-element.69.refs_0_, f32[2,32,8,512]{3,2,1,0:T(8,128)S(1)} %shard_map.77.refs_1_, f32[3,32,8,512]{3,2,1,0:T(8,128)S(1)} %shard_map.79.refs_2_, f32[32,8,512]{2,1,0:T(8,128)S(1)} %get-tuple-element.53.refs_3_.refs_4_, ...), custom_call_target="tpu_custom_call" | custom-call | bytes 4500000 | tf_op jit(solution)/shard_map/pallas_call | solution.py:26
  29.2 2.8 %collective-permute-done.10.refs_1_ = f32[3,32,512]{2,1,0:T(8,128)S(1)} collective-permute-done((f32[3,32,512]{2,1,0:T(8,128)S(1)}, f32[3,32,512]{2,1,0:T(8,128)S(1)}, u32[]{:S(2)}, u32[]{:S(2)}) %collective-permute-start.10) | collective-permute-done | bytes 196640 | tf_op jit(solution)/shard_map/ppermute | solution.py:383
  32.1 0.6 %shard_map.87 = (f32[3,32,8,512]{3,2,1,0:T(8,128)S(1)}, f32[3,16,8,512]{3,2,1,0:T(8,128)S(1)}) custom-call(f32[3,32,8,512]{3,2,1,0:T(8,128)S(1)} %get-tuple-element.70.refs_0_, f32[3,32,512]{2,1,0:T(8,128)S(1)} %collective-permute-done.10.refs_1_, f32[3,32,512]{2,1,0:T(8,128)S(1)} %collective-permute-done.11.refs_2_, ...), custom_call_target="tpu_custom_call" | custom-call | bytes 1200000 | tf_op jit(solution)/shard_map/pallas_call | solution.py:26
  33.3 1.1 %collective-permute-start.13 = (f32[3,8,512]{2,1,0:T(8,128)S(1)}, f32[3,8,512]{2,1,0:T(8,128)S(1)}, u32[]{:S(2)}, u32[]{:S(2)}) collective-permute-start(f32[3,8,512]{2,1,0:T(8,128)S(1)} %get-tuple-element.76), channel_id=1, source_target_pairs={{0,4},{1,5},{2,6},{3,7},{4,0},{5,1},{6,2},{7,3},{8,12},{9,13},{10,... | collective-permute-start | bytes 147464 | tf_op jit(solution)/shard_map/ppermute | solution.py:389
  34.4 1.2 %collective-permute-start.14 = (f32[3,8,512]{2,1,0:T(8,128)S(1)}, f32[3,8,512]{2,1,0:T(8,128)S(1)}, u32[]{:S(2)}, u32[]{:S(2)}) collective-permute-start(f32[3,8,512]{2,1,0:T(8,128)S(1)} %get-tuple-element.77), channel_id=1, source_target_pairs={{0,6},{1,7},{2,4},{3,5},{4,2},{5,3},{6,0},{7,1},{8,14},{9,15},{10,... | collective-permute-start | bytes 147464 | tf_op jit(solution)/shard_map/ppermute | solution.py:389
  35.7 1.2 %collective-permute-start.12 = (f32[3,8,512]{2,1,0:T(8,128)S(1)}, f32[3,8,512]{2,1,0:T(8,128)S(1)}, u32[]{:S(2)}, u32[]{:S(2)}) collective-permute-start(f32[3,8,512]{2,1,0:T(8,128)S(1)} %get-tuple-element.74.refs_6_), channel_id=1, source_target_pairs={{0,2},{1,3},{2,0},{3,1},{4,6},{5,7},{6,4},{7,5},{8,10},{9,11},{10,... | collective-permute-start | bytes 147464 | tf_op jit(solution)/shard_map/ppermute | solution.py:389
  36.8 2.0 %collective-permute-done.13.refs_1_ = f32[3,8,512]{2,1,0:T(8,128)S(1)} collective-permute-done((f32[3,8,512]{2,1,0:T(8,128)S(1)}, f32[3,8,512]{2,1,0:T(8,128)S(1)}, u32[]{:S(2)}, u32[]{:S(2)}) %collective-permute-start.13) | collective-permute-done | bytes 49184 | tf_op jit(solution)/shard_map/ppermute | solution.py:389
  38.8 1.7 %collective-permute-done.14.refs_2_ = f32[3,8,512]{2,1,0:T(8,128)S(1)} collective-permute-done((f32[3,8,512]{2,1,0:T(8,128)S(1)}, f32[3,8,512]{2,1,0:T(8,128)S(1)}, u32[]{:S(2)}, u32[]{:S(2)}) %collective-permute-start.14) | collective-permute-done | bytes 49184 | tf_op jit(solution)/shard_map/ppermute | solution.py:389
  41.0 1.3 %collective-permute-done.17.refs_6_ = f32[6,8,512]{2,1,0:T(8,128)S(1)} collective-permute-done((f32[6,8,512]{2,1,0:T(8,128)S(1)}, f32[6,8,512]{2,1,0:T(8,128)S(1)}, u32[]{:S(2)}, u32[]{:S(2)}) %collective-permute-start.17) | collective-permute-done | bytes 98336 | tf_op jit(solution)/shard_map/ppermute | solution.py:380
  42.3 1.4 %shard_map.89 = f32[3,16,16,512]{3,2,1,0:T(8,128)} custom-call(f32[3,32,8,512]{3,2,1,0:T(8,128)S(1)} %get-tuple-element.75.refs_0_, f32[32,8,512]{2,1,0:T(8,128)S(1)} %get-tuple-element.55.refs_5_.refs_8_.refs_1_, f32[32,8,512]{2,1,0:T(8,128)S(1)} %get-tuple-element.56.refs_6_.refs_9_.refs_2_, f32[6,8,512]{2,1,0:T(8,128)S(1)} %shard_map.88.refs_3_, ...), custom_call_target="tpu_custom_call" | custom-call | bytes 3000000 | tf_op jit(solution)/shard_map/pallas_call | solution.py:26
  (43 shorter events, 4.8 us)
Async XLA Ops:
  0.0 1.4 %copy-start = (f32[3,16,16,512]{3,2,1,0:T(8,128)S(1)}, f32[3,16,16,512]{3,2,1,0:T(8,128)}, u32[]{:S(2)}) copy-start(f32[3,16,16,512]{3,2,1,0:T(8,128)} %refs_0_.3) | copy-start | bytes 4718596
  1.6 2.6 %collective-permute-start = (f32[3,18,8,512]{3,2,1,0:T(8,128)S(1)}, f32[3,18,8,512]{3,2,1,0:T(8,128)S(1)}, u32[]{:S(2)}, u32[]{:S(2)}) collective-permute-start(f32[3,18,8,512]{3,2,1,0:T(8,128)S(1)} %get-tuple-element.44), channel_id=1, source_target_pairs={{0,1},{1,0},{2,3},{3,2},{4,5},{5,4},{6,7},{7,6},{8,9},{9,8},{10,11... | collective-permute-start | bytes 2654216 | tf_op jit(solution)/shard_map/ppermute | solution.py:380
  2.5 1.9 %copy-start.1 = (f32[2,16,16,512]{3,2,1,0:T(8,128)S(1)}, f32[2,16,16,512]{3,2,1,0:T(8,128)}, u32[]{:S(2)}) copy-start(f32[2,16,16,512]{3,2,1,0:T(8,128)} %refs_0_.4) | copy-start | bytes 3145732
  4.1 8.8 %copy-start.4 = (s32[3,100]{1,0:T(4,128)S(1)}, s32[3,100]{1,0:T(4,128)}, u32[]{:S(2)}) copy-start(s32[3,100]{1,0:T(4,128)} %refs_0_.5) | copy-start | bytes 3604
  4.1 8.8 %copy-start.5 = (f32[3,12]{1,0:T(4,128)S(1)}, f32[3,12]{1,0:T(4,128)}, u32[]{:S(2)}) copy-start(f32[3,12]{1,0:T(4,128)} %refs_2_.1) | copy-start | bytes 436
  4.1 8.8 %copy-start.6 = (s32[100]{0:T(128)S(1)}, s32[100]{0:T(128)}, u32[]{:S(2)}) copy-start(s32[100]{0:T(128)} %param.12) | copy-start | bytes 1204
  4.5 10.0 %collective-permute-start.1 = (f32[2,16,8,512]{3,2,1,0:T(8,128)S(1)}, f32[2,16,8,512]{3,2,1,0:T(8,128)S(1)}, u32[]{:S(2)}, u32[]{:S(2)}) collective-permute-start(f32[2,16,8,512]{3,2,1,0:T(8,128)S(1)} %get-tuple-element.50), channel_id=1, source_target_pairs={{0,1},{1,0},{2,3},{3,2},{4,5},{5,4},{6,7},{7,6},{8,9},{9,8},{10,11... | collective-permute-start | bytes 1572872 | tf_op jit(solution)/shard_map/ppermute | solution.py:380
  4.9 3.1 %collective-permute-start.2 = (f32[1,16,8,512]{3,2,1,0:T(8,128)S(1)}, f32[1,16,8,512]{3,2,1,0:T(8,128)S(1)}, u32[]{:S(2)}, u32[]{:S(2)}) collective-permute-start(f32[1,16,8,512]{3,2,1,0:T(8,128)S(1)} %get-tuple-element.46.refs_3_), channel_id=1, source_target_pairs={{0,1},{1,0},{2,3},{3,2},{4,5},{5,4},{6,7},{7,6},{8,9},{9,8},{10,11... | collective-permute-start | bytes 786440 | tf_op jit(solution)/shard_map/ppermute | solution.py:380
  5.0 12.4 %collective-permute-start.3 = (f32[3,32,512]{2,1,0:T(8,128)S(1)}, f32[3,32,512]{2,1,0:T(8,128)S(1)}, u32[]{:S(2)}, u32[]{:S(2)}) collective-permute-start(f32[3,32,512]{2,1,0:T(8,128)S(1)} %get-tuple-element.48.refs_1_), channel_id=1, source_target_pairs={{0,2},{1,8},{2,0},{3,10},{4,6},{5,12},{6,4},{7,14},{8,1},{9,16},{1... | collective-permute-start | bytes 589832 | tf_op jit(solution)/shard_map/ppermute | solution.py:383
  8.5 7.6 %collective-permute-start.6 = (f32[3,8,512]{2,1,0:T(8,128)S(1)}, f32[3,8,512]{2,1,0:T(8,128)S(1)}, u32[]{:S(2)}, u32[]{:S(2)}) collective-permute-start(f32[3,8,512]{2,1,0:T(8,128)S(1)} %get-tuple-element.52.refs_3_.refs_0_), channel_id=1, source_target_pairs={{0,6},{1,7},{2,4},{3,5},{4,2},{5,3},{6,0},{7,1},{8,14},{9,15},{10,... | collective-permute-start | bytes 147464 | tf_op jit(solution)/shard_map/ppermute | solution.py:389
  12.3 5.0 %collective-permute-start.5 = (f32[3,8,512]{2,1,0:T(8,128)S(1)}, f32[3,8,512]{2,1,0:T(8,128)S(1)}, u32[]{:S(2)}, u32[]{:S(2)}) collective-permute-start(f32[3,8,512]{2,1,0:T(8,128)S(1)} %get-tuple-element.52.refs_3_.refs_0_), channel_id=1, source_target_pairs={{0,4},{1,5},{2,6},{3,7},{4,0},{5,1},{6,2},{7,3},{8,12},{9,13},{10,... | collective-permute-start | bytes 147464 | tf_op jit(solution)/shard_map/ppermute | solution.py:389
  12.3 5.0 %collective-permute-start.4 = (f32[3,8,512]{2,1,0:T(8,128)S(1)}, f32[3,8,512]{2,1,0:T(8,128)S(1)}, u32[]{:S(2)}, u32[]{:S(2)}) collective-permute-start(f32[3,8,512]{2,1,0:T(8,128)S(1)} %get-tuple-element.52.refs_3_.refs_0_), channel_id=1, source_target_pairs={{0,2},{1,3},{2,0},{3,1},{4,6},{5,7},{6,4},{7,5},{8,10},{9,11},{10,... | collective-permute-start | bytes 147464 | tf_op jit(solution)/shard_map/ppermute | solution.py:389
  14.5 2.8 %copy-start.3 = (s32[16,512]{1,0:T(8,128)S(1)}, s32[16,512]{1,0:T(8,128)}, u32[]{:S(2)}) copy-start(s32[16,512]{1,0:T(8,128)} %refs_4_.1) | copy-start | bytes 98308
  17.6 6.3 %collective-permute-start.8 = (f32[3,8,512]{2,1,0:T(8,128)S(1)}, f32[3,8,512]{2,1,0:T(8,128)S(1)}, u32[]{:S(2)}, u32[]{:S(2)}) collective-permute-start(f32[3,8,512]{2,1,0:T(8,128)S(1)} %get-tuple-element.62), channel_id=1, source_target_pairs={{0,4},{1,5},{2,6},{3,7},{4,0},{5,1},{6,2},{7,3},{8,12},{9,13},{10,... | collective-permute-start | bytes 147464 | tf_op jit(solution)/shard_map/ppermute | solution.py:389
  19.7 5.9 %collective-permute-start.9 = (f32[3,8,512]{2,1,0:T(8,128)S(1)}, f32[3,8,512]{2,1,0:T(8,128)S(1)}, u32[]{:S(2)}, u32[]{:S(2)}) collective-permute-start(f32[3,8,512]{2,1,0:T(8,128)S(1)} %get-tuple-element.63), channel_id=1, source_target_pairs={{0,6},{1,7},{2,4},{3,5},{4,2},{5,3},{6,0},{7,1},{8,14},{9,15},{10,... | collective-permute-start | bytes 147464 | tf_op jit(solution)/shard_map/ppermute | solution.py:389
  20.9 4.7 %collective-permute-start.7 = (f32[3,8,512]{2,1,0:T(8,128)S(1)}, f32[3,8,512]{2,1,0:T(8,128)S(1)}, u32[]{:S(2)}, u32[]{:S(2)}) collective-permute-start(f32[3,8,512]{2,1,0:T(8,128)S(1)} %get-tuple-element.61.refs_6_), channel_id=1, source_target_pairs={{0,2},{1,3},{2,0},{3,1},{4,6},{5,7},{6,4},{7,5},{8,10},{9,11},{10,... | collective-permute-start | bytes 147464 | tf_op jit(solution)/shard_map/ppermute | solution.py:389
  26.2 5.7 %collective-permute-start.10 = (f32[3,32,512]{2,1,0:T(8,128)S(1)}, f32[3,32,512]{2,1,0:T(8,128)S(1)}, u32[]{:S(2)}, u32[]{:S(2)}) collective-permute-start(f32[3,32,512]{2,1,0:T(8,128)S(1)} %get-tuple-element.71), channel_id=1, source_target_pairs={{0,2},{1,8},{2,0},{3,10},{4,6},{5,12},{6,4},{7,14},{8,1},{9,16},{1... | collective-permute-start | bytes 589832 | tf_op jit(solution)/shard_map/ppermute | solution.py:383
  26.3 5.7 %collective-permute-start.11 = (f32[3,32,512]{2,1,0:T(8,128)S(1)}, f32[3,32,512]{2,1,0:T(8,128)S(1)}, u32[]{:S(2)}, u32[]{:S(2)}) collective-permute-start(f32[3,32,512]{2,1,0:T(8,128)S(1)} %get-tuple-element.72), channel_id=1, source_target_pairs={{0,1},{1,0},{2,3},{3,2},{4,5},{5,4},{6,7},{7,6},{8,9},{9,8},{10,11... | collective-permute-start | bytes 589832 | tf_op jit(solution)/shard_map/ppermute | solution.py:380
  32.7 9.6 %collective-permute-start.15 = (f32[3,16,8,512]{3,2,1,0:T(8,128)S(1)}, f32[3,16,8,512]{3,2,1,0:T(8,128)S(1)}, u32[]{:S(2)}, u32[]{:S(2)}) collective-permute-start(f32[3,16,8,512]{3,2,1,0:T(8,128)S(1)} %get-tuple-element.79), channel_id=1, source_target_pairs={{0,1},{1,0},{2,3},{3,2},{4,5},{5,4},{6,7},{7,6},{8,9},{9,8},{10,11... | collective-permute-start | bytes 2359304 | tf_op jit(solution)/shard_map/ppermute | solution.py:380
  33.3 7.8 %collective-permute-start.16 = (f32[2,16,8,512]{3,2,1,0:T(8,128)S(1)}, f32[2,16,8,512]{3,2,1,0:T(8,128)S(1)}, u32[]{:S(2)}, u32[]{:S(2)}) collective-permute-start(f32[2,16,8,512]{3,2,1,0:T(8,128)S(1)} %get-tuple-element.80), channel_id=1, source_target_pairs={{0,1},{1,0},{2,3},{3,2},{4,5},{5,4},{6,7},{7,6},{8,9},{9,8},{10,11... | collective-permute-start | bytes 1572872 | tf_op jit(solution)/shard_map/ppermute | solution.py:380
  33.3 5.5 %collective-permute-start.13 = (f32[3,8,512]{2,1,0:T(8,128)S(1)}, f32[3,8,512]{2,1,0:T(8,128)S(1)}, u32[]{:S(2)}, u32[]{:S(2)}) collective-permute-start(f32[3,8,512]{2,1,0:T(8,128)S(1)} %get-tuple-element.76), channel_id=1, source_target_pairs={{0,4},{1,5},{2,6},{3,7},{4,0},{5,1},{6,2},{7,3},{8,12},{9,13},{10,... | collective-permute-start | bytes 147464 | tf_op jit(solution)/shard_map/ppermute | solution.py:389
  34.4 6.2 %collective-permute-start.14 = (f32[3,8,512]{2,1,0:T(8,128)S(1)}, f32[3,8,512]{2,1,0:T(8,128)S(1)}, u32[]{:S(2)}, u32[]{:S(2)}) collective-permute-start(f32[3,8,512]{2,1,0:T(8,128)S(1)} %get-tuple-element.77), channel_id=1, source_target_pairs={{0,6},{1,7},{2,4},{3,5},{4,2},{5,3},{6,0},{7,1},{8,14},{9,15},{10,... | collective-permute-start | bytes 147464 | tf_op jit(solution)/shard_map/ppermute | solution.py:389
  35.7 5.2 %collective-permute-start.12 = (f32[3,8,512]{2,1,0:T(8,128)S(1)}, f32[3,8,512]{2,1,0:T(8,128)S(1)}, u32[]{:S(2)}, u32[]{:S(2)}) collective-permute-start(f32[3,8,512]{2,1,0:T(8,128)S(1)} %get-tuple-element.74.refs_6_), channel_id=1, source_target_pairs={{0,2},{1,3},{2,0},{3,1},{4,6},{5,7},{6,4},{7,5},{8,10},{9,11},{10,... | collective-permute-start | bytes 147464 | tf_op jit(solution)/shard_map/ppermute | solution.py:389
  41.0 1.4 %collective-permute-start.17 = (f32[6,8,512]{2,1,0:T(8,128)S(1)}, f32[6,8,512]{2,1,0:T(8,128)S(1)}, u32[]{:S(2)}, u32[]{:S(2)}) collective-permute-start(f32[6,8,512]{2,1,0:T(8,128)S(1)} %shard_map.88.refs_3_), channel_id=1, source_target_pairs={{0,1},{1,0},{2,3},{3,2},{4,5},{5,4},{6,7},{7,6},{8,9},{9,8},{10,11... | collective-permute-start | bytes 294920 | tf_op jit(solution)/shard_map/ppermute | solution.py:380
  (1 other events, 1.0 us)

commit v6 on v5

--- a/solution.py
+++ b/solution.py
@@ -59,6 +59,9 @@
                 at = nz + k // half, slice(k % half, k % half + 1)
                 inner_refs[0][c, k : k + 1, :] = jnp.where(core == 0, behind, before)
                 send_ref[c, at[0], at[1], :] = jnp.where(core == 0, before, behind)
+                first, last = whole_ref[c, k, 0:1, :], whole_ref[c, k, nx - 1 : nx, :]
+                inner_refs[1][c, k : k + 1, :] = jnp.where(core == 0, first, last)
+                inner_refs[2][c, k : k + 1, :] = jnp.where(core == 0, last, first)
 
 
 def store_edges(core, c, k, first, last, outer_ref, inner_ref):
@@ -75,7 +78,15 @@
             out_ref[c, (1 - core) * nz + k] = recv_ref[c, k]
 
 
-def gather_state_kernel(keep_ref, recv_ref, row_ref, out_ref, outer_ref, inner_ref):
+def outer_kernel(keep_ref, recv_ref, outer_ref):
+    parts, nz, _ = keep_ref.shape
+    _, core = chip_and_core()
+    for c in range(parts):
+        outer_ref[c, pl.ds(pl.multiple_of(core * nz, nz), nz), :] = keep_ref[c]
+        outer_ref[c, pl.ds(pl.multiple_of((1 - core) * nz, nz), nz), :] = recv_ref[c]
+
+
+def gather_state_kernel(keep_ref, recv_ref, row_ref, out_ref, inner_ref):
     parts, nz, nx, _ = keep_ref.shape
     gather_kernel(keep_ref, recv_ref, out_ref)
     _, core = chip_and_core()
@@ -84,9 +95,6 @@
         for i in range(nz // nx):
             at = pl.ds(pl.multiple_of((1 - core) * nz + i * nx, nx), nx)
             inner_ref[c, at, :] = recv_ref[c, nz + i]
-        for k in range(2 * nz):
-            first, last = out_ref[c, k, 0:1, :], out_ref[c, k, nx - 1 : nx, :]
-            outer_ref[c, k : k + 1, :] = jnp.where(core == 0, first, last)
 
 
 def source_kernel(cells_ref, bin_ref, table_ref, source_ref):
@@ -382,9 +390,9 @@
     def face(outer):
         return lax.ppermute(outer, ("gx", "gz"), facing)
 
-    def across(parts):
+    def across(parts, far=True):
         there = [None] * len(parts)
-        for j in range(len(parts), 0, -1):
+        for j in sorted(range(1, len(parts) + 1), reverse=far):
             pairs = [(i, i ^ (2 * j)) for i in range(slabs)]
             there[j - 1] = lax.ppermute(parts[j - 1], "gz", pairs)
         return there
@@ -397,14 +405,18 @@
     part = lambda n: (n, half, ny)
     shape = (nz, half, ny)
     extra = -(-nz // half)
-    state_keep, state_send, row = call(
+    state_keep, state_send, row, edge_keep, edge_send = call(
         share_kernel,
-        [(3, *shape), (3, nz + extra, half, ny), (3, nz, ny)],
+        [(3, *shape), (3, nz + extra, half, ny)] + [(3, nz, ny)] * 3,
         (adjoint,),
         0.3,
     )
     keep, send = call(
         share_kernel, [(1, *shape)] * 2, (conductance[None],), 0.1, after=[state_keep]
+    )
+    outer, state_send = call(
+        outer_kernel, [plane], (edge_keep, swap(edge_send)), 0.1,
+        after=[send], through=[state_send],
     )
     ratio, recip, bottom_w, top_w, own, w_send = call(
         slab_kernel,
@@ -413,14 +425,10 @@
         0.5,
         scratch=[pltpu.VMEM(cube, F32)],
     )
-    coefs = across([own] * (chips - 1))
+    coefs = across([own] * (chips - 1), False)
     state_recv = swap(state_send)
-    state, outer, inner = call(
-        gather_state_kernel,
-        [field, plane, plane],
-        (state_keep, state_recv, row),
-        0.3,
-        after=[send],
+    state, inner = call(
+        gather_state_kernel, [field, plane], (state_keep, state_recv, row), 0.3
     )
     (source,) = call(
         source_kernel, [field], (turbine_cells, yaw_bin[None], yaw_table), 1.0, after=[own]

time: 43.9 us -> 43.8 us (level)
  starting transfers between devices: 18 us -> 19.1 us
  waiting for transfers between devices: 14.9 us -> 13.8 us
    ppermute x7 -> x8, waiting for transfers between devices: 2.94 us -> 1.85 us  [swap(): return lax.ppermute(part, 'gz', cores)]
    ppermute x9, starting transfers between devices: 11.5 us -> 12.5 us  [across(): there[j - 1] = lax.ppermute(parts[j - 1], 'gz', pairs)]
    ppermute x7 -> x8, starting transfers between devices: 3.41 us -> 3.78 us  [swap(): return lax.ppermute(part, 'gz', cores)]
    pallas_call x17 -> x18, Pallas kernels: 8.85 us -> 8.83 us  [call(): pl.pallas_call(run, out_shape=[jax.ShapeDtypeStruct(s, F32) for s in outs...]
  transfers between devices with their start and end apart: 18 -> 19, of which waited for: 9 -> 9; matrix products, arithmetic and copies ran while one was open for 0% -> 0% of each run, Pallas kernels for 13% -> 13%
where the time goes in v6:
time: 43.8 us; the launch traced here: 43.6 us
  starting transfers between devices  19.1 us (44%)
  waiting for transfers between devices  13.8 us (32%)
  Pallas kernels  8.83 us (20%)
  local copies, waits for them, and re-layouts  1.75 us (4%)
    ppermute x9, starting transfers between devices, across(): there[j - 1] = lax.ppermute(parts[j - 1], 'gz', pairs)  12.5 us
    ppermute x9, waiting for transfers between devices, across(): there[j - 1] = lax.ppermute(parts[j - 1], 'gz', pairs)  9.09 us
    pallas_call x18, Pallas kernels, call(): pl.pallas_call(run, out_shape=[jax.ShapeDtypeStruct(s, F32) for s in outs...  8.83 us
    ppermute x8, starting transfers between devices, swap(): return lax.ppermute(part, 'gz', cores)  3.78 us
    ppermute x2, waiting for transfers between devices, face(): return lax.ppermute(outer, ('gx', 'gz'), facing)  2.81 us
    ppermute x2, starting transfers between devices, face(): return lax.ppermute(outer, ('gx', 'gz'), facing)  2.79 us
    ppermute x8, waiting for transfers between devices, swap(): return lax.ppermute(part, 'gz', cores)  1.85 us
    unnamed x14, local copies, waits for them, and re-layouts  1.75 us
  transfers between devices with their start and end apart: 19, of which 9 were waited for; matrix products, arithmetic and copies ran while one was open for 0% of the time, Pallas kernels for 13%

profile of v6, /device:TPU:0, one launch (start us, length us, event | category | flops | bytes accessed | tf_op | source)
XLA Modules:
  0.0 43.6 jit_solution(17979150963541001453)
XLA Ops:
  0.0 1.4 %copy-done = f32[3,16,16,512]{3,2,1,0:T(8,128)S(1)} copy-done((f32[3,16,16,512]{3,2,1,0:T(8,128)S(1)}, f32[3,16,16,512]{3,2,1,0:T(8,128)}, u32[]{:S(2)}) %copy-start) | copy-done | bytes 1572888
  2.5 0.6 %collective-permute-done.refs_1_ = f32[3,16,512]{2,1,0:T(8,128)S(1)} collective-permute-done((f32[3,16,512]{2,1,0:T(8,128)S(1)}, f32[3,16,512]{2,1,0:T(8,128)S(1)}, u32[]{:S(2)}, u32[]{:S(2)}) %collective-permute-start) | collective-permute-done | bytes 98336 | tf_op jit(solution)/shard_map/ppermute | solution.py:388
  4.2 2.7 %collective-permute-start.4 = (f32[3,32,512]{2,1,0:T(8,128)S(1)}, f32[3,32,512]{2,1,0:T(8,128)S(1)}, u32[]{:S(2)}, u32[]{:S(2)}) collective-permute-start(f32[3,32,512]{2,1,0:T(8,128)S(1)} %get-tuple-element.54.refs_1_), channel_id=1, source_target_pairs={{0,2},{1,8},{2,0},{3,10},{4,6},{5,12},{6,4},{7,14},{8,1},{9,16},{1... | collective-permute-start | bytes 589832 | tf_op jit(solution)/shard_map/ppermute | solution.py:391
  7.4 4.8 %collective-permute-start.7 = (f32[3,8,512]{2,1,0:T(8,128)S(1)}, f32[3,8,512]{2,1,0:T(8,128)S(1)}, u32[]{:S(2)}, u32[]{:S(2)}) collective-permute-start(f32[3,8,512]{2,1,0:T(8,128)S(1)} %get-tuple-element.58.refs_3_.refs_0_), channel_id=1, source_target_pairs={{0,6},{1,7},{2,4},{3,5},{4,2},{5,3},{6,0},{7,1},{8,14},{9,15},{10,... | collective-permute-start | bytes 147464 | tf_op jit(solution)/shard_map/ppermute | solution.py:397
  12.3 0.6 %collective-permute-start.5 = (f32[3,8,512]{2,1,0:T(8,128)S(1)}, f32[3,8,512]{2,1,0:T(8,128)S(1)}, u32[]{:S(2)}, u32[]{:S(2)}) collective-permute-start(f32[3,8,512]{2,1,0:T(8,128)S(1)} %get-tuple-element.58.refs_3_.refs_0_), channel_id=1, source_target_pairs={{0,2},{1,3},{2,0},{3,1},{4,6},{5,7},{6,4},{7,5},{8,10},{9,11},{10,... | collective-permute-start | bytes 147464 | tf_op jit(solution)/shard_map/ppermute | solution.py:397
  12.9 1.4 %shard_map.80.refs_2_ = f32[3,32,8,512]{3,2,1,0:T(8,128)S(1)} custom-call(s32[3,100]{1,0:T(4,128)S(1)} %copy-done.4, s32[1,100]{1,0:T(1,128)S(1)} %bitcast.3, f32[3,12]{1,0:T(4,128)S(1)} %copy-done.5, f32[3,8,512]{2,1,0:T(8,128)S(1)} %get-tuple-element.58.refs_3_.refs_0_), custom_call_target="tpu_custom_call" | custom-call | bytes 3000000 | tf_op jit(solution)/shard_map/pallas_call | solution.py:26
  14.6 1.5 %shard_map.81 = (f32[3,32,8,512]{3,2,1,0:T(8,128)S(1)}, f32[6,8,512]{2,1,0:T(8,128)S(1)}, f32[2,32,512]{2,1,0:T(8,128)S(1)}, f32[2,2,32,512]{3,2,1,0:T(8,128)S(1)}) custom-call(f32[3,32,8,512]{3,2,1,0:T(8,128)S(1)} %get-tuple-element.53.refs_0_, f32[2,32,8,512]{3,2,1,0:T(8,128)S(1)} %shard_map.78.refs_1_, f32[3,32,8,512]{3,2,1,0:T(8,128)S(1)} %shard_map.80.refs_2_, ...), custom_call_target="tpu_custom_call" | custom-call | bytes 4500000 | tf_op jit(solution)/shard_map/pallas_call | solution.py:26
  16.2 1.1 %collective-permute-done.6.refs_2_ = f32[3,8,512]{2,1,0:T(8,128)S(1)} collective-permute-done((f32[3,8,512]{2,1,0:T(8,128)S(1)}, f32[3,8,512]{2,1,0:T(8,128)S(1)}, u32[]{:S(2)}, u32[]{:S(2)}) %collective-permute-start.6) | collective-permute-done | bytes 49184 | tf_op jit(solution)/shard_map/ppermute | solution.py:397
  17.5 2.1 %collective-permute-start.9 = (f32[3,8,512]{2,1,0:T(8,128)S(1)}, f32[3,8,512]{2,1,0:T(8,128)S(1)}, u32[]{:S(2)}, u32[]{:S(2)}) collective-permute-start(f32[3,8,512]{2,1,0:T(8,128)S(1)} %get-tuple-element.68), channel_id=1, source_target_pairs={{0,4},{1,5},{2,6},{3,7},{4,0},{5,1},{6,2},{7,3},{8,12},{9,13},{10,... | collective-permute-start | bytes 147464 | tf_op jit(solution)/shard_map/ppermute | solution.py:397
  19.6 1.3 %collective-permute-start.10 = (f32[3,8,512]{2,1,0:T(8,128)S(1)}, f32[3,8,512]{2,1,0:T(8,128)S(1)}, u32[]{:S(2)}, u32[]{:S(2)}) collective-permute-start(f32[3,8,512]{2,1,0:T(8,128)S(1)} %get-tuple-element.69), channel_id=1, source_target_pairs={{0,6},{1,7},{2,4},{3,5},{4,2},{5,3},{6,0},{7,1},{8,14},{9,15},{10,... | collective-permute-start | bytes 147464 | tf_op jit(solution)/shard_map/ppermute | solution.py:397
  21.6 2.4 %collective-permute-done.9.refs_1_ = f32[3,8,512]{2,1,0:T(8,128)S(1)} collective-permute-done((f32[3,8,512]{2,1,0:T(8,128)S(1)}, f32[3,8,512]{2,1,0:T(8,128)S(1)}, u32[]{:S(2)}, u32[]{:S(2)}) %collective-permute-start.9) | collective-permute-done | bytes 49184 | tf_op jit(solution)/shard_map/ppermute | solution.py:397
  24.0 1.5 %collective-permute-done.10.refs_2_ = f32[3,8,512]{2,1,0:T(8,128)S(1)} collective-permute-done((f32[3,8,512]{2,1,0:T(8,128)S(1)}, f32[3,8,512]{2,1,0:T(8,128)S(1)}, u32[]{:S(2)}, u32[]{:S(2)}) %collective-permute-start.10) | collective-permute-done | bytes 49184 | tf_op jit(solution)/shard_map/ppermute | solution.py:397
  25.5 0.6 %shard_map.85 = (f32[3,32,8,512]{3,2,1,0:T(8,128)S(1)}, f32[3,32,512]{2,1,0:T(8,128)S(1)}, f32[3,32,512]{2,1,0:T(8,128)S(1)}) custom-call(f32[3,8,512]{2,1,0:T(8,128)S(1)} %collective-permute-done.8.refs_0_, f32[3,8,512]{2,1,0:T(8,128)S(1)} %collective-permute-done.9.refs_1_, f32[3,8,512]{2,1,0:T(8,128)S(1)} %collective-permute-done.10.refs_2_, ...), custom_call_target="tpu_custom_call" | custom-call | bytes 1200000 | tf_op jit(solution)/shard_map/pallas_call | solution.py:26
  26.2 1.6 %collective-permute-start.12 = (f32[3,32,512]{2,1,0:T(8,128)S(1)}, f32[3,32,512]{2,1,0:T(8,128)S(1)}, u32[]{:S(2)}, u32[]{:S(2)}) collective-permute-start(f32[3,32,512]{2,1,0:T(8,128)S(1)} %get-tuple-element.78), channel_id=1, source_target_pairs={{0,1},{1,0},{2,3},{3,2},{4,5},{5,4},{6,7},{7,6},{8,9},{9,8},{10,11... | collective-permute-start | bytes 589832 | tf_op jit(solution)/shard_map/ppermute | solution.py:388
  27.8 1.3 %shard_map.86 = (f32[3,32,8,512]{3,2,1,0:T(8,128)S(1)}, f32[6,8,512]{2,1,0:T(8,128)S(1)}) custom-call(f32[3,32,8,512]{3,2,1,0:T(8,128)S(1)} %get-tuple-element.75.refs_0_, f32[2,32,8,512]{3,2,1,0:T(8,128)S(1)} %shard_map.78.refs_1_, f32[3,32,8,512]{3,2,1,0:T(8,128)S(1)} %shard_map.80.refs_2_, f32[32,8,512]{2,1,0:T(8,128)S(1)} %get-tuple-element.59.refs_3_.refs_4_, ...), custom_call_target="tpu_custom_call" | custom-call | bytes 4500000 | tf_op jit(solution)/shard_map/pallas_call | solution.py:26
  29.1 2.8 %collective-permute-done.11.refs_1_ = f32[3,32,512]{2,1,0:T(8,128)S(1)} collective-permute-done((f32[3,32,512]{2,1,0:T(8,128)S(1)}, f32[3,32,512]{2,1,0:T(8,128)S(1)}, u32[]{:S(2)}, u32[]{:S(2)}) %collective-permute-start.11) | collective-permute-done | bytes 196640 | tf_op jit(solution)/shard_map/ppermute | solution.py:391
  32.0 0.6 %shard_map.88 = (f32[3,32,8,512]{3,2,1,0:T(8,128)S(1)}, f32[3,16,8,512]{3,2,1,0:T(8,128)S(1)}) custom-call(f32[3,32,8,512]{3,2,1,0:T(8,128)S(1)} %get-tuple-element.76.refs_0_, f32[3,32,512]{2,1,0:T(8,128)S(1)} %collective-permute-done.11.refs_1_, f32[3,32,512]{2,1,0:T(8,128)S(1)} %collective-permute-done.12.refs_2_, ...), custom_call_target="tpu_custom_call" | custom-call | bytes 1200000 | tf_op jit(solution)/shard_map/pallas_call | solution.py:26
  33.2 1.1 %collective-permute-start.14 = (f32[3,8,512]{2,1,0:T(8,128)S(1)}, f32[3,8,512]{2,1,0:T(8,128)S(1)}, u32[]{:S(2)}, u32[]{:S(2)}) collective-permute-start(f32[3,8,512]{2,1,0:T(8,128)S(1)} %get-tuple-element.82), channel_id=1, source_target_pairs={{0,4},{1,5},{2,6},{3,7},{4,0},{5,1},{6,2},{7,3},{8,12},{9,13},{10,... | collective-permute-start | bytes 147464 | tf_op jit(solution)/shard_map/ppermute | solution.py:397
  34.3 1.2 %collective-permute-start.15 = (f32[3,8,512]{2,1,0:T(8,128)S(1)}, f32[3,8,512]{2,1,0:T(8,128)S(1)}, u32[]{:S(2)}, u32[]{:S(2)}) collective-permute-start(f32[3,8,512]{2,1,0:T(8,128)S(1)} %get-tuple-element.83), channel_id=1, source_target_pairs={{0,6},{1,7},{2,4},{3,5},{4,2},{5,3},{6,0},{7,1},{8,14},{9,15},{10,... | collective-permute-start | bytes 147464 | tf_op jit(solution)/shard_map/ppermute | solution.py:397
  35.6 1.2 %collective-permute-start.13 = (f32[3,8,512]{2,1,0:T(8,128)S(1)}, f32[3,8,512]{2,1,0:T(8,128)S(1)}, u32[]{:S(2)}, u32[]{:S(2)}) collective-permute-start(f32[3,8,512]{2,1,0:T(8,128)S(1)} %get-tuple-element.80.refs_6_), channel_id=1, source_target_pairs={{0,2},{1,3},{2,0},{3,1},{4,6},{5,7},{6,4},{7,5},{8,10},{9,11},{10,... | collective-permute-start | bytes 147464 | tf_op jit(solution)/shard_map/ppermute | solution.py:397
  36.7 2.0 %collective-permute-done.14.refs_1_ = f32[3,8,512]{2,1,0:T(8,128)S(1)} collective-permute-done((f32[3,8,512]{2,1,0:T(8,128)S(1)}, f32[3,8,512]{2,1,0:T(8,128)S(1)}, u32[]{:S(2)}, u32[]{:S(2)}) %collective-permute-start.14) | collective-permute-done | bytes 49184 | tf_op jit(solution)/shard_map/ppermute | solution.py:397
  38.8 1.7 %collective-permute-done.15.refs_2_ = f32[3,8,512]{2,1,0:T(8,128)S(1)} collective-permute-done((f32[3,8,512]{2,1,0:T(8,128)S(1)}, f32[3,8,512]{2,1,0:T(8,128)S(1)}, u32[]{:S(2)}, u32[]{:S(2)}) %collective-permute-start.15) | collective-permute-done | bytes 49184 | tf_op jit(solution)/shard_map/ppermute | solution.py:397
  41.0 1.3 %collective-permute-done.18.refs_6_ = f32[6,8,512]{2,1,0:T(8,128)S(1)} collective-permute-done((f32[6,8,512]{2,1,0:T(8,128)S(1)}, f32[6,8,512]{2,1,0:T(8,128)S(1)}, u32[]{:S(2)}, u32[]{:S(2)}) %collective-permute-start.18) | collective-permute-done | bytes 98336 | tf_op jit(solution)/shard_map/ppermute | solution.py:388
  42.3 1.4 %shard_map.90 = f32[3,16,16,512]{3,2,1,0:T(8,128)} custom-call(f32[3,32,8,512]{3,2,1,0:T(8,128)S(1)} %get-tuple-element.81.refs_0_, f32[32,8,512]{2,1,0:T(8,128)S(1)} %get-tuple-element.61.refs_5_.refs_8_.refs_1_, f32[32,8,512]{2,1,0:T(8,128)S(1)} %get-tuple-element.62.refs_6_.refs_9_.refs_2_, f32[6,8,512]{2,1,0:T(8,128)S(1)} %shard_map.89.refs_3_, ...), custom_call_target="tpu_custom_call" | custom-call | bytes 3000000 | tf_op jit(solution)/shard_map/pallas_call | solution.py:26
  (46 shorter events, 5.1 us)
Async XLA Ops:
  1.6 1.9 %copy-start.1 = (f32[2,16,16,512]{3,2,1,0:T(8,128)S(1)}, f32[2,16,16,512]{3,2,1,0:T(8,128)}, u32[]{:S(2)}) copy-start(f32[2,16,16,512]{3,2,1,0:T(8,128)} %refs_0_.4) | copy-start | bytes 3145732
  1.6 1.5 %collective-permute-start = (f32[3,16,512]{2,1,0:T(8,128)S(1)}, f32[3,16,512]{2,1,0:T(8,128)S(1)}, u32[]{:S(2)}, u32[]{:S(2)}) collective-permute-start(f32[3,16,512]{2,1,0:T(8,128)S(1)} %get-tuple-element.48), channel_id=1, source_target_pairs={{0,1},{1,0},{2,3},{3,2},{4,5},{5,4},{6,7},{7,6},{8,9},{9,8},{10,11... | collective-permute-start | bytes 294920 | tf_op jit(solution)/shard_map/ppermute | solution.py:388
  2.5 10.4 %copy-start.4 = (s32[3,100]{1,0:T(4,128)S(1)}, s32[3,100]{1,0:T(4,128)}, u32[]{:S(2)}) copy-start(s32[3,100]{1,0:T(4,128)} %refs_0_.5) | copy-start | bytes 3604
  2.5 10.4 %copy-start.5 = (f32[3,12]{1,0:T(4,128)S(1)}, f32[3,12]{1,0:T(4,128)}, u32[]{:S(2)}) copy-start(f32[3,12]{1,0:T(4,128)} %refs_2_.1) | copy-start | bytes 436
  2.5 10.4 %copy-start.6 = (s32[100]{0:T(128)S(1)}, s32[100]{0:T(128)}, u32[]{:S(2)}) copy-start(s32[100]{0:T(128)} %param.12) | copy-start | bytes 1204
  3.1 11.3 %collective-permute-start.1 = (f32[3,18,8,512]{3,2,1,0:T(8,128)S(1)}, f32[3,18,8,512]{3,2,1,0:T(8,128)S(1)}, u32[]{:S(2)}, u32[]{:S(2)}) collective-permute-start(f32[3,18,8,512]{3,2,1,0:T(8,128)S(1)} %get-tuple-element.51), channel_id=1, source_target_pairs={{0,1},{1,0},{2,3},{3,2},{4,5},{5,4},{6,7},{7,6},{8,9},{9,8},{10,11... | collective-permute-start | bytes 2654216 | tf_op jit(solution)/shard_map/ppermute | solution.py:388
  3.6 8.6 %collective-permute-start.2 = (f32[2,16,8,512]{3,2,1,0:T(8,128)S(1)}, f32[2,16,8,512]{3,2,1,0:T(8,128)S(1)}, u32[]{:S(2)}, u32[]{:S(2)}) collective-permute-start(f32[2,16,8,512]{3,2,1,0:T(8,128)S(1)} %get-tuple-element.56), channel_id=1, source_target_pairs={{0,1},{1,0},{2,3},{3,2},{4,5},{5,4},{6,7},{7,6},{8,9},{9,8},{10,11... | collective-permute-start | bytes 1572872 | tf_op jit(solution)/shard_map/ppermute | solution.py:388
  3.8 3.1 %collective-permute-start.3 = (f32[1,16,8,512]{3,2,1,0:T(8,128)S(1)}, f32[1,16,8,512]{3,2,1,0:T(8,128)S(1)}, u32[]{:S(2)}, u32[]{:S(2)}) collective-permute-start(f32[1,16,8,512]{3,2,1,0:T(8,128)S(1)} %get-tuple-element.49.refs_2_), channel_id=1, source_target_pairs={{0,1},{1,0},{2,3},{3,2},{4,5},{5,4},{6,7},{7,6},{8,9},{9,8},{10,11... | collective-permute-start | bytes 786440 | tf_op jit(solution)/shard_map/ppermute | solution.py:388
  4.2 13.1 %collective-permute-start.4 = (f32[3,32,512]{2,1,0:T(8,128)S(1)}, f32[3,32,512]{2,1,0:T(8,128)S(1)}, u32[]{:S(2)}, u32[]{:S(2)}) collective-permute-start(f32[3,32,512]{2,1,0:T(8,128)S(1)} %get-tuple-element.54.refs_1_), channel_id=1, source_target_pairs={{0,2},{1,8},{2,0},{3,10},{4,6},{5,12},{6,4},{7,14},{8,1},{9,16},{1... | collective-permute-start | bytes 589832 | tf_op jit(solution)/shard_map/ppermute | solution.py:391
  7.4 8.7 %collective-permute-start.7 = (f32[3,8,512]{2,1,0:T(8,128)S(1)}, f32[3,8,512]{2,1,0:T(8,128)S(1)}, u32[]{:S(2)}, u32[]{:S(2)}) collective-permute-start(f32[3,8,512]{2,1,0:T(8,128)S(1)} %get-tuple-element.58.refs_3_.refs_0_), channel_id=1, source_target_pairs={{0,6},{1,7},{2,4},{3,5},{4,2},{5,3},{6,0},{7,1},{8,14},{9,15},{10,... | collective-permute-start | bytes 147464 | tf_op jit(solution)/shard_map/ppermute | solution.py:397
  12.3 5.0 %collective-permute-start.6 = (f32[3,8,512]{2,1,0:T(8,128)S(1)}, f32[3,8,512]{2,1,0:T(8,128)S(1)}, u32[]{:S(2)}, u32[]{:S(2)}) collective-permute-start(f32[3,8,512]{2,1,0:T(8,128)S(1)} %get-tuple-element.58.refs_3_.refs_0_), channel_id=1, source_target_pairs={{0,4},{1,5},{2,6},{3,7},{4,0},{5,1},{6,2},{7,3},{8,12},{9,13},{10,... | collective-permute-start | bytes 147464 | tf_op jit(solution)/shard_map/ppermute | solution.py:397
  12.3 5.0 %collective-permute-start.5 = (f32[3,8,512]{2,1,0:T(8,128)S(1)}, f32[3,8,512]{2,1,0:T(8,128)S(1)}, u32[]{:S(2)}, u32[]{:S(2)}) collective-permute-start(f32[3,8,512]{2,1,0:T(8,128)S(1)} %get-tuple-element.58.refs_3_.refs_0_), channel_id=1, source_target_pairs={{0,2},{1,3},{2,0},{3,1},{4,6},{5,7},{6,4},{7,5},{8,10},{9,11},{10,... | collective-permute-start | bytes 147464 | tf_op jit(solution)/shard_map/ppermute | solution.py:397
  14.6 2.7 %copy-start.3 = (s32[16,512]{1,0:T(8,128)S(1)}, s32[16,512]{1,0:T(8,128)}, u32[]{:S(2)}) copy-start(s32[16,512]{1,0:T(8,128)} %refs_4_.1) | copy-start | bytes 98308
  17.5 6.5 %collective-permute-start.9 = (f32[3,8,512]{2,1,0:T(8,128)S(1)}, f32[3,8,512]{2,1,0:T(8,128)S(1)}, u32[]{:S(2)}, u32[]{:S(2)}) collective-permute-start(f32[3,8,512]{2,1,0:T(8,128)S(1)} %get-tuple-element.68), channel_id=1, source_target_pairs={{0,4},{1,5},{2,6},{3,7},{4,0},{5,1},{6,2},{7,3},{8,12},{9,13},{10,... | collective-permute-start | bytes 147464 | tf_op jit(solution)/shard_map/ppermute | solution.py:397
  19.6 5.9 %collective-permute-start.10 = (f32[3,8,512]{2,1,0:T(8,128)S(1)}, f32[3,8,512]{2,1,0:T(8,128)S(1)}, u32[]{:S(2)}, u32[]{:S(2)}) collective-permute-start(f32[3,8,512]{2,1,0:T(8,128)S(1)} %get-tuple-element.69), channel_id=1, source_target_pairs={{0,6},{1,7},{2,4},{3,5},{4,2},{5,3},{6,0},{7,1},{8,14},{9,15},{10,... | collective-permute-start | bytes 147464 | tf_op jit(solution)/shard_map/ppermute | solution.py:397
  20.9 4.6 %collective-permute-start.8 = (f32[3,8,512]{2,1,0:T(8,128)S(1)}, f32[3,8,512]{2,1,0:T(8,128)S(1)}, u32[]{:S(2)}, u32[]{:S(2)}) collective-permute-start(f32[3,8,512]{2,1,0:T(8,128)S(1)} %get-tuple-element.67.refs_6_), channel_id=1, source_target_pairs={{0,2},{1,3},{2,0},{3,1},{4,6},{5,7},{6,4},{7,5},{8,10},{9,11},{10,... | collective-permute-start | bytes 147464 | tf_op jit(solution)/shard_map/ppermute | solution.py:397
  26.2 5.7 %collective-permute-start.11 = (f32[3,32,512]{2,1,0:T(8,128)S(1)}, f32[3,32,512]{2,1,0:T(8,128)S(1)}, u32[]{:S(2)}, u32[]{:S(2)}) collective-permute-start(f32[3,32,512]{2,1,0:T(8,128)S(1)} %get-tuple-element.77), channel_id=1, source_target_pairs={{0,2},{1,8},{2,0},{3,10},{4,6},{5,12},{6,4},{7,14},{8,1},{9,16},{1... | collective-permute-start | bytes 589832 | tf_op jit(solution)/shard_map/ppermute | solution.py:391
  26.2 5.7 %collective-permute-start.12 = (f32[3,32,512]{2,1,0:T(8,128)S(1)}, f32[3,32,512]{2,1,0:T(8,128)S(1)}, u32[]{:S(2)}, u32[]{:S(2)}) collective-permute-start(f32[3,32,512]{2,1,0:T(8,128)S(1)} %get-tuple-element.78), channel_id=1, source_target_pairs={{0,1},{1,0},{2,3},{3,2},{4,5},{5,4},{6,7},{7,6},{8,9},{9,8},{10,11... | collective-permute-start | bytes 589832 | tf_op jit(solution)/shard_map/ppermute | solution.py:388
  32.6 9.6 %collective-permute-start.16 = (f32[3,16,8,512]{3,2,1,0:T(8,128)S(1)}, f32[3,16,8,512]{3,2,1,0:T(8,128)S(1)}, u32[]{:S(2)}, u32[]{:S(2)}) collective-permute-start(f32[3,16,8,512]{3,2,1,0:T(8,128)S(1)} %get-tuple-element.85), channel_id=1, source_target_pairs={{0,1},{1,0},{2,3},{3,2},{4,5},{5,4},{6,7},{7,6},{8,9},{9,8},{10,11... | collective-permute-start | bytes 2359304 | tf_op jit(solution)/shard_map/ppermute | solution.py:388
  33.2 7.8 %collective-permute-start.17 = (f32[2,16,8,512]{3,2,1,0:T(8,128)S(1)}, f32[2,16,8,512]{3,2,1,0:T(8,128)S(1)}, u32[]{:S(2)}, u32[]{:S(2)}) collective-permute-start(f32[2,16,8,512]{3,2,1,0:T(8,128)S(1)} %get-tuple-element.86), channel_id=1, source_target_pairs={{0,1},{1,0},{2,3},{3,2},{4,5},{5,4},{6,7},{7,6},{8,9},{9,8},{10,11... | collective-permute-start | bytes 1572872 | tf_op jit(solution)/shard_map/ppermute | solution.py:388
  33.2 5.5 %collective-permute-start.14 = (f32[3,8,512]{2,1,0:T(8,128)S(1)}, f32[3,8,512]{2,1,0:T(8,128)S(1)}, u32[]{:S(2)}, u32[]{:S(2)}) collective-permute-start(f32[3,8,512]{2,1,0:T(8,128)S(1)} %get-tuple-element.82), channel_id=1, source_target_pairs={{0,4},{1,5},{2,6},{3,7},{4,0},{5,1},{6,2},{7,3},{8,12},{9,13},{10,... | collective-permute-start | bytes 147464 | tf_op jit(solution)/shard_map/ppermute | solution.py:397
  34.3 6.2 %collective-permute-start.15 = (f32[3,8,512]{2,1,0:T(8,128)S(1)}, f32[3,8,512]{2,1,0:T(8,128)S(1)}, u32[]{:S(2)}, u32[]{:S(2)}) collective-permute-start(f32[3,8,512]{2,1,0:T(8,128)S(1)} %get-tuple-element.83), channel_id=1, source_target_pairs={{0,6},{1,7},{2,4},{3,5},{4,2},{5,3},{6,0},{7,1},{8,14},{9,15},{10,... | collective-permute-start | bytes 147464 | tf_op jit(solution)/shard_map/ppermute | solution.py:397
  35.6 5.2 %collective-permute-start.13 = (f32[3,8,512]{2,1,0:T(8,128)S(1)}, f32[3,8,512]{2,1,0:T(8,128)S(1)}, u32[]{:S(2)}, u32[]{:S(2)}) collective-permute-start(f32[3,8,512]{2,1,0:T(8,128)S(1)} %get-tuple-element.80.refs_6_), channel_id=1, source_target_pairs={{0,2},{1,3},{2,0},{3,1},{4,6},{5,7},{6,4},{7,5},{8,10},{9,11},{10,... | collective-permute-start | bytes 147464 | tf_op jit(solution)/shard_map/ppermute | solution.py:397
  40.9 1.4 %collective-permute-start.18 = (f32[6,8,512]{2,1,0:T(8,128)S(1)}, f32[6,8,512]{2,1,0:T(8,128)S(1)}, u32[]{:S(2)}, u32[]{:S(2)}) collective-permute-start(f32[6,8,512]{2,1,0:T(8,128)S(1)} %shard_map.89.refs_3_), channel_id=1, source_target_pairs={{0,1},{1,0},{2,3},{3,2},{4,5},{5,4},{6,7},{7,6},{8,9},{9,8},{10,11... | collective-permute-start | bytes 294920 | tf_op jit(solution)/shard_map/ppermute | solution.py:388
  (2 other events, 2.4 us)

commit v7 on v6

--- a/solution.py
+++ b/solution.py
@@ -431,7 +431,7 @@
         gather_state_kernel, [field, plane], (state_keep, state_recv, row), 0.3
     )
     (source,) = call(
-        source_kernel, [field], (turbine_cells, yaw_bin[None], yaw_table), 1.0, after=[own]
+        source_kernel, [field], (turbine_cells, yaw_bin[None], yaw_table), 1.0
     )
     flow_keep, flow_recv = share(base_flow, [outer])
     (flow,) = call(gather_kernel, [(2, *cube)], (flow_keep, flow_recv), 0.1)

time: 43.8 us -> 43.8 us (level)
  no operation moved by 1% of the time
where the time goes in v7:
time: 43.8 us; the launch traced here: 43.6 us
  starting transfers between devices  19.1 us (44%)
  waiting for transfers between devices  13.8 us (32%)
  Pallas kernels  8.83 us (20%)
  local copies, waits for them, and re-layouts  1.75 us (4%)
    ppermute x9, starting transfers between devices, across(): there[j - 1] = lax.ppermute(parts[j - 1], 'gz', pairs)  12.5 us
    ppermute x9, waiting for transfers between devices, across(): there[j - 1] = lax.ppermute(parts[j - 1], 'gz', pairs)  9.09 us
    pallas_call x18, Pallas kernels, call(): pl.pallas_call(run, out_shape=[jax.ShapeDtypeStruct(s, F32) for s in outs...  8.83 us
    ppermute x8, starting transfers between devices, swap(): return lax.ppermute(part, 'gz', cores)  3.78 us
    ppermute x2, waiting for transfers between devices, face(): return lax.ppermute(outer, ('gx', 'gz'), facing)  2.81 us
    ppermute x2, starting transfers between devices, face(): return lax.ppermute(outer, ('gx', 'gz'), facing)  2.79 us
    ppermute x8, waiting for transfers between devices, swap(): return lax.ppermute(part, 'gz', cores)  1.85 us
    unnamed x14, local copies, waits for them, and re-layouts  1.75 us
  transfers between devices with their start and end apart: 19, of which 9 were waited for; matrix products, arithmetic and copies ran while one was open for 0% of the time, Pallas kernels for 13%

profile of v7, /device:TPU:0, one launch (start us, length us, event | category | flops | bytes accessed | tf_op | source)
XLA Modules:
  0.0 43.6 jit_solution(1400818607442487075)
XLA Ops:
  0.0 1.4 %copy-done = f32[3,16,16,512]{3,2,1,0:T(8,128)S(1)} copy-done((f32[3,16,16,512]{3,2,1,0:T(8,128)S(1)}, f32[3,16,16,512]{3,2,1,0:T(8,128)}, u32[]{:S(2)}) %copy-start) | copy-done | bytes 1572888
  2.5 0.6 %collective-permute-done.refs_1_ = f32[3,16,512]{2,1,0:T(8,128)S(1)} collective-permute-done((f32[3,16,512]{2,1,0:T(8,128)S(1)}, f32[3,16,512]{2,1,0:T(8,128)S(1)}, u32[]{:S(2)}, u32[]{:S(2)}) %collective-permute-start) | collective-permute-done | bytes 98336 | tf_op jit(solution)/shard_map/ppermute | solution.py:388
  4.2 2.7 %collective-permute-start.4 = (f32[3,32,512]{2,1,0:T(8,128)S(1)}, f32[3,32,512]{2,1,0:T(8,128)S(1)}, u32[]{:S(2)}, u32[]{:S(2)}) collective-permute-start(f32[3,32,512]{2,1,0:T(8,128)S(1)} %get-tuple-element.54.refs_1_), channel_id=1, source_target_pairs={{0,2},{1,8},{2,0},{3,10},{4,6},{5,12},{6,4},{7,14},{8,1},{9,16},{1... | collective-permute-start | bytes 589832 | tf_op jit(solution)/shard_map/ppermute | solution.py:391
  7.4 4.8 %collective-permute-start.7 = (f32[3,8,512]{2,1,0:T(8,128)S(1)}, f32[3,8,512]{2,1,0:T(8,128)S(1)}, u32[]{:S(2)}, u32[]{:S(2)}) collective-permute-start(f32[3,8,512]{2,1,0:T(8,128)S(1)} %get-tuple-element.65.refs_0_), channel_id=1, source_target_pairs={{0,6},{1,7},{2,4},{3,5},{4,2},{5,3},{6,0},{7,1},{8,14},{9,15},{10,... | collective-permute-start | bytes 147464 | tf_op jit(solution)/shard_map/ppermute | solution.py:397
  12.3 0.6 %collective-permute-start.5 = (f32[3,8,512]{2,1,0:T(8,128)S(1)}, f32[3,8,512]{2,1,0:T(8,128)S(1)}, u32[]{:S(2)}, u32[]{:S(2)}) collective-permute-start(f32[3,8,512]{2,1,0:T(8,128)S(1)} %get-tuple-element.65.refs_0_), channel_id=1, source_target_pairs={{0,2},{1,3},{2,0},{3,1},{4,6},{5,7},{6,4},{7,5},{8,10},{9,11},{10,... | collective-permute-start | bytes 147464 | tf_op jit(solution)/shard_map/ppermute | solution.py:397
  12.9 1.4 %shard_map.79.refs_2_ = f32[3,32,8,512]{3,2,1,0:T(8,128)S(1)} custom-call(s32[3,100]{1,0:T(4,128)S(1)} %copy-done.4, s32[1,100]{1,0:T(1,128)S(1)} %bitcast.3, f32[3,12]{1,0:T(4,128)S(1)} %copy-done.5), custom_call_target="tpu_custom_call" | custom-call | bytes 3000000 | tf_op jit(solution)/shard_map/pallas_call | solution.py:26
  14.6 1.5 %shard_map.81 = (f32[3,32,8,512]{3,2,1,0:T(8,128)S(1)}, f32[6,8,512]{2,1,0:T(8,128)S(1)}, f32[2,32,512]{2,1,0:T(8,128)S(1)}, f32[2,2,32,512]{3,2,1,0:T(8,128)S(1)}) custom-call(f32[3,32,8,512]{3,2,1,0:T(8,128)S(1)} %get-tuple-element.53.refs_0_, f32[2,32,8,512]{3,2,1,0:T(8,128)S(1)} %shard_map.78.refs_1_, f32[3,32,8,512]{3,2,1,0:T(8,128)S(1)} %shard_map.79.refs_2_, ...), custom_call_target="tpu_custom_call" | custom-call | bytes 4500000 | tf_op jit(solution)/shard_map/pallas_call | solution.py:26
  16.2 1.1 %collective-permute-done.6.refs_2_ = f32[3,8,512]{2,1,0:T(8,128)S(1)} collective-permute-done((f32[3,8,512]{2,1,0:T(8,128)S(1)}, f32[3,8,512]{2,1,0:T(8,128)S(1)}, u32[]{:S(2)}, u32[]{:S(2)}) %collective-permute-start.6) | collective-permute-done | bytes 49184 | tf_op jit(solution)/shard_map/ppermute | solution.py:397
  17.5 2.1 %collective-permute-start.9 = (f32[3,8,512]{2,1,0:T(8,128)S(1)}, f32[3,8,512]{2,1,0:T(8,128)S(1)}, u32[]{:S(2)}, u32[]{:S(2)}) collective-permute-start(f32[3,8,512]{2,1,0:T(8,128)S(1)} %get-tuple-element.68), channel_id=1, source_target_pairs={{0,4},{1,5},{2,6},{3,7},{4,0},{5,1},{6,2},{7,3},{8,12},{9,13},{10,... | collective-permute-start | bytes 147464 | tf_op jit(solution)/shard_map/ppermute | solution.py:397
  19.6 1.3 %collective-permute-start.10 = (f32[3,8,512]{2,1,0:T(8,128)S(1)}, f32[3,8,512]{2,1,0:T(8,128)S(1)}, u32[]{:S(2)}, u32[]{:S(2)}) collective-permute-start(f32[3,8,512]{2,1,0:T(8,128)S(1)} %get-tuple-element.69), channel_id=1, source_target_pairs={{0,6},{1,7},{2,4},{3,5},{4,2},{5,3},{6,0},{7,1},{8,14},{9,15},{10,... | collective-permute-start | bytes 147464 | tf_op jit(solution)/shard_map/ppermute | solution.py:397
  21.6 2.4 %collective-permute-done.9.refs_1_ = f32[3,8,512]{2,1,0:T(8,128)S(1)} collective-permute-done((f32[3,8,512]{2,1,0:T(8,128)S(1)}, f32[3,8,512]{2,1,0:T(8,128)S(1)}, u32[]{:S(2)}, u32[]{:S(2)}) %collective-permute-start.9) | collective-permute-done | bytes 49184 | tf_op jit(solution)/shard_map/ppermute | solution.py:397
  24.0 1.5 %collective-permute-done.10.refs_2_ = f32[3,8,512]{2,1,0:T(8,128)S(1)} collective-permute-done((f32[3,8,512]{2,1,0:T(8,128)S(1)}, f32[3,8,512]{2,1,0:T(8,128)S(1)}, u32[]{:S(2)}, u32[]{:S(2)}) %collective-permute-start.10) | collective-permute-done | bytes 49184 | tf_op jit(solution)/shard_map/ppermute | solution.py:397
  25.5 0.6 %shard_map.85 = (f32[3,32,8,512]{3,2,1,0:T(8,128)S(1)}, f32[3,32,512]{2,1,0:T(8,128)S(1)}, f32[3,32,512]{2,1,0:T(8,128)S(1)}) custom-call(f32[3,8,512]{2,1,0:T(8,128)S(1)} %collective-permute-done.8.refs_0_, f32[3,8,512]{2,1,0:T(8,128)S(1)} %collective-permute-done.9.refs_1_, f32[3,8,512]{2,1,0:T(8,128)S(1)} %collective-permute-done.10.refs_2_, ...), custom_call_target="tpu_custom_call" | custom-call | bytes 1200000 | tf_op jit(solution)/shard_map/pallas_call | solution.py:26
  26.2 1.6 %collective-permute-start.12 = (f32[3,32,512]{2,1,0:T(8,128)S(1)}, f32[3,32,512]{2,1,0:T(8,128)S(1)}, u32[]{:S(2)}, u32[]{:S(2)}) collective-permute-start(f32[3,32,512]{2,1,0:T(8,128)S(1)} %get-tuple-element.78), channel_id=1, source_target_pairs={{0,1},{1,0},{2,3},{3,2},{4,5},{5,4},{6,7},{7,6},{8,9},{9,8},{10,11... | collective-permute-start | bytes 589832 | tf_op jit(solution)/shard_map/ppermute | solution.py:388
  27.8 1.3 %shard_map.86 = (f32[3,32,8,512]{3,2,1,0:T(8,128)S(1)}, f32[6,8,512]{2,1,0:T(8,128)S(1)}) custom-call(f32[3,32,8,512]{3,2,1,0:T(8,128)S(1)} %get-tuple-element.75.refs_0_, f32[2,32,8,512]{3,2,1,0:T(8,128)S(1)} %shard_map.78.refs_1_, f32[3,32,8,512]{3,2,1,0:T(8,128)S(1)} %shard_map.79.refs_2_, f32[32,8,512]{2,1,0:T(8,128)S(1)} %get-tuple-element.58.refs_3_.refs_4_, ...), custom_call_target="tpu_custom_call" | custom-call | bytes 4500000 | tf_op jit(solution)/shard_map/pallas_call | solution.py:26
  29.1 2.8 %collective-permute-done.11.refs_1_ = f32[3,32,512]{2,1,0:T(8,128)S(1)} collective-permute-done((f32[3,32,512]{2,1,0:T(8,128)S(1)}, f32[3,32,512]{2,1,0:T(8,128)S(1)}, u32[]{:S(2)}, u32[]{:S(2)}) %collective-permute-start.11) | collective-permute-done | bytes 196640 | tf_op jit(solution)/shard_map/ppermute | solution.py:391
  32.0 0.6 %shard_map.88 = (f32[3,32,8,512]{3,2,1,0:T(8,128)S(1)}, f32[3,16,8,512]{3,2,1,0:T(8,128)S(1)}) custom-call(f32[3,32,8,512]{3,2,1,0:T(8,128)S(1)} %get-tuple-element.76.refs_0_, f32[3,32,512]{2,1,0:T(8,128)S(1)} %collective-permute-done.11.refs_1_, f32[3,32,512]{2,1,0:T(8,128)S(1)} %collective-permute-done.12.refs_2_, ...), custom_call_target="tpu_custom_call" | custom-call | bytes 1200000 | tf_op jit(solution)/shard_map/pallas_call | solution.py:26
  33.2 1.1 %collective-permute-start.14 = (f32[3,8,512]{2,1,0:T(8,128)S(1)}, f32[3,8,512]{2,1,0:T(8,128)S(1)}, u32[]{:S(2)}, u32[]{:S(2)}) collective-permute-start(f32[3,8,512]{2,1,0:T(8,128)S(1)} %get-tuple-element.82), channel_id=1, source_target_pairs={{0,4},{1,5},{2,6},{3,7},{4,0},{5,1},{6,2},{7,3},{8,12},{9,13},{10,... | collective-permute-start | bytes 147464 | tf_op jit(solution)/shard_map/ppermute | solution.py:397
  34.3 1.2 %collective-permute-start.15 = (f32[3,8,512]{2,1,0:T(8,128)S(1)}, f32[3,8,512]{2,1,0:T(8,128)S(1)}, u32[]{:S(2)}, u32[]{:S(2)}) collective-permute-start(f32[3,8,512]{2,1,0:T(8,128)S(1)} %get-tuple-element.83), channel_id=1, source_target_pairs={{0,6},{1,7},{2,4},{3,5},{4,2},{5,3},{6,0},{7,1},{8,14},{9,15},{10,... | collective-permute-start | bytes 147464 | tf_op jit(solution)/shard_map/ppermute | solution.py:397
  35.6 1.2 %collective-permute-start.13 = (f32[3,8,512]{2,1,0:T(8,128)S(1)}, f32[3,8,512]{2,1,0:T(8,128)S(1)}, u32[]{:S(2)}, u32[]{:S(2)}) collective-permute-start(f32[3,8,512]{2,1,0:T(8,128)S(1)} %get-tuple-element.80.refs_6_), channel_id=1, source_target_pairs={{0,2},{1,3},{2,0},{3,1},{4,6},{5,7},{6,4},{7,5},{8,10},{9,11},{10,... | collective-permute-start | bytes 147464 | tf_op jit(solution)/shard_map/ppermute | solution.py:397
  36.7 2.0 %collective-permute-done.14.refs_1_ = f32[3,8,512]{2,1,0:T(8,128)S(1)} collective-permute-done((f32[3,8,512]{2,1,0:T(8,128)S(1)}, f32[3,8,512]{2,1,0:T(8,128)S(1)}, u32[]{:S(2)}, u32[]{:S(2)}) %collective-permute-start.14) | collective-permute-done | bytes 49184 | tf_op jit(solution)/shard_map/ppermute | solution.py:397
  38.8 1.7 %collective-permute-done.15.refs_2_ = f32[3,8,512]{2,1,0:T(8,128)S(1)} collective-permute-done((f32[3,8,512]{2,1,0:T(8,128)S(1)}, f32[3,8,512]{2,1,0:T(8,128)S(1)}, u32[]{:S(2)}, u32[]{:S(2)}) %collective-permute-start.15) | collective-permute-done | bytes 49184 | tf_op jit(solution)/shard_map/ppermute | solution.py:397
  41.0 1.3 %collective-permute-done.18.refs_6_ = f32[6,8,512]{2,1,0:T(8,128)S(1)} collective-permute-done((f32[6,8,512]{2,1,0:T(8,128)S(1)}, f32[6,8,512]{2,1,0:T(8,128)S(1)}, u32[]{:S(2)}, u32[]{:S(2)}) %collective-permute-start.18) | collective-permute-done | bytes 98336 | tf_op jit(solution)/shard_map/ppermute | solution.py:388
  42.3 1.4 %shard_map.90 = f32[3,16,16,512]{3,2,1,0:T(8,128)} custom-call(f32[3,32,8,512]{3,2,1,0:T(8,128)S(1)} %get-tuple-element.81.refs_0_, f32[32,8,512]{2,1,0:T(8,128)S(1)} %get-tuple-element.60.refs_5_.refs_8_.refs_1_, f32[32,8,512]{2,1,0:T(8,128)S(1)} %get-tuple-element.61.refs_6_.refs_9_.refs_2_, f32[6,8,512]{2,1,0:T(8,128)S(1)} %shard_map.89.refs_3_, ...), custom_call_target="tpu_custom_call" | custom-call | bytes 3000000 | tf_op jit(solution)/shard_map/pallas_call | solution.py:26
  (46 shorter events, 5.1 us)
Async XLA Ops:
  1.6 1.9 %copy-start.1 = (f32[2,16,16,512]{3,2,1,0:T(8,128)S(1)}, f32[2,16,16,512]{3,2,1,0:T(8,128)}, u32[]{:S(2)}) copy-start(f32[2,16,16,512]{3,2,1,0:T(8,128)} %refs_0_.4) | copy-start | bytes 3145732
  1.6 1.5 %collective-permute-start = (f32[3,16,512]{2,1,0:T(8,128)S(1)}, f32[3,16,512]{2,1,0:T(8,128)S(1)}, u32[]{:S(2)}, u32[]{:S(2)}) collective-permute-start(f32[3,16,512]{2,1,0:T(8,128)S(1)} %get-tuple-element.48), channel_id=1, source_target_pairs={{0,1},{1,0},{2,3},{3,2},{4,5},{5,4},{6,7},{7,6},{8,9},{9,8},{10,11... | collective-permute-start | bytes 294920 | tf_op jit(solution)/shard_map/ppermute | solution.py:388
  2.5 10.4 %copy-start.4 = (s32[3,100]{1,0:T(4,128)S(1)}, s32[3,100]{1,0:T(4,128)}, u32[]{:S(2)}) copy-start(s32[3,100]{1,0:T(4,128)} %refs_0_.5) | copy-start | bytes 3604
  2.5 10.4 %copy-start.5 = (f32[3,12]{1,0:T(4,128)S(1)}, f32[3,12]{1,0:T(4,128)}, u32[]{:S(2)}) copy-start(f32[3,12]{1,0:T(4,128)} %refs_2_.1) | copy-start | bytes 436
  2.5 10.4 %copy-start.6 = (s32[100]{0:T(128)S(1)}, s32[100]{0:T(128)}, u32[]{:S(2)}) copy-start(s32[100]{0:T(128)} %param.12) | copy-start | bytes 1204
  3.1 11.3 %collective-permute-start.1 = (f32[3,18,8,512]{3,2,1,0:T(8,128)S(1)}, f32[3,18,8,512]{3,2,1,0:T(8,128)S(1)}, u32[]{:S(2)}, u32[]{:S(2)}) collective-permute-start(f32[3,18,8,512]{3,2,1,0:T(8,128)S(1)} %get-tuple-element.51), channel_id=1, source_target_pairs={{0,1},{1,0},{2,3},{3,2},{4,5},{5,4},{6,7},{7,6},{8,9},{9,8},{10,11... | collective-permute-start | bytes 2654216 | tf_op jit(solution)/shard_map/ppermute | solution.py:388
  3.6 8.6 %collective-permute-start.2 = (f32[2,16,8,512]{3,2,1,0:T(8,128)S(1)}, f32[2,16,8,512]{3,2,1,0:T(8,128)S(1)}, u32[]{:S(2)}, u32[]{:S(2)}) collective-permute-start(f32[2,16,8,512]{3,2,1,0:T(8,128)S(1)} %get-tuple-element.56), channel_id=1, source_target_pairs={{0,1},{1,0},{2,3},{3,2},{4,5},{5,4},{6,7},{7,6},{8,9},{9,8},{10,11... | collective-permute-start | bytes 1572872 | tf_op jit(solution)/shard_map/ppermute | solution.py:388
  3.8 3.1 %collective-permute-start.3 = (f32[1,16,8,512]{3,2,1,0:T(8,128)S(1)}, f32[1,16,8,512]{3,2,1,0:T(8,128)S(1)}, u32[]{:S(2)}, u32[]{:S(2)}) collective-permute-start(f32[1,16,8,512]{3,2,1,0:T(8,128)S(1)} %get-tuple-element.49.refs_2_), channel_id=1, source_target_pairs={{0,1},{1,0},{2,3},{3,2},{4,5},{5,4},{6,7},{7,6},{8,9},{9,8},{10,11... | collective-permute-start | bytes 786440 | tf_op jit(solution)/shard_map/ppermute | solution.py:388
  4.2 13.1 %collective-permute-start.4 = (f32[3,32,512]{2,1,0:T(8,128)S(1)}, f32[3,32,512]{2,1,0:T(8,128)S(1)}, u32[]{:S(2)}, u32[]{:S(2)}) collective-permute-start(f32[3,32,512]{2,1,0:T(8,128)S(1)} %get-tuple-element.54.refs_1_), channel_id=1, source_target_pairs={{0,2},{1,8},{2,0},{3,10},{4,6},{5,12},{6,4},{7,14},{8,1},{9,16},{1... | collective-permute-start | bytes 589832 | tf_op jit(solution)/shard_map/ppermute | solution.py:391
  7.4 8.7 %collective-permute-start.7 = (f32[3,8,512]{2,1,0:T(8,128)S(1)}, f32[3,8,512]{2,1,0:T(8,128)S(1)}, u32[]{:S(2)}, u32[]{:S(2)}) collective-permute-start(f32[3,8,512]{2,1,0:T(8,128)S(1)} %get-tuple-element.65.refs_0_), channel_id=1, source_target_pairs={{0,6},{1,7},{2,4},{3,5},{4,2},{5,3},{6,0},{7,1},{8,14},{9,15},{10,... | collective-permute-start | bytes 147464 | tf_op jit(solution)/shard_map/ppermute | solution.py:397
  12.3 5.0 %collective-permute-start.6 = (f32[3,8,512]{2,1,0:T(8,128)S(1)}, f32[3,8,512]{2,1,0:T(8,128)S(1)}, u32[]{:S(2)}, u32[]{:S(2)}) collective-permute-start(f32[3,8,512]{2,1,0:T(8,128)S(1)} %get-tuple-element.65.refs_0_), channel_id=1, source_target_pairs={{0,4},{1,5},{2,6},{3,7},{4,0},{5,1},{6,2},{7,3},{8,12},{9,13},{10,... | collective-permute-start | bytes 147464 | tf_op jit(solution)/shard_map/ppermute | solution.py:397
  12.3 5.0 %collective-permute-start.5 = (f32[3,8,512]{2,1,0:T(8,128)S(1)}, f32[3,8,512]{2,1,0:T(8,128)S(1)}, u32[]{:S(2)}, u32[]{:S(2)}) collective-permute-start(f32[3,8,512]{2,1,0:T(8,128)S(1)} %get-tuple-element.65.refs_0_), channel_id=1, source_target_pairs={{0,2},{1,3},{2,0},{3,1},{4,6},{5,7},{6,4},{7,5},{8,10},{9,11},{10,... | collective-permute-start | bytes 147464 | tf_op jit(solution)/shard_map/ppermute | solution.py:397
  14.6 2.7 %copy-start.3 = (s32[16,512]{1,0:T(8,128)S(1)}, s32[16,512]{1,0:T(8,128)}, u32[]{:S(2)}) copy-start(s32[16,512]{1,0:T(8,128)} %refs_4_.1) | copy-start | bytes 98308
  17.5 6.5 %collective-permute-start.9 = (f32[3,8,512]{2,1,0:T(8,128)S(1)}, f32[3,8,512]{2,1,0:T(8,128)S(1)}, u32[]{:S(2)}, u32[]{:S(2)}) collective-permute-start(f32[3,8,512]{2,1,0:T(8,128)S(1)} %get-tuple-element.68), channel_id=1, source_target_pairs={{0,4},{1,5},{2,6},{3,7},{4,0},{5,1},{6,2},{7,3},{8,12},{9,13},{10,... | collective-permute-start | bytes 147464 | tf_op jit(solution)/shard_map/ppermute | solution.py:397
  19.6 5.9 %collective-permute-start.10 = (f32[3,8,512]{2,1,0:T(8,128)S(1)}, f32[3,8,512]{2,1,0:T(8,128)S(1)}, u32[]{:S(2)}, u32[]{:S(2)}) collective-permute-start(f32[3,8,512]{2,1,0:T(8,128)S(1)} %get-tuple-element.69), channel_id=1, source_target_pairs={{0,6},{1,7},{2,4},{3,5},{4,2},{5,3},{6,0},{7,1},{8,14},{9,15},{10,... | collective-permute-start | bytes 147464 | tf_op jit(solution)/shard_map/ppermute | solution.py:397
  20.9 4.6 %collective-permute-start.8 = (f32[3,8,512]{2,1,0:T(8,128)S(1)}, f32[3,8,512]{2,1,0:T(8,128)S(1)}, u32[]{:S(2)}, u32[]{:S(2)}) collective-permute-start(f32[3,8,512]{2,1,0:T(8,128)S(1)} %get-tuple-element.67.refs_6_), channel_id=1, source_target_pairs={{0,2},{1,3},{2,0},{3,1},{4,6},{5,7},{6,4},{7,5},{8,10},{9,11},{10,... | collective-permute-start | bytes 147464 | tf_op jit(solution)/shard_map/ppermute | solution.py:397
  26.2 5.7 %collective-permute-start.11 = (f32[3,32,512]{2,1,0:T(8,128)S(1)}, f32[3,32,512]{2,1,0:T(8,128)S(1)}, u32[]{:S(2)}, u32[]{:S(2)}) collective-permute-start(f32[3,32,512]{2,1,0:T(8,128)S(1)} %get-tuple-element.77), channel_id=1, source_target_pairs={{0,2},{1,8},{2,0},{3,10},{4,6},{5,12},{6,4},{7,14},{8,1},{9,16},{1... | collective-permute-start | bytes 589832 | tf_op jit(solution)/shard_map/ppermute | solution.py:391
  26.2 5.7 %collective-permute-start.12 = (f32[3,32,512]{2,1,0:T(8,128)S(1)}, f32[3,32,512]{2,1,0:T(8,128)S(1)}, u32[]{:S(2)}, u32[]{:S(2)}) collective-permute-start(f32[3,32,512]{2,1,0:T(8,128)S(1)} %get-tuple-element.78), channel_id=1, source_target_pairs={{0,1},{1,0},{2,3},{3,2},{4,5},{5,4},{6,7},{7,6},{8,9},{9,8},{10,11... | collective-permute-start | bytes 589832 | tf_op jit(solution)/shard_map/ppermute | solution.py:388
  32.6 9.6 %collective-permute-start.16 = (f32[3,16,8,512]{3,2,1,0:T(8,128)S(1)}, f32[3,16,8,512]{3,2,1,0:T(8,128)S(1)}, u32[]{:S(2)}, u32[]{:S(2)}) collective-permute-start(f32[3,16,8,512]{3,2,1,0:T(8,128)S(1)} %get-tuple-element.85), channel_id=1, source_target_pairs={{0,1},{1,0},{2,3},{3,2},{4,5},{5,4},{6,7},{7,6},{8,9},{9,8},{10,11... | collective-permute-start | bytes 2359304 | tf_op jit(solution)/shard_map/ppermute | solution.py:388
  33.2 7.8 %collective-permute-start.17 = (f32[2,16,8,512]{3,2,1,0:T(8,128)S(1)}, f32[2,16,8,512]{3,2,1,0:T(8,128)S(1)}, u32[]{:S(2)}, u32[]{:S(2)}) collective-permute-start(f32[2,16,8,512]{3,2,1,0:T(8,128)S(1)} %get-tuple-element.86), channel_id=1, source_target_pairs={{0,1},{1,0},{2,3},{3,2},{4,5},{5,4},{6,7},{7,6},{8,9},{9,8},{10,11... | collective-permute-start | bytes 1572872 | tf_op jit(solution)/shard_map/ppermute | solution.py:388
  33.2 5.5 %collective-permute-start.14 = (f32[3,8,512]{2,1,0:T(8,128)S(1)}, f32[3,8,512]{2,1,0:T(8,128)S(1)}, u32[]{:S(2)}, u32[]{:S(2)}) collective-permute-start(f32[3,8,512]{2,1,0:T(8,128)S(1)} %get-tuple-element.82), channel_id=1, source_target_pairs={{0,4},{1,5},{2,6},{3,7},{4,0},{5,1},{6,2},{7,3},{8,12},{9,13},{10,... | collective-permute-start | bytes 147464 | tf_op jit(solution)/shard_map/ppermute | solution.py:397
  34.3 6.2 %collective-permute-start.15 = (f32[3,8,512]{2,1,0:T(8,128)S(1)}, f32[3,8,512]{2,1,0:T(8,128)S(1)}, u32[]{:S(2)}, u32[]{:S(2)}) collective-permute-start(f32[3,8,512]{2,1,0:T(8,128)S(1)} %get-tuple-element.83), channel_id=1, source_target_pairs={{0,6},{1,7},{2,4},{3,5},{4,2},{5,3},{6,0},{7,1},{8,14},{9,15},{10,... | collective-permute-start | bytes 147464 | tf_op jit(solution)/shard_map/ppermute | solution.py:397
  35.6 5.2 %collective-permute-start.13 = (f32[3,8,512]{2,1,0:T(8,128)S(1)}, f32[3,8,512]{2,1,0:T(8,128)S(1)}, u32[]{:S(2)}, u32[]{:S(2)}) collective-permute-start(f32[3,8,512]{2,1,0:T(8,128)S(1)} %get-tuple-element.80.refs_6_), channel_id=1, source_target_pairs={{0,2},{1,3},{2,0},{3,1},{4,6},{5,7},{6,4},{7,5},{8,10},{9,11},{10,... | collective-permute-start | bytes 147464 | tf_op jit(solution)/shard_map/ppermute | solution.py:397
  40.9 1.4 %collective-permute-start.18 = (f32[6,8,512]{2,1,0:T(8,128)S(1)}, f32[6,8,512]{2,1,0:T(8,128)S(1)}, u32[]{:S(2)}, u32[]{:S(2)}) collective-permute-start(f32[6,8,512]{2,1,0:T(8,128)S(1)} %shard_map.89.refs_3_), channel_id=1, source_target_pairs={{0,1},{1,0},{2,3},{3,2},{4,5},{5,4},{6,7},{7,6},{8,9},{9,8},{10,11... | collective-permute-start | bytes 294920 | tf_op jit(solution)/shard_map/ppermute | solution.py:388
  (2 other events, 2.4 us)
